TPU v7x, 32 devices: a whole 2x2x4 slice. The times are simulated.
32 devices in a mesh: tx: 4 (over x, core), ty: 8 (over z, y).
Axes of the slice: x: 2, y: 2, z: 4, core: 2. Of those that a mesh axis runs over, the one named last changes fastest.
Arguments:
- solution: float32 [4, 512, 2048], P(None, 'tx', 'ty'), may hold values from -6 to 6
- residual: float32 [4, 512, 2048], P(None, 'tx', 'ty')
- direction: float32 [4, 512, 2048], P(None, 'tx', 'ty')
- blocks: bfloat16 [8192, 128, 256], P(('tx', 'ty')), may hold values from -0.375 to 0.375
- bin_owner: int32 [8192, 1], P(('tx', 'ty')), may hold values from 0 to 31; in each aligned block of 256 rows (0 to 255, 256 to 511, ...) at most 12 rows name the same one
- bin_tile: int32 [8192], P(('tx', 'ty')), may hold values from 0 to 127
Outputs:
- next_solution: float32 [4, 512, 2048], P(None, 'tx', 'ty')
- next_residual: float32 [4, 512, 2048], P(None, 'tx', 'ty')
- next_direction: float32 [4, 512, 2048], P(None, 'tx', 'ty')
Inputs may be any that keep to these rules, and one draw needn't show every extreme that they name: `bin_owner`: among the bins of one device, at most 12 name the same owner, and on some devices some owner is named by exactly 12 of them.
All inputs are finite; a program needn't handle non-finite values.
Results may differ from a plain program's by a relative error of at most 0.0024.
Values may be sent and summed in bfloat16 or wider, within the bound.
No kernel may reach another device: no remote copies, remote signals or barrier semaphores. Data moves between devices by JAX's collectives and lax.ppermute only.
A program may use at most 128 MiB of HBM per device.

v0:
```python
import jax
import jax.numpy as jnp
from jax import lax
from jax.sharding import PartitionSpec as P

TILE_SIDE = 16


smooth_weight = 0.25


def padded_2(shard, sides, width):
    for axis, dim in sides:
        size, length = (lax.axis_size(axis), shard.shape[dim])
        up = [(i, (i + 1) % size) for i in range(size - 1)]
        down = [(j, i) for i, j in up]
        last = lax.slice_in_dim(shard, length - width, length, axis=dim)
        initial = lax.slice_in_dim(shard, 0, width, axis=dim)
        before = lax.ppermute(last, axis, up)
        after = lax.ppermute(initial, axis, down)
        shard = jnp.concatenate([before, shard, after], axis=dim)
    return shard


def to_tiles(field):
    beacons, rows, cols = field.shape
    across = rows // TILE_SIDE
    down = cols // TILE_SIDE
    shaped = field.reshape(beacons, across, TILE_SIDE, down, TILE_SIDE).transpose(1, 3, 0, 2, 4)
    return shaped.reshape(across * down, beacons, TILE_SIDE * TILE_SIDE)


def to_field(tiles, rows, cols):
    beacons = tiles.shape[1]
    across = rows // TILE_SIDE
    down = cols // TILE_SIDE
    shaped = tiles.reshape(across, down, beacons, TILE_SIDE, TILE_SIDE).transpose(2, 0, 3, 1, 4)
    return shaped.reshape(beacons, rows, cols)


def laplace_local(field):
    padded = padded_2(field.astype(jnp.bfloat16), (("tx", 1), ("ty", 2)), 1).astype(field.dtype)
    near = padded[:, 2:, 1:-1] + padded[:, :-2, 1:-1] + padded[:, 1:-1, 2:] + padded[:, 1:-1, :-2]
    return 4.0 * field - near


def per_device(solution, residual, direction, blocks, bin_owner, bin_tile):
    beacons, rows, cols = direction.shape
    cells = TILE_SIDE * TILE_SIDE
    across_x = lax.axis_size("tx")
    across_y = lax.axis_size("ty")
    devices = across_x * across_y
    count = blocks.shape[0]
    cap = max(2, 3 * count // (2 * devices))
    owner = bin_owner[:, 0]
    member = (owner[:, None] == jnp.arange(devices, dtype=jnp.int32)[None, :]).astype(jnp.int32)
    before = jnp.cumsum(member, axis=0) - member
    rank = jnp.sum(before * member, axis=1)
    slot = owner * cap + rank
    request = jnp.full((devices * cap,), -1, jnp.int32).at[slot].set(bin_tile)
    wanted = lax.all_to_all(
        request.reshape(devices, cap), ("tx", "ty"), split_axis=0, concat_axis=0, tiled=True
    )
    wanted = jnp.maximum(wanted.reshape(devices * cap), 0)
    own_tiles = to_tiles(direction.astype(jnp.bfloat16))
    outgoing = jnp.take(own_tiles, wanted, axis=0)
    fetched = lax.all_to_all(
        outgoing.reshape(devices, cap, beacons, cells),
        ("tx", "ty"),
        split_axis=0,
        concat_axis=0,
        tiled=True,
    )
    fetched = fetched.reshape(devices * cap, beacons, cells)
    picked = jnp.take(fetched, slot, axis=0)
    samples = jnp.einsum("bsc,bkc->bks", blocks, picked, preferred_element_type=jnp.float32).astype(
        jnp.bfloat16
    )
    adjoint = jnp.einsum("bsc,bks->bkc", blocks, samples, preferred_element_type=jnp.float32)
    returned = jnp.zeros((devices * cap, beacons, cells), jnp.float32).at[slot].set(adjoint)
    arrived = lax.all_to_all(
        returned.reshape(devices, cap, beacons, cells),
        ("tx", "ty"),
        split_axis=0,
        concat_axis=0,
        tiled=True,
    )
    arrived = arrived.reshape(devices * cap, beacons, cells)
    data_tiles = jnp.zeros(own_tiles.shape, jnp.float32).at[wanted].add(arrived)
    image = to_field(data_tiles, rows, cols) + smooth_weight * laplace_local(direction)
    norm_old = lax.psum(jnp.sum(residual * residual, axis=(1, 2)), ("tx", "ty"))
    curvature = lax.psum(jnp.sum(direction * image, axis=(1, 2)), ("tx", "ty"))
    alpha = norm_old / curvature
    next_residual = residual - alpha[:, None, None] * image
    norm_new = lax.psum(jnp.sum(next_residual * next_residual, axis=(1, 2)), ("tx", "ty"))
    next_solution = solution + alpha[:, None, None] * direction
    next_direction = next_residual + (norm_new / norm_old)[:, None, None] * direction
    return (next_solution, next_residual, next_direction)


def solution(mesh):
    placed = (
        P(None, "tx", "ty"),
        P(None, "tx", "ty"),
        P(None, "tx", "ty"),
        P(("tx", "ty"), None, None),
        P(("tx", "ty"), None),
        P(("tx", "ty")),
    )
    return jax.shard_map(
        per_device,
        mesh=mesh,
        in_specs=placed,
        out_specs=(P(None, "tx", "ty"), P(None, "tx", "ty"), P(None, "tx", "ty")),
        check_vma=False,
    )
```

profile of v0, /device:TPU:0, one launch (start us, length us, event | category | flops | bytes accessed | tf_op | source)
XLA Modules:
  0.0 246.8 jit_solution(11422151003134133526)
XLA Ops:
  3.6 1.6 scatter_custom_fusion
  5.9 7.3 %all-to-all-start = ((s32[32,1,12]{2,1,0:T(1,128)}), s32[32,1,12]{2,1,0:T(1,128)S(1)}, u32[]{:S(2)}, u32[]{:S(2)}) async-start(s32[32,1,12]{2,1,0:T(1,128)} %bitcast.5), calls=%async_computation | async-start | bytes 32768 | tf_op jit(solution)/shard_map/all_to_all | solution.py:61
  14.3 2.5 %reshape.85 = bf16[4,8,16,16,16]{4,3,2,1,0:T(8,128)(2,1)} reshape(bf16[4,128,256]{2,1,0:T(8,128)(2,1)S(1)} %convert_element_type.19) | data formatting | bytes 524288 | tf_op jit(solution)/shard_map/reshape | solution.py:29
  16.7 2.1 copy.32
  18.9 2.0 reshape.86
  21.5 2.3 gather_fusion
  23.9 1.4 broadcast_select_fusion
  25.3 5.8 %all-to-all-start.1 = ((bf16[32,12,4,256]{3,2,1,0:T(4,128)(2,1)}), bf16[32,12,4,256]{3,2,1,0:T(4,128)(2,1)S(1)}, u32[]{:S(2)}, u32[]{:S(2)}) async-start(bf16[32,12,4,256]{3,2,1,0:T(4,128)(2,1)} %broadcast_select_fusion), calls=%async_computation.1 | async-start | bytes 1572864 | tf_op jit(solution)/shard_map/all_to_all | solution.py:67
  31.1 22.0 %all-to-all-done.1 = bf16[32,12,4,256]{3,2,1,0:T(4,128)(2,1)S(1)} async-done(((bf16[32,12,4,256]{3,2,1,0:T(4,128)(2,1)}), bf16[32,12,4,256]{3,2,1,0:T(4,128)(2,1)S(1)}, u32[]{:S(2)}, u32[]{:S(2)}) %all-to-all-start.1) | async-done | bytes 786464 | tf_op jit(solution)/shard_map/all_to_all | solution.py:67
  54.2 16.9 %fusion = f32[256,4,256]{2,1,0:T(4,128)S(1)} fusion(bf16[256,128,256]{2,1,0:T(8,128)(2,1)} %param.9, bf16[256,4,256]{2,1,0:T(4,128)(2,1)S(1)} %gather_fusion.1, pred[256]{0:T(512)(128)(4,1)S(1)} %get-tuple-element.9), kind=kOutput, calls=%fused_computation.8 | convolution fusion | flops 134610944 | bytes 18350336 | tf_op jit(solution)/shard_map/bsc,bks->bkc/dot_general | solution.py:79
  71.1 1.4 broadcast_in_dim.38
  72.5 24.0 %scatter_fusion = f32[384,4,256]{2,1,0:T(4,128)} fusion(f32[384,4,256]{2,1,0:T(4,128)} %broadcast_in_dim.38, s32[256]{0:T(256)S(1)} %bitcast.53, f32[256,4,256]{2,1,0:T(4,128)S(1)} %fusion), kind=kCustom, calls=%fused_computation.3 | custom fusion | bytes 3146752 | tf_op jit(solution)/shard_map/scatter | solution.py:80
  96.5 2.7 %all-to-all-start.2 = ((f32[32,12,4,256]{3,2,1,0:T(4,128)}), f32[32,12,4,256]{3,2,1,0:T(4,128)S(1)}, u32[]{:S(2)}, u32[]{:S(2)}) async-start(f32[32,12,4,256]{3,2,1,0:T(4,128)} %bitcast.10), calls=%async_computation.2 | async-start | bytes 3145728 | tf_op jit(solution)/shard_map/all_to_all | solution.py:81
  99.2 1.3 collective-permute-start.1
  100.5 3.0 %collective-permute-start = (bf16[4,1,256]{2,1,0:T(2,128)(2,1)S(1)}, bf16[4,1,256]{2,1,0:T(2,128)(2,1)S(1)}, u32[]{:S(2)}, u32[]{:S(2)}) collective-permute-start(bf16[4,1,256]{2,1,0:T(2,128)(2,1)S(1)} %get-tuple-element.15), channel_id=1, source_target_pairs={{0,8},{8,16},{16,24},{1,9},{9,17},{17,25},{2,10},{10,18},{18,26},{... | collective-permute-start | bytes 6152 | tf_op jit(solution)/shard_map/ppermute | solution.py:19
  105.8 4.7 %collective-permute-start.2 = (bf16[4,130,1]{2,1,0:T(8,128)(2,1)S(1)}, bf16[4,130,1]{2,1,0:T(8,128)(2,1)S(1)}, u32[]{:S(2)}, u32[]{:S(2)}) collective-permute-start(bf16[4,130,1]{2,1,0:T(8,128)(2,1)S(1)} %get-tuple-element.13), channel_id=1, source_target_pairs={{0,1},{1,2},{2,3},{3,4},{4,5},{5,6},{6,7},{8,9},{9,10},{10,11},{11... | collective-permute-start | bytes 3128 | tf_op jit(solution)/shard_map/ppermute | solution.py:19
  110.6 10.1 %collective-permute-done.3 = bf16[4,130,1]{2,1,0:T(8,128)(2,1)S(1)} collective-permute-done((bf16[4,130,1]{2,1,0:T(8,128)(2,1)S(1)}, bf16[4,130,1]{2,1,0:T(8,128)(2,1)S(1)}, u32[]{:S(2)}, u32[]{:S(2)}) %collective-permute-start.3) | collective-permute-done | bytes 1072 | tf_op jit(solution)/shard_map/ppermute | solution.py:20
  121.0 17.0 %all-to-all-done.2 = f32[32,12,4,256]{3,2,1,0:T(4,128)S(1)} async-done(((f32[32,12,4,256]{3,2,1,0:T(4,128)}), f32[32,12,4,256]{3,2,1,0:T(4,128)S(1)}, u32[]{:S(2)}, u32[]{:S(2)}) %all-to-all-start.2) | async-done | bytes 1572896 | tf_op jit(solution)/shard_map/all_to_all | solution.py:81
  138.1 14.5 %scatter_fusion.1 = f32[128,4,256]{2,1,0:T(4,128)S(1)} fusion(f32[128,4,256]{2,1,0:T(4,128)S(1)} %broadcast_in_dim.36, s32[384]{0:T(512)S(1)} %reshape.126, f32[384,4,256]{2,1,0:T(4,128)S(1)} %bitcast.48), kind=kCustom, calls=%fused_computation.4 | custom fusion | flops 393216 | bytes 4720128 | tf_op jit(solution)/shard_map/scatter-add | solution.py:89
  152.7 2.6 %reshape.90 = f32[8,16,4,16,16]{4,3,1,0,2:T(8,128)} reshape(f32[128,4,256]{2,0,1:T(8,128)S(1)} %copy.27) | data formatting | bytes 1048576 | tf_op jit(solution)/shard_map/reshape | solution.py:37
  155.3 5.9 %copy.28 = f32[4,8,16,16,16]{4,3,2,1,0:T(8,128)} copy(f32[4,8,16,16,16]{4,2,3,1,0:T(8,128)} %bitcast.46) | data formatting | bytes 1048576 | tf_op jit(solution)/shard_map/transpose | solution.py:37
  161.2 3.6 %reshape.91 = f32[4,128,256]{2,1,0:T(8,128)S(1)} reshape(f32[4,8,16,16,16]{4,3,2,1,0:T(8,128)} %copy.28) | data formatting | bytes 1048576 | tf_op jit(solution)/shard_map/reshape | solution.py:38
  165.4 41.5 %all-reduce = (f32[4]{0:T(128)S(1)}, f32[4]{0:T(128)S(1)}) all-reduce(f32[4]{0:T(128)S(1)} %get-tuple-element.17, f32[4]{0:T(128)S(1)} %get-tuple-element.7), channel_id=1, replica_groups=mesh['tx'=4,'ty'=8] {'tx','ty'}, use_global_device_ids=true, to_apply=%region_1.2 | all-reduce | flops 8 | bytes 64 | tf_op jit(solution)/shard_map/psum | solution.py:91
  207.2 38.5 %psum.23 = f32[4]{0:T(128)S(1)} all-reduce(f32[4]{0:T(128)S(1)} %get-tuple-element.5), channel_id=1, replica_groups=mesh['tx'=4,'ty'=8] {'tx','ty'}, use_global_device_ids=true, to_apply=%region_11.12 | all-reduce | flops 4 | bytes 32 | tf_op jit(solution)/shard_map/psum | solution.py:95
  (43 shorter events, 11.3 us)
Async XLA Ops:
  5.9 15.2 %all-to-all-start = ((s32[32,1,12]{2,1,0:T(1,128)}), s32[32,1,12]{2,1,0:T(1,128)S(1)}, u32[]{:S(2)}, u32[]{:S(2)}) async-start(s32[32,1,12]{2,1,0:T(1,128)} %bitcast.5), calls=%async_computation | async-start | bytes 32768 | tf_op jit(solution)/shard_map/all_to_all | solution.py:61
  25.3 27.8 %all-to-all-start.1 = ((bf16[32,12,4,256]{3,2,1,0:T(4,128)(2,1)}), bf16[32,12,4,256]{3,2,1,0:T(4,128)(2,1)S(1)}, u32[]{:S(2)}, u32[]{:S(2)}) async-start(bf16[32,12,4,256]{3,2,1,0:T(4,128)(2,1)} %broadcast_select_fusion), calls=%async_computation.1 | async-start | bytes 1572864 | tf_op jit(solution)/shard_map/all_to_all | solution.py:67
  96.5 41.5 %all-to-all-start.2 = ((f32[32,12,4,256]{3,2,1,0:T(4,128)}), f32[32,12,4,256]{3,2,1,0:T(4,128)S(1)}, u32[]{:S(2)}, u32[]{:S(2)}) async-start(f32[32,12,4,256]{3,2,1,0:T(4,128)} %bitcast.10), calls=%async_computation.2 | async-start | bytes 3145728 | tf_op jit(solution)/shard_map/all_to_all | solution.py:81
  99.2 4.3 %collective-permute-start.1 = (bf16[4,1,256]{2,1,0:T(2,128)(2,1)S(1)}, bf16[4,1,256]{2,1,0:T(2,128)(2,1)S(1)}, u32[]{:S(2)}, u32[]{:S(2)}) collective-permute-start(bf16[4,1,256]{2,1,0:T(2,128)(2,1)S(1)} %get-tuple-element.16), channel_id=1, source_target_pairs={{8,0},{16,8},{24,16},{9,1},{17,9},{25,17},{10,2},{18,10},{26,18},{... | collective-permute-start | bytes 6152 | tf_op jit(solution)/shard_map/ppermute | solution.py:20
  100.5 3.8 %collective-permute-start = (bf16[4,1,256]{2,1,0:T(2,128)(2,1)S(1)}, bf16[4,1,256]{2,1,0:T(2,128)(2,1)S(1)}, u32[]{:S(2)}, u32[]{:S(2)}) collective-permute-start(bf16[4,1,256]{2,1,0:T(2,128)(2,1)S(1)} %get-tuple-element.15), channel_id=1, source_target_pairs={{0,8},{8,16},{16,24},{1,9},{9,17},{17,25},{2,10},{10,18},{18,26},{... | collective-permute-start | bytes 6152 | tf_op jit(solution)/shard_map/ppermute | solution.py:19
  104.5 16.2 %collective-permute-start.3 = (bf16[4,130,1]{2,1,0:T(8,128)(2,1)S(1)}, bf16[4,130,1]{2,1,0:T(8,128)(2,1)S(1)}, u32[]{:S(2)}, u32[]{:S(2)}) collective-permute-start(bf16[4,130,1]{2,1,0:T(8,128)(2,1)S(1)} %get-tuple-element.14), channel_id=1, source_target_pairs={{1,0},{2,1},{3,2},{4,3},{5,4},{6,5},{7,6},{9,8},{10,9},{11,10},{12... | collective-permute-start | bytes 3128 | tf_op jit(solution)/shard_map/ppermute | solution.py:20
  105.8 14.9 %collective-permute-start.2 = (bf16[4,130,1]{2,1,0:T(8,128)(2,1)S(1)}, bf16[4,130,1]{2,1,0:T(8,128)(2,1)S(1)}, u32[]{:S(2)}, u32[]{:S(2)}) collective-permute-start(bf16[4,130,1]{2,1,0:T(8,128)(2,1)S(1)} %get-tuple-element.13), channel_id=1, source_target_pairs={{0,1},{1,2},{2,3},{3,4},{4,5},{5,6},{6,7},{8,9},{9,10},{10,11},{11... | collective-permute-start | bytes 3128 | tf_op jit(solution)/shard_map/ppermute | solution.py:19
  161.2 3.6 %copy-start = (f32[4,128,256]{2,1,0:T(8,128)S(1)}, f32[4,128,256]{2,1,0:T(8,128)}, u32[]{:S(2)}) copy-start(f32[4,128,256]{2,1,0:T(8,128)} %param.8) | copy-start | bytes 1572868
  161.2 3.6 %copy-start.1 = (f32[4,128,256]{2,1,0:T(8,128)S(1)}, f32[4,128,256]{2,1,0:T(8,128)}, u32[]{:S(2)}) copy-start(f32[4,128,256]{2,1,0:T(8,128)} %param.7) | copy-start | bytes 1572868
  164.8 80.9 %copy-start.3 = (f32[4,128,256]{2,1,0:T(8,128)S(1)}, f32[4,128,256]{2,1,0:T(8,128)}, u32[]{:S(2)}) copy-start(f32[4,128,256]{2,1,0:T(8,128)} %param.6) | copy-start | bytes 1572868
  207.2 39.7 %copy-start.2 = (f32[4,128,256]{2,1,0:T(8,128)}, f32[4,128,256]{2,1,0:T(8,128)S(1)}, u32[]{:S(2)}) copy-start(f32[4,128,256]{2,1,0:T(8,128)S(1)} %get-tuple-element.6) | copy-start | bytes 1572868
where the time goes:
time: 248 us; the launch traced here: 247 us
  blocking collectives  80 us (32%)
  local copies, waits for them, and re-layouts  50.9 us (21%)
  waiting for transfers between devices  49.9 us (20%)
  starting transfers between devices  26.2 us (11%)
  other arithmetic  22.1 us (9%)
  matrix products  16.9 us (7%)
    psum x1, blocking collectives, per_device(): norm_old = lax.psum(jnp.sum(residual * residual, axis=(1, 2)), ('tx', 'ty'))  41.5 us
    psum x1, blocking collectives, per_device(): lax.psum(jnp.sum(next_residual * next_residual, axis=(1, 2)), ('tx', 'ty'))  38.5 us
    scatter x1, local copies, waits for them, and re-layouts, per_device(): jnp.zeros((devices * cap, beacons, cells), jnp.float32).at[slot]  24 us
    all_to_all x1, waiting for transfers between devices, per_device(): lax.all_to_all(outgoing.reshape(devices, cap, beacons, cells), ('tx', 'ty...  22 us
    all_to_all x1, waiting for transfers between devices, per_device(): lax.all_to_all(returned.reshape(devices, cap, beacons, cells), ('tx', 'ty...  17 us
    dot_general x1, matrix products, per_device(): jnp.einsum('bsc,bks->bkc', blocks, samples, preferred_element_type=jnp.fl...  16.9 us
    scatter-add x1, other arithmetic, per_device(): data_tiles = jnp.zeros(own_tiles.shape, jnp.float32).at[wanted].add(arrived)  14.5 us
    ppermute x2, waiting for transfers between devices, padded_2(): after = lax.ppermute(initial, axis, down)  10.1 us
  transfers between devices with their start and end apart: 7, of which 4 were waited for; matrix products, arithmetic and copies ran while one was open for 3% of the time, Pallas kernels for 0%

commit v1 on v0

v1 whole, which is shorter than its diff:
```python
import functools

import jax
import jax.numpy as jnp
from jax import lax
from jax.experimental import pallas as pl
from jax.experimental.pallas import tpu as pltpu
from jax.sharding import PartitionSpec as P

TILE_SIDE = 16
LANES = 128
SUB = 8
smooth_weight = 0.25

AXES = ("tx", "ty")


def whole(memory=pltpu.VMEM):
    return pl.BlockSpec(memory_space=memory)


def params(mib):
    return pltpu.CompilerParams(vmem_limit_bytes=mib << 20)


def swap_chunks(x):
    row = lax.broadcasted_iota(jnp.int32, (SUB, LANES), 0)
    chunk = lax.broadcasted_iota(jnp.int32, (SUB, LANES), 1) // TILE_SIDE
    for s in (1, 2, 4):
        row_bit, chunk_bit = (row & s) != 0, (chunk & s) != 0
        up = pltpu.roll(pltpu.roll(x, SUB - s, 1), TILE_SIDE * s, 2)
        down = pltpu.roll(pltpu.roll(x, s, 1), LANES - TILE_SIDE * s, 2)
        x = jnp.where((row_bit == chunk_bit)[None], x, jnp.where(row_bit[None], down, up))
    return x


def prep_kernel(cap, owner_ref, tile_ref, slot_ref, request_ref):
    devices, bins = request_ref.shape[0], owner_ref.shape[1]
    owner = owner_ref[...]
    member = (lax.broadcasted_iota(jnp.int32, (devices, bins), 0) == owner).astype(jnp.float32)
    earlier = (
        lax.broadcasted_iota(jnp.int32, (bins, bins), 0) < lax.broadcasted_iota(jnp.int32, (bins, bins), 1)
    ).astype(jnp.bfloat16)
    member16 = member.astype(jnp.bfloat16)
    before = jnp.dot(member16, earlier, preferred_element_type=jnp.float32)
    rank = jnp.sum(before * member, axis=0, keepdims=True).astype(jnp.int32)
    slot_ref[...] = owner * cap + rank
    place = lax.broadcasted_iota(jnp.int32, (request_ref.shape[1], bins), 0) == rank
    named = jnp.where(place, tile_ref[...] + 1, 0).astype(jnp.float32).astype(jnp.bfloat16)
    request = lax.dot_general(member16, named, (((1,), (1,)), ((), ())), preferred_element_type=jnp.float32)
    request_ref[...] = request.astype(jnp.int32) - 1


def prep(owner, tile, devices, cap):
    bins = owner.shape[1]
    return pl.pallas_call(
        functools.partial(prep_kernel, cap),
        in_specs=[whole(), whole()],
        out_specs=[whole(), whole()],
        out_shape=[
            jax.ShapeDtypeStruct((1, bins), jnp.int32),
            jax.ShapeDtypeStruct((devices, cap), jnp.int32),
        ],
        compiler_params=params(8),
        name="prep",
    )(owner, tile)


def tiles_kernel(field_ref, out_ref):
    beacons, rows, cols = field_ref.shape
    bands, groups = rows // TILE_SIDE, cols // LANES
    for k in range(beacons):
        for g in range(groups):
            x = field_ref[k, :, g * LANES : (g + 1) * LANES].reshape(bands * 2, SUB, LANES)
            x = swap_chunks(x.astype(jnp.bfloat16).astype(jnp.float32))
            for band in range(bands):
                for h in range(2):
                    at = ((band * groups + g) * 8 + h * beacons + k) * SUB
                    out_ref[at : at + SUB, :] = x[band * 2 + h]


def tiles(field):
    beacons, rows, cols = field.shape
    return pl.pallas_call(
        tiles_kernel,
        in_specs=[whole()],
        out_specs=whole(),
        out_shape=jax.ShapeDtypeStruct((beacons * rows * cols // LANES, LANES), jnp.float32),
        compiler_params=params(8),
        name="tiles",
    )(field)


def gather_kernel(wanted_ref, tiles_ref, out_ref):
    devices, cap = wanted_ref.shape

    def at(d, r):
        t = jnp.maximum(wanted_ref[d, r], 0)
        return tiles_ref[pl.ds((t // SUB) * 64 + t % SUB, SUB, stride=SUB), :]

    def body(d, carry):
        for r in range(0, cap - 1, 2):
            pair = jnp.concatenate([at(d, r), at(d, r + 1)], axis=0)
            out_ref[d, r * SUB : (r + 2) * SUB, :] = pair.astype(jnp.bfloat16)
        if cap % 2:
            pair = jnp.concatenate([at(d, cap - 1), jnp.zeros((SUB, LANES), jnp.float32)], axis=0)
            out_ref[d, (cap - 1) * SUB : (cap + 1) * SUB, :] = pair.astype(jnp.bfloat16)
        return carry

    lax.fori_loop(0, devices, body, 0)


def gather(wanted, own, lines):
    devices = wanted.shape[0]
    return pl.pallas_call(
        gather_kernel,
        in_specs=[whole(pltpu.SMEM), whole()],
        out_specs=whole(),
        out_shape=jax.ShapeDtypeStruct((devices, lines, LANES), jnp.bfloat16),
        compiler_params=params(8),
        name="gather",
    )(wanted, own)


def bins_kernel(chunk, cap, slot_ref, fetched_ref, blocks_ref, out_ref, pick, ret):
    step = pl.program_id(0)
    devices, lines, _ = fetched_ref.shape
    samples, cells = blocks_ref.shape[1:]

    @pl.when(step == 0)
    def _():
        for d in range(devices):
            pick[pl.ds(d * lines, lines), :] = fetched_ref[d].astype(jnp.float32)
            ret[pl.ds(d * lines, lines), :] = jnp.zeros((lines, LANES), jnp.float32)

    low = lax.broadcasted_iota(jnp.int32, (SUB, LANES), 0) < 4
    lane = lax.broadcasted_iota(jnp.int32, (samples, LANES), 1) // 4

    def line(b):
        slot = slot_ref[0, b]
        return pl.multiple_of((slot // cap) * lines + (slot % cap) * SUB if lines != cap * SUB else slot * SUB, SUB)

    for g in range(chunk // 32):
        first = step * chunk + g * 32
        pairs = []
        for p in range(16):
            f0 = pick[pl.ds(line(first + 2 * p), SUB), :]
            f1 = pick[pl.ds(line(first + 2 * p + 1), SUB), :]
            left = jnp.where(low, f0, pltpu.roll(f1, 4, 0))
            right = jnp.where(low, pltpu.roll(f0, 4, 0), f1)
            pairs.append(jnp.concatenate([left, right], axis=1))
        picked = jnp.concatenate(pairs, axis=0).astype(jnp.bfloat16)
        held = jnp.zeros((samples, LANES), jnp.float32)
        for j in range(0, 32, 4):
            m = blocks_ref[pl.ds(g * 32 + j, 4)].reshape(4 * samples, cells)
            s = lax.dot_general(m, picked, (((1,), (1,)), ((), ())), preferred_element_type=jnp.float32)
            for q in range(4):
                held = jnp.where(lane == j + q, s[q * samples : (q + 1) * samples], held)
        held = held.T
        for p in range(16):
            s = held[SUB * p : SUB * p + SUB]
            s = jnp.concatenate([jnp.where(low, s, 0.0), jnp.where(low, 0.0, s)], axis=1).astype(jnp.bfloat16)
            m = blocks_ref[pl.ds(g * 32 + 2 * p, 2)].reshape(2 * samples, cells)
            a = lax.dot_general(s, m, (((1,), (0,)), ((), ())), preferred_element_type=jnp.float32)
            left, right = a[:, :LANES], a[:, LANES:]
            ret[pl.ds(line(first + 2 * p), SUB), :] = jnp.where(low, left, pltpu.roll(right, 4, 0))
            ret[pl.ds(line(first + 2 * p + 1), SUB), :] = jnp.where(low, pltpu.roll(left, 4, 0), right)

    @pl.when(step == pl.num_programs(0) - 1)
    def _():
        for d in range(devices):
            out_ref[d] = ret[pl.ds(d * lines, lines), :].astype(jnp.bfloat16)


def bins(slot, fetched, blocks, cap):
    devices, lines, _ = fetched.shape
    count, samples, cells = blocks.shape
    chunk = 64
    return pl.pallas_call(
        functools.partial(bins_kernel, chunk, cap),
        grid=(count // chunk,),
        in_specs=[
            whole(pltpu.SMEM),
            pl.BlockSpec((devices, lines, LANES), lambda i: (0, 0, 0)),
            pl.BlockSpec((chunk, samples, cells), lambda i: (i, 0, 0)),
        ],
        out_specs=pl.BlockSpec((devices, lines, LANES), lambda i: (0, 0, 0)),
        out_shape=jax.ShapeDtypeStruct((devices, lines, LANES), jnp.bfloat16),
        scratch_shapes=[pltpu.VMEM((devices * lines, LANES), jnp.float32)] * 2,
        compiler_params=params(30),
        name="bins",
    )(slot, fetched, blocks)


def laplace_kernel(field_ref, above_ref, below_ref, sides_ref, out_ref):
    beacons, rows, cols = field_ref.shape
    row = lax.broadcasted_iota(jnp.int32, (rows, cols), 0)
    col = lax.broadcasted_iota(jnp.int32, (rows, cols), 1)
    sides = sides_ref[...].T
    for k in range(beacons):
        x = field_ref[k]
        up = jnp.where(row == 0, above_ref[k : k + 1, :], pltpu.roll(x, 1, 0))
        down = jnp.where(row == rows - 1, below_ref[k : k + 1, :], pltpu.roll(x, rows - 1, 0))
        left = jnp.where(col == 0, sides[:, k : k + 1], pltpu.roll(x, 1, 1))
        right = jnp.where(col == cols - 1, sides[:, beacons + k : beacons + k + 1], pltpu.roll(x, cols - 1, 1))
        out_ref[k] = smooth_weight * (4.0 * x - (down + up + right + left))


def laplace(field, above, below, sides):
    return pl.pallas_call(
        laplace_kernel,
        in_specs=[whole()] * 4,
        out_specs=whole(),
        out_shape=jax.ShapeDtypeStruct(field.shape, jnp.float32),
        compiler_params=params(8),
        name="laplace",
    )(field, above, below, sides)


def image_kernel(wanted_ref, arrived_ref, smooth_ref, direction_ref, residual_ref, image_ref, stats_ref, even, odd):
    devices, cap = wanted_ref.shape
    beacons, rows, cols = direction_ref.shape
    bands, groups = rows // TILE_SIDE, cols // LANES
    even[...] = jnp.zeros_like(even)
    odd[...] = jnp.zeros_like(odd)

    def body(d, carry):
        for r in range(0, cap, 2):
            pair = arrived_ref[d, r * SUB : (r + 2) * SUB, :].astype(jnp.float32)
            at = pl.ds(pl.multiple_of(jnp.maximum(wanted_ref[d, r], 0) * SUB, SUB), SUB)
            even[at, :] += pair[:SUB]
            if r + 1 < cap:
                at = pl.ds(pl.multiple_of(jnp.maximum(wanted_ref[d, r + 1], 0) * SUB, SUB), SUB)
                odd[at, :] += pair[SUB:]
        return carry

    lax.fori_loop(0, devices, body, 0)
    lane = lax.broadcasted_iota(jnp.int32, (1, LANES), 1)
    stats = jnp.zeros((1, LANES), jnp.float32)
    for k in range(beacons):
        largest = jnp.zeros((SUB, LANES), jnp.float32)
        for g in range(groups):
            x = []
            for band in range(bands):
                for h in range(2):
                    at = pl.ds((band * groups + g) * 64 + h * beacons + k, SUB, stride=SUB)
                    x.append(even[at, :] + odd[at, :])
            x = swap_chunks(jnp.stack(x)).reshape(rows, LANES)
            x = x + smooth_ref[k, :, g * LANES : (g + 1) * LANES]
            image_ref[k, :, g * LANES : (g + 1) * LANES] = x
            largest = jnp.maximum(largest, jnp.max(jnp.abs(x).reshape(bands * 2, SUB, LANES), axis=0))
        largest = jnp.maximum(jnp.max(largest, axis=(0, 1), keepdims=True), 1e-30)
        x, d, r = image_ref[k], direction_ref[k], residual_ref[k]
        scaled = x * (1.0 / largest)
        for q, term in enumerate((r * r, d * x, r * scaled, scaled * scaled)):
            stats = jnp.where(lane == q * beacons + k, jnp.sum(term, axis=(0, 1), keepdims=True), stats)
        stats = jnp.where(lane == 4 * beacons + k, largest, stats)
    stats_ref[...] = jnp.broadcast_to(stats, stats_ref.shape)


def image_of(wanted, arrived, smooth, direction, residual):
    beacons, rows, cols = direction.shape
    return pl.pallas_call(
        image_kernel,
        in_specs=[whole(pltpu.SMEM)] + [whole()] * 4,
        out_specs=[whole(), whole()],
        out_shape=[
            jax.ShapeDtypeStruct(direction.shape, jnp.float32),
            jax.ShapeDtypeStruct((wanted.shape[0], LANES), jnp.float32),
        ],
        scratch_shapes=[pltpu.VMEM((beacons * rows * cols // LANES, LANES), jnp.float32)] * 2,
        compiler_params=params(16),
        name="image",
    )(wanted, arrived, smooth, direction, residual)


def update_kernel(beacons, stats_ref, solution_ref, residual_ref, direction_ref, image_ref, sol_ref, res_ref, dir_ref):
    k = pl.program_id(0)
    stats = stats_ref[...]
    lane = lax.broadcasted_iota(jnp.int32, stats.shape, 1)

    def column(q):
        return jnp.sum(jnp.where(lane == q * beacons + k, stats, 0.0), axis=1, keepdims=True)

    rr, di, ri, ii, unit = (column(q) for q in range(5))
    norm_old = jnp.sum(rr, axis=0, keepdims=True)
    alpha = norm_old / jnp.sum(di, axis=0, keepdims=True)
    size = alpha * unit
    norm_new = norm_old + jnp.sum(size * (size * ii - 2.0 * ri), axis=0, keepdims=True)
    beta = norm_new / norm_old
    d = direction_ref[...][0]
    res = residual_ref[...][0] - alpha * image_ref[...][0]
    sol_ref[...] = (solution_ref[...][0] + alpha * d)[None]
    res_ref[...] = res[None]
    dir_ref[...] = (res + beta * d)[None]


def update(stats, solution, residual, direction, image):
    beacons, rows, cols = direction.shape
    block = pl.BlockSpec((1, rows, cols), lambda k: (k, 0, 0))
    return pl.pallas_call(
        functools.partial(update_kernel, beacons),
        grid=(beacons,),
        in_specs=[pl.BlockSpec(stats.shape, lambda k: (0, 0))] + [block] * 4,
        out_specs=[block] * 3,
        out_shape=[jax.ShapeDtypeStruct(direction.shape, jnp.float32)] * 3,
        compiler_params=params(8),
        name="update",
    )(stats, solution, residual, direction, image)


def exchange(x):
    return lax.all_to_all(x, AXES, split_axis=0, concat_axis=0, tiled=True)


def shift(x, axis, step):
    size = lax.axis_size(axis)
    return lax.ppermute(x, axis, [(i, i + step) for i in range(size) if 0 <= i + step < size])


def per_device(solution, residual, direction, blocks, bin_owner, bin_tile):
    devices = lax.axis_size("tx") * lax.axis_size("ty")
    count = blocks.shape[0]
    cap = max(2, 3 * count // (2 * devices))
    lines = -(-cap // 2) * 2 * SUB

    slot, request = prep(bin_owner.reshape(1, count), bin_tile.reshape(1, count), devices, cap)
    wanted = exchange(request)
    own = tiles(direction)
    edges = direction.astype(jnp.bfloat16)
    above = shift(edges[:, -1, :], "tx", 1).astype(jnp.float32)
    below = shift(edges[:, 0, :], "tx", -1).astype(jnp.float32)
    left = shift(edges[:, :, -1], "ty", 1).astype(jnp.float32)
    right = shift(edges[:, :, 0], "ty", -1).astype(jnp.float32)
    smooth = laplace(direction, above, below, jnp.concatenate([left, right], axis=0))
    fetched = exchange(gather(wanted, own, lines))
    arrived = exchange(bins(slot, fetched, blocks, cap))
    image, stats = image_of(wanted, arrived, smooth, direction, residual)
    return update(exchange(stats), solution, residual, direction, image)


def solution(mesh):
    placed = (
        P(None, "tx", "ty"),
        P(None, "tx", "ty"),
        P(None, "tx", "ty"),
        P(AXES, None, None),
        P(AXES, None),
        P(AXES),
    )
    return jax.shard_map(
        per_device,
        mesh=mesh,
        in_specs=placed,
        out_specs=(P(None, "tx", "ty"),) * 3,
        check_vma=False,
    )
```

time: 248 us -> 98.9 us (0.40)
  blocking collectives: 80 us -> 32.8 us
  local copies, waits for them, and re-layouts: 50.9 us -> 9 us
  waiting for transfers between devices: 49.9 us -> 16.7 us
  other arithmetic: 22.1 us -> 0.02 us
  Pallas kernels: 0 us -> 20.5 us
  matrix products: 16.9 us -> 0 us
  starting transfers between devices: 26.2 us -> 18.5 us
    psum x2 -> x0, blocking collectives: 80 us -> none  [the longest x1 41.5 us: per_device(): norm_old = lax.psum(jnp.sum(residual * residual, axis=(1, 2)), ('tx', 'ty'))]
    all_to_all x0 -> x2, blocking collectives: none -> 32.8 us  [exchange(): return lax.all_to_all(x, AXES, split_axis=0, concat_axis=0, tiled=True)]
    all_to_all x3 -> x2, waiting for transfers between devices: 39 us -> 13.3 us  [exchange(): return lax.all_to_all(x, AXES, split_axis=0, concat_axis=0, tiled=True)]
    scatter x2 -> x0, local copies, waits for them, and re-layouts: 25.6 us -> none  [the longest x1 24 us: per_device(): jnp.zeros((devices * cap, beacons, cells), jnp.float32).at[slot]]
    pallas_call x0 -> x7, Pallas kernels: none -> 20.5 us  [the longest x1 10.2 us: bins(): pl.pallas_call(functools.partial(bins_kernel, chunk, cap), grid=(count //...]
    dot_general x1 -> x0, matrix products: 16.9 us -> none  [per_device(): jnp.einsum('bsc,bks->bkc', blocks, samples, preferred_element_type=jnp.fl...]
    scatter-add x1 -> x0, other arithmetic: 14.5 us -> none  [per_device(): data_tiles = jnp.zeros(own_tiles.shape, jnp.float32).at[wanted].add(arrived)]
    reshape x6 -> x0, local copies, waits for them, and re-layouts: 13 us -> none  [the longest x2 4.6 us: to_tiles(): field.reshape(beacons, across, TILE_SIDE, down, TILE_SIDE)]
  transfers between devices with their start and end apart: 7 -> 6, of which waited for: 4 -> 3; matrix products, arithmetic and copies ran while one was open for 3% -> 1% of each run, Pallas kernels for 0% -> 2%
where the time goes in v1:
time: 98.9 us; the launch traced here: 98.4 us
  blocking collectives  32.8 us (33%)
  Pallas kernels  20.5 us (21%)
  starting transfers between devices  18.5 us (19%)
  waiting for transfers between devices  16.7 us (17%)
  local copies, waits for them, and re-layouts  9 us (9%)
    all_to_all x2, blocking collectives, exchange(): return lax.all_to_all(x, AXES, split_axis=0, concat_axis=0, tiled=True)  32.8 us
    all_to_all x2, waiting for transfers between devices, exchange(): return lax.all_to_all(x, AXES, split_axis=0, concat_axis=0, tiled=True)  13.3 us
    pallas_call x1, Pallas kernels, bins(): pl.pallas_call(functools.partial(bins_kernel, chunk, cap), grid=(count //...  10.2 us
    all_to_all x2, starting transfers between devices, exchange(): return lax.all_to_all(x, AXES, split_axis=0, concat_axis=0, tiled=True)  9.92 us
    ppermute x4, starting transfers between devices, shift(): lax.ppermute(x, axis, [(i, i + step) for i in range(size) if 0 <= i + ste...  8.61 us
    unnamed x15, local copies, waits for them, and re-layouts  8.41 us
    ppermute x4, waiting for transfers between devices, shift(): lax.ppermute(x, axis, [(i, i + step) for i in range(size) if 0 <= i + ste...  3.41 us
    pallas_call x1, Pallas kernels, image_of(): pl.pallas_call(image_kernel, in_specs=[whole(pltpu.SMEM)] + [whole()] * 4...  3.34 us
  transfers between devices with their start and end apart: 6, of which 3 were waited for; matrix products, arithmetic and copies ran while one was open for 1% of the time, Pallas kernels for 2%

profile of v1, /device:TPU:0, one launch (start us, length us, event | category | flops | bytes accessed | tf_op | source)
XLA Modules:
  0.0 98.4 jit_solution(6965322141844641144)
XLA Ops:
  0.6 0.7 copy-done.5
  1.3 0.7 copy-done.6
  2.0 0.9 prep.1
  2.9 7.3 %all-to-all-start = ((s32[32,1,12]{2,1,0:T(1,128)}), s32[32,1,12]{2,1,0:T(1,128)S(1)}, u32[]{:S(2)}, u32[]{:S(2)}) async-start(s32[32,1,12]{2,1,0:T(1,128)} %bitcast.3), calls=%async_computation | async-start | bytes 32768 | tf_op jit(solution)/shard_map/all_to_all | solution.py:313
  10.2 1.0 %copy-done.1 = f32[4,128,256]{2,1,0:T(8,128)S(1)} copy-done((f32[4,128,256]{2,1,0:T(8,128)S(1)}, f32[4,128,256]{2,1,0:T(8,128)}, u32[]{:S(2)}) %copy-start.1) | copy-done | bytes 524312
  11.2 1.1 %tiles.1.tiles_ref = f32[1024,128]{1,0:T(8,128)S(1)} custom-call(f32[4,128,256]{2,1,0:T(8,128)S(1)} %copy-done.1), custom_call_target="tpu_custom_call" | custom-call | tf_op jit(solution)/shard_map/tiles/pallas_call | solution.py:84
  12.3 4.9 %all-to-all-done = s32[32,1,12]{2,1,0:T(1,128)S(1)} async-done(((s32[32,1,12]{2,1,0:T(1,128)}), s32[32,1,12]{2,1,0:T(1,128)S(1)}, u32[]{:S(2)}, u32[]{:S(2)}) %all-to-all-start) | async-done | bytes 1568 | tf_op jit(solution)/shard_map/all_to_all | solution.py:313
  17.2 2.5 %gather.1 = bf16[32,96,128]{2,1,0:T(8,128)(2,1)S(1)} custom-call(s32[32,12]{1,0:T(8,128)S(1)} %bitcast.16, f32[1024,128]{1,0:T(8,128)S(1)} %tiles.1.tiles_ref), custom_call_target="tpu_custom_call" | custom-call | tf_op jit(solution)/shard_map/gather/pallas_call | solution.py:115
  19.8 23.7 %all_to_all.32.fetched_ref = bf16[32,96,128]{2,1,0:T(8,128)(2,1)S(1)} all-to-all(bf16[32,96,128]{2,1,0:T(8,128)(2,1)S(1)} %gather.1), channel_id=1, replica_groups=mesh['tx'=4,'ty'=8] {'tx','ty'}, dimensions={0} | all-to-all | bytes 1572864 | tf_op jit(solution)/shard_map/all_to_all | solution.py:313
  43.5 5.8 %copy-done = bf16[256,128,256]{2,1,0:T(8,128)(2,1)S(1)} copy-done((bf16[256,128,256]{2,1,0:T(8,128)(2,1)S(1)}, bf16[256,128,256]{2,1,0:T(8,128)(2,1)}, u32[]{:S(2)}) %copy-start) | copy-done | bytes 16777240
  49.3 10.2 %bins.1 = bf16[32,96,128]{2,1,0:T(8,128)(2,1)} custom-call(s32[1,256]{1,0:T(1,128)S(1)} %get-tuple-element.8.slot_ref, bf16[32,96,128]{2,1,0:T(8,128)(2,1)S(1)} %all_to_all.32.fetched_ref, bf16[256,128,256]{2,1,0:T(8,128)(2,1)S(1)} %copy-done), custom_call_target="tpu_custom_call" | custom-call | tf_op jit(solution)/shard_map/bins/pallas_call | solution.py:179
  59.4 2.6 %all-to-all-start.2 = ((bf16[32,96,128]{2,1,0:T(8,128)(2,1)}), bf16[32,96,128]{2,1,0:T(8,128)(2,1)S(1)}, u32[]{:S(2)}, u32[]{:S(2)}) async-start(bf16[32,96,128]{2,1,0:T(8,128)(2,1)} %bins.1), calls=%async_computation.2 | async-start | bytes 1572864 | tf_op jit(solution)/shard_map/all_to_all | solution.py:313
  62.1 0.2 copy.16
  62.3 1.3 %collective-permute-start.3 = (bf16[4,128]{1,0:T(4,128)(2,1)S(1)}, bf16[4,128]{1,0:T(4,128)(2,1)S(1)}, u32[]{:S(2)}, u32[]{:S(2)}) collective-permute-start(bf16[4,128]{1,0:T(4,128)(2,1)S(1)} %get-tuple-element.12), channel_id=1, source_target_pairs={{1,0},{2,1},{3,2},{4,3},{5,4},{6,5},{7,6},{9,8},{10,9},{11,10},{12... | collective-permute-start | bytes 3080 | tf_op jit(solution)/shard_map/ppermute | solution.py:318
  63.6 4.5 %collective-permute-start.2 = (bf16[4,128]{1,0:T(4,128)(2,1)S(1)}, bf16[4,128]{1,0:T(4,128)(2,1)S(1)}, u32[]{:S(2)}, u32[]{:S(2)}) collective-permute-start(bf16[4,128]{1,0:T(4,128)(2,1)S(1)} %get-tuple-element.11), channel_id=1, source_target_pairs={{0,1},{1,2},{2,3},{3,4},{4,5},{5,6},{6,7},{8,9},{9,10},{10,11},{11... | collective-permute-start | bytes 3080 | tf_op jit(solution)/shard_map/ppermute | solution.py:318
  68.2 0.2 fusion
  68.6 1.5 %collective-permute-start = (bf16[4,256]{1,0:T(4,128)(2,1)S(1)}, bf16[4,256]{1,0:T(4,128)(2,1)S(1)}, u32[]{:S(2)}, u32[]{:S(2)}) collective-permute-start(bf16[4,256]{1,0:T(4,128)(2,1)S(1)} %bitcast.22), channel_id=1, source_target_pairs={{0,8},{8,16},{16,24},{1,9},{9,17},{17,25},{2,10},{10,18},{18,26},{... | collective-permute-start | bytes 6152 | tf_op jit(solution)/shard_map/ppermute | solution.py:318
  70.3 1.3 %collective-permute-start.1 = (bf16[4,256]{1,0:T(4,128)(2,1)S(1)}, bf16[4,256]{1,0:T(4,128)(2,1)S(1)}, u32[]{:S(2)}, u32[]{:S(2)}) collective-permute-start(bf16[4,256]{1,0:T(4,128)(2,1)S(1)} %bitcast.23), channel_id=1, source_target_pairs={{8,0},{16,8},{24,16},{9,1},{17,9},{25,17},{10,2},{18,10},{26,18},{... | collective-permute-start | bytes 6152 | tf_op jit(solution)/shard_map/ppermute | solution.py:318
  71.6 3.4 %collective-permute-done.1 = bf16[4,256]{1,0:T(4,128)(2,1)S(1)} collective-permute-done((bf16[4,256]{1,0:T(4,128)(2,1)S(1)}, bf16[4,256]{1,0:T(4,128)(2,1)S(1)}, u32[]{:S(2)}, u32[]{:S(2)}) %collective-permute-start.1) | collective-permute-done | bytes 2080 | tf_op jit(solution)/shard_map/ppermute | solution.py:318
  75.0 0.6 laplace.1.smooth_ref
  75.6 8.4 %all-to-all-done.2.arrived_ref = bf16[32,96,128]{2,1,0:T(8,128)(2,1)S(1)} async-done(((bf16[32,96,128]{2,1,0:T(8,128)(2,1)}), bf16[32,96,128]{2,1,0:T(8,128)(2,1)S(1)}, u32[]{:S(2)}, u32[]{:S(2)}) %all-to-all-start.2) | async-done | bytes 786464 | tf_op jit(solution)/shard_map/all_to_all | solution.py:313
  84.1 3.3 %image.1 = (f32[4,128,256]{2,1,0:T(8,128)S(1)}, f32[32,128]{1,0:T(8,128)S(1)}) custom-call(s32[32,12]{1,0:T(8,128)S(1)} %bitcast.17, bf16[32,96,128]{2,1,0:T(8,128)(2,1)S(1)} %all-to-all-done.2.arrived_ref, f32[4,128,256]{2,1,0:T(8,128)S(1)} %laplace.1.smooth_ref, f32[4,128,256]{2,1,0:T(8,128)S(1)} %copy-done.2, f32[4,128,256]{2,1,0:T(8,128)S(1)} %copy-done.3), custom_call_target="tpu_custom_call" | custom-call | tf_op jit(solution)/shard_map/image/pallas_call | solution.py:263
  87.4 9.1 %all_to_all.33 = f32[32,1,128]{2,1,0:T(1,128)S(1)} all-to-all(f32[32,1,128]{2,1,0:T(1,128)S(1)} %bitcast.19), channel_id=1, replica_groups=mesh['tx'=4,'ty'=8] {'tx','ty'}, dimensions={0} | all-to-all | bytes 32768 | tf_op jit(solution)/shard_map/all_to_all | solution.py:313
  96.5 1.9 %update.1 = (f32[4,128,256]{2,1,0:T(8,128)}, f32[4,128,256]{2,1,0:T(8,128)}, f32[4,128,256]{2,1,0:T(8,128)}) custom-call(f32[32,128]{1,0:T(8,128)S(1)} %bitcast.18, f32[4,128,256]{2,1,0:T(8,128)S(1)} %copy-done.4, f32[4,128,256]{2,1,0:T(8,128)S(1)} %copy-done.3, f32[4,128,256]{2,1,0:T(8,128)S(1)} %copy-done.2, f32[4,128,256]{2,1,0:T(8,128)S(1)} %get-tuple-element.10.image_ref), custom_call_target="tpu_custom_call" | custom-call | tf_op jit(solution)/shard_map/update/pallas_call | solution.py:301
  (19 shorter events, 0.4 us)
Async XLA Ops:
  0.6 0.7 copy-start.5
  1.3 0.7 copy-start.6
  2.9 14.3 %all-to-all-start = ((s32[32,1,12]{2,1,0:T(1,128)}), s32[32,1,12]{2,1,0:T(1,128)S(1)}, u32[]{:S(2)}, u32[]{:S(2)}) async-start(s32[32,1,12]{2,1,0:T(1,128)} %bitcast.3), calls=%async_computation | async-start | bytes 32768 | tf_op jit(solution)/shard_map/all_to_all | solution.py:313
  10.2 1.0 %copy-start.1 = (f32[4,128,256]{2,1,0:T(8,128)S(1)}, f32[4,128,256]{2,1,0:T(8,128)}, u32[]{:S(2)}) copy-start(f32[4,128,256]{2,1,0:T(8,128)} %direction_ref.3) | copy-start | bytes 1572868
  11.2 50.8 %copy-start.2 = (f32[4,128,256]{2,1,0:T(8,128)S(1)}, f32[4,128,256]{2,1,0:T(8,128)}, u32[]{:S(2)}) copy-start(f32[4,128,256]{2,1,0:T(8,128)} %direction_ref.3) | copy-start | bytes 1572868
  11.2 72.8 %copy-start.3 = (f32[4,128,256]{2,1,0:T(8,128)S(1)}, f32[4,128,256]{2,1,0:T(8,128)}, u32[]{:S(2)}) copy-start(f32[4,128,256]{2,1,0:T(8,128)} %residual_ref.3) | copy-start | bytes 1572868
  11.2 85.3 %copy-start.4 = (f32[4,128,256]{2,1,0:T(8,128)S(1)}, f32[4,128,256]{2,1,0:T(8,128)}, u32[]{:S(2)}) copy-start(f32[4,128,256]{2,1,0:T(8,128)} %solution_ref.1) | copy-start | bytes 1572868
  43.5 5.8 %copy-start = (bf16[256,128,256]{2,1,0:T(8,128)(2,1)S(1)}, bf16[256,128,256]{2,1,0:T(8,128)(2,1)}, u32[]{:S(2)}) copy-start(bf16[256,128,256]{2,1,0:T(8,128)(2,1)} %blocks_ref.1) | copy-start | bytes 50331652
  59.4 24.6 %all-to-all-start.2 = ((bf16[32,96,128]{2,1,0:T(8,128)(2,1)}), bf16[32,96,128]{2,1,0:T(8,128)(2,1)S(1)}, u32[]{:S(2)}, u32[]{:S(2)}) async-start(bf16[32,96,128]{2,1,0:T(8,128)(2,1)} %bins.1), calls=%async_computation.2 | async-start | bytes 1572864 | tf_op jit(solution)/shard_map/all_to_all | solution.py:313
  62.3 9.2 %collective-permute-start.3 = (bf16[4,128]{1,0:T(4,128)(2,1)S(1)}, bf16[4,128]{1,0:T(4,128)(2,1)S(1)}, u32[]{:S(2)}, u32[]{:S(2)}) collective-permute-start(bf16[4,128]{1,0:T(4,128)(2,1)S(1)} %get-tuple-element.12), channel_id=1, source_target_pairs={{1,0},{2,1},{3,2},{4,3},{5,4},{6,5},{7,6},{9,8},{10,9},{11,10},{12... | collective-permute-start | bytes 3080 | tf_op jit(solution)/shard_map/ppermute | solution.py:318
  63.6 7.9 %collective-permute-start.2 = (bf16[4,128]{1,0:T(4,128)(2,1)S(1)}, bf16[4,128]{1,0:T(4,128)(2,1)S(1)}, u32[]{:S(2)}, u32[]{:S(2)}) collective-permute-start(bf16[4,128]{1,0:T(4,128)(2,1)S(1)} %get-tuple-element.11), channel_id=1, source_target_pairs={{0,1},{1,2},{2,3},{3,4},{4,5},{5,6},{6,7},{8,9},{9,10},{10,11},{11... | collective-permute-start | bytes 3080 | tf_op jit(solution)/shard_map/ppermute | solution.py:318
  68.6 3.0 %collective-permute-start = (bf16[4,256]{1,0:T(4,128)(2,1)S(1)}, bf16[4,256]{1,0:T(4,128)(2,1)S(1)}, u32[]{:S(2)}, u32[]{:S(2)}) collective-permute-start(bf16[4,256]{1,0:T(4,128)(2,1)S(1)} %bitcast.22), channel_id=1, source_target_pairs={{0,8},{8,16},{16,24},{1,9},{9,17},{17,25},{2,10},{10,18},{18,26},{... | collective-permute-start | bytes 6152 | tf_op jit(solution)/shard_map/ppermute | solution.py:318
  70.3 4.8 %collective-permute-start.1 = (bf16[4,256]{1,0:T(4,128)(2,1)S(1)}, bf16[4,256]{1,0:T(4,128)(2,1)S(1)}, u32[]{:S(2)}, u32[]{:S(2)}) collective-permute-start(bf16[4,256]{1,0:T(4,128)(2,1)S(1)} %bitcast.23), channel_id=1, source_target_pairs={{8,0},{16,8},{24,16},{9,1},{17,9},{25,17},{10,2},{18,10},{26,18},{... | collective-permute-start | bytes 6152 | tf_op jit(solution)/shard_map/ppermute | solution.py:318

commit v2 on v1

v2 whole, which is shorter than its diff:
```python
import functools

import jax
import jax.numpy as jnp
from jax import lax
from jax.experimental import pallas as pl
from jax.experimental.pallas import tpu as pltpu
from jax.sharding import PartitionSpec as P

TILE_SIDE = 16
LANES = 128
SUB = 8
smooth_weight = 0.25

AXES = ("tx", "ty")


def whole(memory=pltpu.VMEM):
    return pl.BlockSpec(memory_space=memory)


def params(mib):
    return pltpu.CompilerParams(vmem_limit_bytes=mib << 20)


def swap_chunks(x):
    row = lax.broadcasted_iota(jnp.int32, (SUB, LANES), 0)
    chunk = lax.broadcasted_iota(jnp.int32, (SUB, LANES), 1) // TILE_SIDE
    for s in (1, 2, 4):
        row_bit, chunk_bit = (row & s) != 0, (chunk & s) != 0
        other = pltpu.roll(pltpu.roll(x, s, 1), LANES - TILE_SIDE * s, 2)
        if s < 4:
            up = pltpu.roll(pltpu.roll(x, SUB - s, 1), TILE_SIDE * s, 2)
            other = jnp.where(row_bit[None], other, up)
        x = jnp.where((row_bit == chunk_bit)[None], x, other)
    return x


def prep_kernel(cap, owner_ref, tile_ref, slot_ref, request_ref):
    devices, bins = request_ref.shape[0], owner_ref.shape[1]
    owner = owner_ref[...]
    member = (lax.broadcasted_iota(jnp.int32, (devices, bins), 0) == owner).astype(jnp.float32)
    earlier = (
        lax.broadcasted_iota(jnp.int32, (bins, bins), 0) < lax.broadcasted_iota(jnp.int32, (bins, bins), 1)
    ).astype(jnp.bfloat16)
    member16 = member.astype(jnp.bfloat16)
    before = jnp.dot(member16, earlier, preferred_element_type=jnp.float32)
    rank = jnp.sum(before * member, axis=0, keepdims=True).astype(jnp.int32)
    slot_ref[...] = owner * cap + rank
    place = lax.broadcasted_iota(jnp.int32, (request_ref.shape[1], bins), 0) == rank
    named = jnp.where(place, tile_ref[...] + 1, 0).astype(jnp.float32).astype(jnp.bfloat16)
    request = lax.dot_general(member16, named, (((1,), (1,)), ((), ())), preferred_element_type=jnp.float32)
    request_ref[...] = request.astype(jnp.int32) - 1


def prep(owner, tile, devices, cap):
    bins = owner.shape[1]
    return pl.pallas_call(
        functools.partial(prep_kernel, cap),
        in_specs=[whole(), whole()],
        out_specs=[whole(), whole()],
        out_shape=[
            jax.ShapeDtypeStruct((1, bins), jnp.int32),
            jax.ShapeDtypeStruct((devices, cap), jnp.int32),
        ],
        compiler_params=params(60),
        name="prep",
    )(owner, tile)


def tiles_kernel(field_ref, out_ref, top_ref, bottom_ref, sides_ref):
    beacons, rows, cols = field_ref.shape
    bands, groups = rows // TILE_SIDE, cols // LANES
    for k in range(beacons):
        for g in range(groups):
            x = field_ref[k, :, g * LANES : (g + 1) * LANES].reshape(bands * 2, SUB, LANES)
            x = swap_chunks(x.astype(jnp.bfloat16).astype(jnp.float32))
            for band in range(bands):
                for h in range(2):
                    at = (band * groups + g) * SUB * SUB + h * beacons + k
                    out_ref[pl.ds(at, SUB, stride=SUB), :] = x[band * 2 + h]
    top_ref[...] = field_ref[:, 0, :].astype(jnp.bfloat16)
    bottom_ref[...] = field_ref[:, rows - 1, :].astype(jnp.bfloat16)
    lane = lax.broadcasted_iota(jnp.int32, (rows, LANES), 1)
    ends = jnp.zeros((rows, LANES), jnp.float32)
    for k in range(beacons):
        ends = jnp.where(lane == k, field_ref[k, :, cols - 1 :], ends)
        ends = jnp.where(lane == beacons + k, field_ref[k, :, :1], ends)
    sides_ref[...] = ends.T[: 2 * beacons].astype(jnp.bfloat16)


def tiles(field):
    beacons, rows, cols = field.shape
    return pl.pallas_call(
        tiles_kernel,
        in_specs=[whole()],
        out_specs=[whole()] * 4,
        out_shape=[
            jax.ShapeDtypeStruct((beacons * rows * cols // LANES, LANES), jnp.float32),
            jax.ShapeDtypeStruct((beacons, cols), jnp.bfloat16),
            jax.ShapeDtypeStruct((beacons, cols), jnp.bfloat16),
            jax.ShapeDtypeStruct((2 * beacons, rows), jnp.bfloat16),
        ],
        compiler_params=params(8),
        name="tiles",
    )(field)


def gather_kernel(wanted_ref, tiles_ref, out_ref):
    devices, cap = wanted_ref.shape

    def at(d, r):
        return tiles_ref[pl.ds(pl.multiple_of(jnp.maximum(wanted_ref[d, r], 0) * SUB, SUB), SUB), :]

    def body(d, carry):
        for r in range(0, cap - 1, 2):
            pair = jnp.concatenate([at(d, r), at(d, r + 1)], axis=0)
            out_ref[d, r * SUB : (r + 2) * SUB, :] = pair.astype(jnp.bfloat16)
        if cap % 2:
            pair = jnp.concatenate([at(d, cap - 1), jnp.zeros((SUB, LANES), jnp.float32)], axis=0)
            out_ref[d, (cap - 1) * SUB : (cap + 1) * SUB, :] = pair.astype(jnp.bfloat16)
        return carry

    lax.fori_loop(0, devices, body, 0, unroll=4)


def gather(wanted, own, lines):
    devices = wanted.shape[0]
    return pl.pallas_call(
        gather_kernel,
        in_specs=[whole(pltpu.SMEM), whole()],
        out_specs=whole(),
        out_shape=jax.ShapeDtypeStruct((devices, lines, LANES), jnp.bfloat16),
        compiler_params=params(8),
        name="gather",
    )(wanted, own)


def bins_kernel(group, cap, slot_ref, fetched_ref, blocks_ref, out_ref, held, pick, ret, sems):
    devices, lines, _ = fetched_ref.shape
    count, samples, cells = blocks_ref.shape

    def fetch(i):
        part = pl.ds(i * group, group)
        return pltpu.make_async_copy(blocks_ref.at[part], held.at[part], sems.at[i])

    for i in range(count // group):
        fetch(i).start()
    for d in range(devices):
        pick[pl.ds(d * lines, lines), :] = fetched_ref[d].astype(jnp.float32)
        ret[pl.ds(d * lines, lines), :] = jnp.zeros((lines, LANES), jnp.float32)
    low = lax.broadcasted_iota(jnp.int32, (SUB, LANES), 0) < 4

    def line(b):
        slot = slot_ref[0, b]
        at = slot * SUB if lines == cap * SUB else (slot // cap) * lines + (slot % cap) * SUB
        return pl.multiple_of(at, SUB)

    def body(i, carry):
        fetch(i).wait()
        first = i * group
        sampled = []
        for p in range(group // 2):
            f0 = pick[pl.ds(line(first + 2 * p), SUB), :]
            f1 = pick[pl.ds(line(first + 2 * p + 1), SUB), :]
            left = jnp.where(low, f0, pltpu.roll(f1, 4, 0))
            right = jnp.where(low, pltpu.roll(f0, 4, 0), f1)
            x = jnp.concatenate([left, right], axis=1).astype(jnp.bfloat16)
            m = held[pl.ds(first + 2 * p, 2)].reshape(2 * samples, cells)
            s = lax.dot_general(x, m, (((1,), (1,)), ((), ())), preferred_element_type=jnp.float32)
            s = jnp.concatenate([jnp.where(low, s[:, :samples], 0.0), jnp.where(low, 0.0, s[:, samples:])], axis=1)
            sampled.append(s.astype(jnp.bfloat16))
        for p in range(group // 2):
            m = held[pl.ds(first + 2 * p, 2)].reshape(2 * samples, cells)
            a = jnp.dot(sampled[p], m, preferred_element_type=jnp.float32)
            left, right = a[:, :LANES], a[:, LANES:]
            ret[pl.ds(line(first + 2 * p), SUB), :] = jnp.where(low, left, pltpu.roll(right, 4, 0))
            ret[pl.ds(line(first + 2 * p + 1), SUB), :] = jnp.where(low, pltpu.roll(left, 4, 0), right)
        return carry

    lax.fori_loop(0, count // group, body, 0)
    for d in range(devices):
        out_ref[d] = ret[pl.ds(d * lines, lines), :].astype(jnp.bfloat16)


def bins(slot, fetched, blocks, cap):
    devices, lines, _ = fetched.shape
    group = 32
    return pl.pallas_call(
        functools.partial(bins_kernel, group, cap),
        in_specs=[whole(pltpu.SMEM), whole(), whole(pl.ANY)],
        out_specs=whole(),
        out_shape=jax.ShapeDtypeStruct((devices, lines, LANES), jnp.bfloat16),
        scratch_shapes=[
            pltpu.VMEM(blocks.shape, jnp.bfloat16),
            pltpu.VMEM((devices * lines, LANES), jnp.float32),
            pltpu.VMEM((devices * lines, LANES), jnp.float32),
            pltpu.SemaphoreType.DMA((blocks.shape[0] // group,)),
        ],
        compiler_params=params(50),
        name="bins",
    )(slot, fetched, blocks)


def laplace_kernel(field_ref, above_ref, below_ref, left_ref, right_ref, out_ref):
    beacons, rows, cols = field_ref.shape
    row = lax.broadcasted_iota(jnp.int32, (rows, cols), 0)
    col = lax.broadcasted_iota(jnp.int32, (rows, cols), 1)
    above, below = above_ref[...].astype(jnp.float32), below_ref[...].astype(jnp.float32)
    sides = jnp.concatenate([left_ref[...].astype(jnp.float32), right_ref[...].astype(jnp.float32)], axis=0).T
    for k in range(beacons):
        x = field_ref[k]
        up = jnp.where(row == 0, above[k : k + 1, :], pltpu.roll(x, 1, 0))
        down = jnp.where(row == rows - 1, below[k : k + 1, :], pltpu.roll(x, rows - 1, 0))
        left = jnp.where(col == 0, sides[:, k : k + 1], pltpu.roll(x, 1, 1))
        right = jnp.where(col == cols - 1, sides[:, beacons + k : beacons + k + 1], pltpu.roll(x, cols - 1, 1))
        out_ref[k] = smooth_weight * (4.0 * x - (down + up + right + left))


def laplace(field, above, below, left, right):
    return pl.pallas_call(
        laplace_kernel,
        in_specs=[whole()] * 5,
        out_specs=whole(),
        out_shape=jax.ShapeDtypeStruct(field.shape, jnp.float32),
        compiler_params=params(8),
        name="laplace",
    )(field, above, below, left, right)


def image_kernel(wanted_ref, arrived_ref, smooth_ref, direction_ref, residual_ref, image_ref, stats_ref, *sums):
    devices, cap = wanted_ref.shape
    beacons, rows, cols = direction_ref.shape
    bands, groups = rows // TILE_SIDE, cols // LANES
    for total in sums:
        total[...] = jnp.zeros_like(total)

    def body(d, carry):
        for r in range(0, cap, 2):
            pair = arrived_ref[d, r * SUB : (r + 2) * SUB, :].astype(jnp.float32)
            for q in range(min(2, cap - r)):
                at = pl.ds(pl.multiple_of(jnp.maximum(wanted_ref[d, r + q], 0) * SUB, SUB), SUB)
                sums[(r + q) % len(sums)][at, :] += pair[q * SUB : (q + 1) * SUB]
        return carry

    lax.fori_loop(0, devices, body, 0, unroll=2)
    lines = []
    units = []
    for k in range(beacons):
        unit = jnp.zeros((SUB, LANES), jnp.float32)
        for g in range(groups):
            x = []
            for band in range(bands):
                for h in range(2):
                    at = pl.ds((band * groups + g) * SUB * SUB + h * beacons + k, SUB, stride=SUB)
                    x.append(sum(total[at, :] for total in sums))
            x = swap_chunks(jnp.stack(x)).reshape(rows, LANES)
            x = x + smooth_ref[k, :, g * LANES : (g + 1) * LANES]
            image_ref[k, :, g * LANES : (g + 1) * LANES] = x
            unit = jnp.maximum(unit, jnp.max(jnp.abs(x).reshape(bands * 2, SUB, LANES), axis=0))
        unit = jnp.maximum(unit, 1e-30)
        inverse = 1.0 / unit
        terms = [jnp.zeros((SUB, LANES), jnp.float32)] * 4
        for i in range(rows // SUB):
            for g in range(groups):
                at = (k, slice(i * SUB, (i + 1) * SUB), slice(g * LANES, (g + 1) * LANES))
                x, d, r = image_ref[at], direction_ref[at], residual_ref[at]
                scaled = x * inverse
                terms = [t + v for t, v in zip(terms, (r * r, d * x, r * scaled, scaled * scaled))]
        lines.append(terms)
        units.append(unit)
    largest = [jnp.max(unit, axis=(0, 1), keepdims=True) for unit in units]
    rows_of = []
    for q in range(4):
        for k in range(beacons):
            t = lines[k][q]
            if q >= 2:
                share = units[k] * (1.0 / largest[k])
                t = t * share if q == 2 else t * share * share
            rows_of.append(jnp.sum(t, axis=0, keepdims=True))
    for k in range(beacons):
        first = lax.broadcasted_iota(jnp.int32, (1, LANES), 1) == 0
        rows_of.append(jnp.where(first, largest[k], 0.0))
    rows_of.append(jnp.zeros((LANES - len(rows_of), LANES), jnp.float32))
    stats = jnp.sum(jnp.concatenate(rows_of, axis=0).T, axis=0, keepdims=True)
    stats_ref[...] = jnp.broadcast_to(stats, stats_ref.shape)


def image_of(wanted, arrived, smooth, direction, residual):
    beacons, rows, cols = direction.shape
    return pl.pallas_call(
        image_kernel,
        in_specs=[whole(pltpu.SMEM)] + [whole()] * 4,
        out_specs=[whole(), whole()],
        out_shape=[
            jax.ShapeDtypeStruct(direction.shape, jnp.float32),
            jax.ShapeDtypeStruct((wanted.shape[0], LANES), jnp.float32),
        ],
        scratch_shapes=[pltpu.VMEM((beacons * rows * cols // LANES, LANES), jnp.float32)] * 4,
        compiler_params=params(16),
        name="image",
    )(wanted, arrived, smooth, direction, residual)


def update_kernel(
    stats_ref, solution_ref, residual_ref, direction_ref, image_ref, sol_ref, res_ref, dir_ref, sol, res, dire, sems
):
    beacons = direction_ref.shape[0]
    stats = stats_ref[...]

    def column(x, q):
        return pltpu.roll(x, LANES - q * beacons, 1) if q else x

    total = jnp.sum(stats, axis=0, keepdims=True)
    total = jnp.broadcast_to(total, (SUB, LANES))
    alpha = total / column(total, 1)
    size = alpha[:1] * column(stats, 4)
    moved = jnp.sum(size * (size * column(stats, 3) - 2.0 * column(stats, 2)), axis=0, keepdims=True)
    beta = (total + moved) / total
    copies = []
    for k in range(beacons):
        a, b = alpha[:1, k : k + 1], beta[:1, k : k + 1]
        d = direction_ref[k]
        r = residual_ref[k] - a * image_ref[k]
        sol[k] = solution_ref[k] + a * d
        res[k] = r
        dire[k] = r + b * d
        for q, (held, out) in enumerate(((sol, sol_ref), (res, res_ref), (dire, dir_ref))):
            copies.append(pltpu.make_async_copy(held.at[k], out.at[k], sems.at[q, k]))
            copies[-1].start()
    for copy in copies:
        copy.wait()


def update(stats, solution, residual, direction, image):
    return pl.pallas_call(
        update_kernel,
        in_specs=[whole()] * 5,
        out_specs=[whole(pl.ANY)] * 3,
        out_shape=[jax.ShapeDtypeStruct(direction.shape, jnp.float32)] * 3,
        scratch_shapes=[pltpu.VMEM(direction.shape, jnp.float32)] * 3
        + [pltpu.SemaphoreType.DMA((3, direction.shape[0]))],
        compiler_params=params(16),
        name="update",
    )(stats, solution, residual, direction, image)


def exchange(x):
    return lax.all_to_all(x, AXES, split_axis=0, concat_axis=0, tiled=True)


def shift(x, axis, step):
    size = lax.axis_size(axis)
    return lax.ppermute(x, axis, [(i, i + step) for i in range(size) if 0 <= i + step < size])


def per_device(solution, residual, direction, blocks, bin_owner, bin_tile):
    devices = lax.axis_size("tx") * lax.axis_size("ty")
    count = blocks.shape[0]
    cap = max(2, 3 * count // (2 * devices))
    lines = -(-cap // 2) * 2 * SUB

    slot, request = prep(bin_owner.reshape(1, count), bin_tile.reshape(1, count), devices, cap)
    wanted = exchange(request)
    own, top, bottom, sides = tiles(direction)
    above, below = shift(bottom, "tx", 1), shift(top, "tx", -1)
    beacons = direction.shape[0]
    left, right = shift(sides[:beacons], "ty", 1), shift(sides[beacons:], "ty", -1)
    smooth = laplace(direction, above, below, left, right)
    fetched = exchange(gather(wanted, own, lines))
    arrived = exchange(bins(slot, fetched, blocks, cap))
    image, stats = image_of(wanted, arrived, smooth, direction, residual)
    return update(exchange(stats), solution, residual, direction, image)


def solution(mesh):
    placed = (
        P(None, "tx", "ty"),
        P(None, "tx", "ty"),
        P(None, "tx", "ty"),
        P(AXES, None, None),
        P(AXES, None),
        P(AXES),
    )
    return jax.shard_map(
        per_device,
        mesh=mesh,
        in_specs=placed,
        out_specs=(P(None, "tx", "ty"),) * 3,
        check_vma=False,
    )
```

time: 98.9 us -> 91.8 us (0.928)
  local copies, waits for them, and re-layouts: 9 us -> 1.73 us
    unnamed x15 -> x10, local copies, waits for them, and re-layouts: 8.41 us -> 1.73 us
    all_to_all x2, waiting for transfers between devices: 13.3 us -> 15.6 us  [exchange(): return lax.all_to_all(x, AXES, split_axis=0, concat_axis=0, tiled=True)]
    ppermute x4, waiting for transfers between devices: 3.41 us -> 1.29 us  [shift(): lax.ppermute(x, axis, [(i, i + step) for i in range(size) if 0 <= i + ste...]
    pallas_call x1, Pallas kernels: 2.54 us -> 1.45 us  [gather(): pl.pallas_call(gather_kernel, in_specs=[whole(pltpu.SMEM), whole()], out_...]
  transfers between devices with their start and end apart: 6 -> 6, of which waited for: 3 -> 4; matrix products, arithmetic and copies ran while one was open for 1% -> 0% of each run, Pallas kernels for 2% -> 2%
where the time goes in v2:
time: 91.8 us; the launch traced here: 91.4 us
  blocking collectives  32.8 us (36%)
  Pallas kernels  20.1 us (22%)
  starting transfers between devices  19.1 us (21%)
  waiting for transfers between devices  16.9 us (18%)
  local copies, waits for them, and re-layouts  1.73 us (2%)
    all_to_all x2, blocking collectives, exchange(): return lax.all_to_all(x, AXES, split_axis=0, concat_axis=0, tiled=True)  32.8 us
    all_to_all x2, waiting for transfers between devices, exchange(): return lax.all_to_all(x, AXES, split_axis=0, concat_axis=0, tiled=True)  15.6 us
    pallas_call x1, Pallas kernels, bins(): pl.pallas_call(functools.partial(bins_kernel, group, cap), in_specs=[whol...  10.7 us
    all_to_all x2, starting transfers between devices, exchange(): return lax.all_to_all(x, AXES, split_axis=0, concat_axis=0, tiled=True)  9.94 us
    ppermute x4, starting transfers between devices, shift(): lax.ppermute(x, axis, [(i, i + step) for i in range(size) if 0 <= i + ste...  9.15 us
    pallas_call x1, Pallas kernels, image_of(): pl.pallas_call(image_kernel, in_specs=[whole(pltpu.SMEM)] + [whole()] * 4...  3.17 us
  transfers between devices with their start and end apart: 6, of which 4 were waited for; matrix products, arithmetic and copies ran while one was open for 0% of the time, Pallas kernels for 2%

profile of v2, /device:TPU:0, one launch (start us, length us, event | category | flops | bytes accessed | tf_op | source)
XLA Modules:
  0.0 91.4 jit_solution(15240619626428559309)
XLA Ops:
  0.6 1.6 %prep.1 = (s32[1,256]{1,0:T(1,128)}, s32[32,12]{1,0:T(8,128)}) custom-call(s32[1,256]{1,0:T(1,128)} %bitcast.15, s32[1,256]{1,0:T(1,128)} %bitcast.16), custom_call_target="tpu_custom_call" | custom-call | tf_op jit(solution)/shard_map/prep/pallas_call | solution.py:58
  2.2 7.3 %all-to-all-start = ((s32[32,1,12]{2,1,0:T(1,128)}), s32[32,1,12]{2,1,0:T(1,128)S(1)}, u32[]{:S(2)}, u32[]{:S(2)}) async-start(s32[32,1,12]{2,1,0:T(1,128)} %bitcast.14), calls=%async_computation | async-start | bytes 32768 | tf_op jit(solution)/shard_map/all_to_all | solution.py:349
  9.5 0.0 copy-start
  9.5 1.0 %copy-done = f32[4,128,256]{2,1,0:T(8,128)S(1)} copy-done((f32[4,128,256]{2,1,0:T(8,128)S(1)}, f32[4,128,256]{2,1,0:T(8,128)}, u32[]{:S(2)}) %copy-start) | copy-done | bytes 524312
  10.6 1.3 %tiles.1 = (f32[1024,128]{1,0:T(8,128)S(1)}, bf16[4,256]{1,0:T(4,128)(2,1)S(1)}, bf16[4,256]{1,0:T(4,128)(2,1)S(1)}, bf16[8,128]{1,0:T(8,128)(2,1)S(1)}) custom-call(f32[4,128,256]{2,1,0:T(8,128)S(1)} %copy-done), custom_call_target="tpu_custom_call" | custom-call | tf_op jit(solution)/shard_map/tiles/pallas_call | solution.py:94
  11.9 4.7 %all-to-all-done = s32[32,1,12]{2,1,0:T(1,128)S(1)} async-done(((s32[32,1,12]{2,1,0:T(1,128)}), s32[32,1,12]{2,1,0:T(1,128)S(1)}, u32[]{:S(2)}, u32[]{:S(2)}) %all-to-all-start) | async-done | bytes 1568 | tf_op jit(solution)/shard_map/all_to_all | solution.py:349
  16.6 1.4 %gather.1 = bf16[32,96,128]{2,1,0:T(8,128)(2,1)S(1)} custom-call(s32[32,12]{1,0:T(8,128)S(1)} %bitcast.10, f32[1024,128]{1,0:T(8,128)S(1)} %get-tuple-element.13.tiles_ref), custom_call_target="tpu_custom_call" | custom-call | tf_op jit(solution)/shard_map/gather/pallas_call | solution.py:129
  18.0 23.7 %all_to_all.32.fetched_ref = bf16[32,96,128]{2,1,0:T(8,128)(2,1)S(1)} all-to-all(bf16[32,96,128]{2,1,0:T(8,128)(2,1)S(1)} %gather.1), channel_id=1, replica_groups=mesh['tx'=4,'ty'=8] {'tx','ty'}, dimensions={0} | all-to-all | bytes 1572864 | tf_op jit(solution)/shard_map/all_to_all | solution.py:349
  41.7 0.7 copy-done.4
  42.4 10.7 %bins.1 = bf16[32,96,128]{2,1,0:T(8,128)(2,1)} custom-call(s32[1,256]{1,0:T(1,128)S(1)} %copy-done.4, bf16[32,96,128]{2,1,0:T(8,128)(2,1)S(1)} %all_to_all.32.fetched_ref, bf16[256,128,256]{2,1,0:T(8,128)(2,1)} %blocks_ref.1), custom_call_target="tpu_custom_call" | custom-call | tf_op jit(solution)/shard_map/bins/pallas_call | solution.py:189
  53.1 2.6 %all-to-all-start.2 = ((bf16[32,96,128]{2,1,0:T(8,128)(2,1)}), bf16[32,96,128]{2,1,0:T(8,128)(2,1)S(1)}, u32[]{:S(2)}, u32[]{:S(2)}) async-start(bf16[32,96,128]{2,1,0:T(8,128)(2,1)} %bins.1), calls=%async_computation.2 | async-start | bytes 1572864 | tf_op jit(solution)/shard_map/all_to_all | solution.py:349
  55.8 2.0 %collective-permute-start = (bf16[4,256]{1,0:T(4,128)(2,1)S(1)}, bf16[4,256]{1,0:T(4,128)(2,1)S(1)}, u32[]{:S(2)}, u32[]{:S(2)}) collective-permute-start(bf16[4,256]{1,0:T(4,128)(2,1)S(1)} %get-tuple-element.14), channel_id=1, source_target_pairs={{0,8},{8,16},{16,24},{1,9},{9,17},{17,25},{2,10},{10,18},{18,26},{... | collective-permute-start | bytes 6152 | tf_op jit(solution)/shard_map/ppermute | solution.py:354
  57.8 1.3 %collective-permute-start.1 = (bf16[4,256]{1,0:T(4,128)(2,1)S(1)}, bf16[4,256]{1,0:T(4,128)(2,1)S(1)}, u32[]{:S(2)}, u32[]{:S(2)}) collective-permute-start(bf16[4,256]{1,0:T(4,128)(2,1)S(1)} %get-tuple-element.15), channel_id=1, source_target_pairs={{8,0},{16,8},{24,16},{9,1},{17,9},{25,17},{10,2},{18,10},{26,18},{... | collective-permute-start | bytes 6152 | tf_op jit(solution)/shard_map/ppermute | solution.py:354
  59.1 1.3 %collective-permute-start.3 = (bf16[4,128]{1,0:T(4,128)(2,1)S(1)}, bf16[4,128]{1,0:T(4,128)(2,1)S(1)}, u32[]{:S(2)}, u32[]{:S(2)}) collective-permute-start(bf16[4,128]{1,0:T(4,128)(2,1)S(1)} %get-tuple-element.19), channel_id=1, source_target_pairs={{1,0},{2,1},{3,2},{4,3},{5,4},{6,5},{7,6},{9,8},{10,9},{11,10},{12... | collective-permute-start | bytes 3080 | tf_op jit(solution)/shard_map/ppermute | solution.py:354
  60.4 4.5 %collective-permute-start.2 = (bf16[4,128]{1,0:T(4,128)(2,1)S(1)}, bf16[4,128]{1,0:T(4,128)(2,1)S(1)}, u32[]{:S(2)}, u32[]{:S(2)}) collective-permute-start(bf16[4,128]{1,0:T(4,128)(2,1)S(1)} %get-tuple-element.20), channel_id=1, source_target_pairs={{0,1},{1,2},{2,3},{3,4},{4,5},{5,6},{6,7},{8,9},{9,10},{10,11},{11... | collective-permute-start | bytes 3080 | tf_op jit(solution)/shard_map/ppermute | solution.py:354
  64.9 0.5 collective-permute-done.3.right_ref
  65.5 0.8 collective-permute-done.2.left_ref
  66.2 0.0 collective-permute-done.above_ref
  66.2 0.0 collective-permute-done.1.below_ref
  66.2 0.6 laplace.1.smooth_ref
  66.8 10.9 %all-to-all-done.2.arrived_ref = bf16[32,96,128]{2,1,0:T(8,128)(2,1)S(1)} async-done(((bf16[32,96,128]{2,1,0:T(8,128)(2,1)}), bf16[32,96,128]{2,1,0:T(8,128)(2,1)S(1)}, u32[]{:S(2)}, u32[]{:S(2)}) %all-to-all-start.2) | async-done | bytes 786464 | tf_op jit(solution)/shard_map/all_to_all | solution.py:349
  77.7 3.2 %image.1 = (f32[4,128,256]{2,1,0:T(8,128)S(1)}, f32[32,128]{1,0:T(8,128)S(1)}) custom-call(s32[32,12]{1,0:T(8,128)S(1)} %bitcast.11, bf16[32,96,128]{2,1,0:T(8,128)(2,1)S(1)} %all-to-all-done.2.arrived_ref, f32[4,128,256]{2,1,0:T(8,128)S(1)} %laplace.1.smooth_ref, f32[4,128,256]{2,1,0:T(8,128)S(1)} %copy-done.1, f32[4,128,256]{2,1,0:T(8,128)S(1)} %copy-done.2), custom_call_target="tpu_custom_call" | custom-call | tf_op jit(solution)/shard_map/image/pallas_call | solution.py:291
  80.9 9.1 %all_to_all.33 = f32[32,1,128]{2,1,0:T(1,128)S(1)} all-to-all(f32[32,1,128]{2,1,0:T(1,128)S(1)} %bitcast.13), channel_id=1, replica_groups=mesh['tx'=4,'ty'=8] {'tx','ty'}, dimensions={0} | all-to-all | bytes 32768 | tf_op jit(solution)/shard_map/all_to_all | solution.py:349
  90.0 1.4 %update.1 = (f32[4,128,256]{2,1,0:T(8,128)}, f32[4,128,256]{2,1,0:T(8,128)}, f32[4,128,256]{2,1,0:T(8,128)}) custom-call(f32[32,128]{1,0:T(8,128)S(1)} %bitcast.12, f32[4,128,256]{2,1,0:T(8,128)S(1)} %copy-done.3, f32[4,128,256]{2,1,0:T(8,128)S(1)} %copy-done.2, f32[4,128,256]{2,1,0:T(8,128)S(1)} %copy-done.1, f32[4,128,256]{2,1,0:T(8,128)S(1)} %get-tuple-element.18.image_ref), custom_call_target="tpu_custom_call" | custom-call | tf_op jit(solution)/shard_map/update/pallas_call | solution.py:336
  (8 shorter events, 0.0 us)
Async XLA Ops:
  2.2 14.3 %all-to-all-start = ((s32[32,1,12]{2,1,0:T(1,128)}), s32[32,1,12]{2,1,0:T(1,128)S(1)}, u32[]{:S(2)}, u32[]{:S(2)}) async-start(s32[32,1,12]{2,1,0:T(1,128)} %bitcast.14), calls=%async_computation | async-start | bytes 32768 | tf_op jit(solution)/shard_map/all_to_all | solution.py:349
  9.5 1.0 %copy-start = (f32[4,128,256]{2,1,0:T(8,128)S(1)}, f32[4,128,256]{2,1,0:T(8,128)}, u32[]{:S(2)}) copy-start(f32[4,128,256]{2,1,0:T(8,128)} %direction_ref.3) | copy-start | bytes 1572868
  10.6 55.7 %copy-start.1 = (f32[4,128,256]{2,1,0:T(8,128)S(1)}, f32[4,128,256]{2,1,0:T(8,128)}, u32[]{:S(2)}) copy-start(f32[4,128,256]{2,1,0:T(8,128)} %direction_ref.3) | copy-start | bytes 1572868
  10.6 67.1 %copy-start.2 = (f32[4,128,256]{2,1,0:T(8,128)S(1)}, f32[4,128,256]{2,1,0:T(8,128)}, u32[]{:S(2)}) copy-start(f32[4,128,256]{2,1,0:T(8,128)} %residual_ref.3) | copy-start | bytes 1572868
  10.6 79.4 %copy-start.3 = (f32[4,128,256]{2,1,0:T(8,128)S(1)}, f32[4,128,256]{2,1,0:T(8,128)}, u32[]{:S(2)}) copy-start(f32[4,128,256]{2,1,0:T(8,128)} %solution_ref.1) | copy-start | bytes 1572868
  41.7 0.7 copy-start.4
  53.1 24.6 %all-to-all-start.2 = ((bf16[32,96,128]{2,1,0:T(8,128)(2,1)}), bf16[32,96,128]{2,1,0:T(8,128)(2,1)S(1)}, u32[]{:S(2)}, u32[]{:S(2)}) async-start(bf16[32,96,128]{2,1,0:T(8,128)(2,1)} %bins.1), calls=%async_computation.2 | async-start | bytes 1572864 | tf_op jit(solution)/shard_map/all_to_all | solution.py:349
  55.8 10.5 %collective-permute-start = (bf16[4,256]{1,0:T(4,128)(2,1)S(1)}, bf16[4,256]{1,0:T(4,128)(2,1)S(1)}, u32[]{:S(2)}, u32[]{:S(2)}) collective-permute-start(bf16[4,256]{1,0:T(4,128)(2,1)S(1)} %get-tuple-element.14), channel_id=1, source_target_pairs={{0,8},{8,16},{16,24},{1,9},{9,17},{17,25},{2,10},{10,18},{18,26},{... | collective-permute-start | bytes 6152 | tf_op jit(solution)/shard_map/ppermute | solution.py:354
  57.8 8.5 %collective-permute-start.1 = (bf16[4,256]{1,0:T(4,128)(2,1)S(1)}, bf16[4,256]{1,0:T(4,128)(2,1)S(1)}, u32[]{:S(2)}, u32[]{:S(2)}) collective-permute-start(bf16[4,256]{1,0:T(4,128)(2,1)S(1)} %get-tuple-element.15), channel_id=1, source_target_pairs={{8,0},{16,8},{24,16},{9,1},{17,9},{25,17},{10,2},{18,10},{26,18},{... | collective-permute-start | bytes 6152 | tf_op jit(solution)/shard_map/ppermute | solution.py:354
  59.1 6.4 %collective-permute-start.3 = (bf16[4,128]{1,0:T(4,128)(2,1)S(1)}, bf16[4,128]{1,0:T(4,128)(2,1)S(1)}, u32[]{:S(2)}, u32[]{:S(2)}) collective-permute-start(bf16[4,128]{1,0:T(4,128)(2,1)S(1)} %get-tuple-element.19), channel_id=1, source_target_pairs={{1,0},{2,1},{3,2},{4,3},{5,4},{6,5},{7,6},{9,8},{10,9},{11,10},{12... | collective-permute-start | bytes 3080 | tf_op jit(solution)/shard_map/ppermute | solution.py:354
  60.4 5.8 %collective-permute-start.2 = (bf16[4,128]{1,0:T(4,128)(2,1)S(1)}, bf16[4,128]{1,0:T(4,128)(2,1)S(1)}, u32[]{:S(2)}, u32[]{:S(2)}) collective-permute-start(bf16[4,128]{1,0:T(4,128)(2,1)S(1)} %get-tuple-element.20), channel_id=1, source_target_pairs={{0,1},{1,2},{2,3},{3,4},{4,5},{5,6},{6,7},{8,9},{9,10},{10,11},{11... | collective-permute-start | bytes 3080 | tf_op jit(solution)/shard_map/ppermute | solution.py:354

commit v3 on v2

--- a/solution.py
+++ b/solution.py
@@ -25,44 +25,53 @@
 
 def swap_chunks(x):
     row = lax.broadcasted_iota(jnp.int32, (SUB, LANES), 0)
-    chunk = lax.broadcasted_iota(jnp.int32, (SUB, LANES), 1) // TILE_SIDE
+    chunk = SUB - 1 - lax.broadcasted_iota(jnp.int32, (SUB, LANES), 1) // TILE_SIDE
+    x = pltpu.roll(x, 0, 2, stride=TILE_SIDE, stride_axis=1)
     for s in (1, 2, 4):
-        row_bit, chunk_bit = (row & s) != 0, (chunk & s) != 0
-        other = pltpu.roll(pltpu.roll(x, s, 1), LANES - TILE_SIDE * s, 2)
-        if s < 4:
-            up = pltpu.roll(pltpu.roll(x, SUB - s, 1), TILE_SIDE * s, 2)
-            other = jnp.where(row_bit[None], other, up)
-        x = jnp.where((row_bit == chunk_bit)[None], x, other)
+        x = jnp.where(((chunk & s) != 0)[None], pltpu.roll(x, s, 1), x)
+    x = pltpu.roll(x, TILE_SIDE, 2, stride=TILE_SIDE, stride_axis=1)
+    x = pltpu.roll(x, 4, 1)
+    for s in (1, 2):
+        x = jnp.where(((row & s) != 0)[None], pltpu.roll(x, s, 1), pltpu.roll(x, SUB - s, 1))
     return x
 
 
-def prep_kernel(cap, owner_ref, tile_ref, slot_ref, request_ref):
+def prep_kernel(step, owner_hbm, tile_hbm, line_ref, request_ref, owner_ref, tile_ref, sems):
     devices, bins = request_ref.shape[0], owner_ref.shape[1]
-    owner = owner_ref[...]
-    member = (lax.broadcasted_iota(jnp.int32, (devices, bins), 0) == owner).astype(jnp.float32)
+    copies = [
+        pltpu.make_async_copy(a, b, sems.at[i])
+        for i, (a, b) in enumerate(((owner_hbm, owner_ref), (tile_hbm, tile_ref)))
+    ]
+    for copy in copies:
+        copy.start()
     earlier = (
         lax.broadcasted_iota(jnp.int32, (bins, bins), 0) < lax.broadcasted_iota(jnp.int32, (bins, bins), 1)
     ).astype(jnp.bfloat16)
+    copies[0].wait()
+    owner = owner_ref[...]
+    member = (lax.broadcasted_iota(jnp.int32, (devices, bins), 0) == owner).astype(jnp.float32)
     member16 = member.astype(jnp.bfloat16)
     before = jnp.dot(member16, earlier, preferred_element_type=jnp.float32)
     rank = jnp.sum(before * member, axis=0, keepdims=True).astype(jnp.int32)
-    slot_ref[...] = owner * cap + rank
+    line_ref[...] = owner * step + rank * SUB
     place = lax.broadcasted_iota(jnp.int32, (request_ref.shape[1], bins), 0) == rank
-    named = jnp.where(place, tile_ref[...] + 1, 0).astype(jnp.float32).astype(jnp.bfloat16)
+    copies[1].wait()
+    named = jnp.where(place, tile_ref[...], 0).astype(jnp.float32).astype(jnp.bfloat16)
     request = lax.dot_general(member16, named, (((1,), (1,)), ((), ())), preferred_element_type=jnp.float32)
-    request_ref[...] = request.astype(jnp.int32) - 1
-
-
-def prep(owner, tile, devices, cap):
+    request_ref[...] = request.astype(jnp.int32) * SUB
+
+
+def prep(owner, tile, devices, cap, lines):
     bins = owner.shape[1]
     return pl.pallas_call(
-        functools.partial(prep_kernel, cap),
-        in_specs=[whole(), whole()],
-        out_specs=[whole(), whole()],
+        functools.partial(prep_kernel, lines),
+        in_specs=[whole(pl.ANY)] * 2,
+        out_specs=[whole()] * 2,
         out_shape=[
             jax.ShapeDtypeStruct((1, bins), jnp.int32),
             jax.ShapeDtypeStruct((devices, cap), jnp.int32),
         ],
+        scratch_shapes=[pltpu.VMEM((1, bins), jnp.int32)] * 2 + [pltpu.SemaphoreType.DMA((2,))],
         compiler_params=params(60),
         name="prep",
     )(owner, tile)
@@ -110,7 +119,7 @@
     devices, cap = wanted_ref.shape
 
     def at(d, r):
-        return tiles_ref[pl.ds(pl.multiple_of(jnp.maximum(wanted_ref[d, r], 0) * SUB, SUB), SUB), :]
+        return tiles_ref[pl.ds(pl.multiple_of(wanted_ref[d, r], SUB), SUB), :]
 
     def body(d, carry):
         for r in range(0, cap - 1, 2):
@@ -136,70 +145,94 @@
     )(wanted, own)
 
 
-def bins_kernel(group, cap, slot_ref, fetched_ref, blocks_ref, out_ref, held, pick, ret, sems):
+def bins_kernel(
+    group, line_ref, fetched_ref, blocks_ref, out_ref, held_ref, turn_a, turn_b, samp_a, samp_b, pick, ret, sems
+):
     devices, lines, _ = fetched_ref.shape
     count, samples, cells = blocks_ref.shape
+    groups, pairs = count // group, group // 2
 
     def fetch(i):
         part = pl.ds(i * group, group)
-        return pltpu.make_async_copy(blocks_ref.at[part], held.at[part], sems.at[i])
-
-    for i in range(count // group):
+        return pltpu.make_async_copy(blocks_ref.at[part], held_ref.at[part], sems.at[i])
+
+    for i in range(groups):
         fetch(i).start()
     for d in range(devices):
         pick[pl.ds(d * lines, lines), :] = fetched_ref[d].astype(jnp.float32)
         ret[pl.ds(d * lines, lines), :] = jnp.zeros((lines, LANES), jnp.float32)
+    samp_b[...] = jnp.zeros_like(samp_b)
     low = lax.broadcasted_iota(jnp.int32, (SUB, LANES), 0) < 4
 
+    def weights(g, p):
+        return held_ref[pl.ds(g * group + 2 * p, 2)].reshape(2 * samples, cells)
+
+    def turn(g, to):
+        for p in range(pairs):
+            to[p] = weights(g, p).T
+
     def line(b):
-        slot = slot_ref[0, b]
-        at = slot * SUB if lines == cap * SUB else (slot // cap) * lines + (slot % cap) * SUB
-        return pl.multiple_of(at, SUB)
-
-    def body(i, carry):
-        fetch(i).wait()
-        first = i * group
-        sampled = []
-        for p in range(group // 2):
-            f0 = pick[pl.ds(line(first + 2 * p), SUB), :]
-            f1 = pick[pl.ds(line(first + 2 * p + 1), SUB), :]
+        return pl.ds(pl.multiple_of(line_ref[0, b], SUB), SUB)
+
+    def sample(g, turned, to):
+        for p in range(pairs):
+            f0 = pick[line(g * group + 2 * p), :]
+            f1 = pick[line(g * group + 2 * p + 1), :]
             left = jnp.where(low, f0, pltpu.roll(f1, 4, 0))
             right = jnp.where(low, pltpu.roll(f0, 4, 0), f1)
             x = jnp.concatenate([left, right], axis=1).astype(jnp.bfloat16)
-            m = held[pl.ds(first + 2 * p, 2)].reshape(2 * samples, cells)
-            s = lax.dot_general(x, m, (((1,), (1,)), ((), ())), preferred_element_type=jnp.float32)
-            s = jnp.concatenate([jnp.where(low, s[:, :samples], 0.0), jnp.where(low, 0.0, s[:, samples:])], axis=1)
-            sampled.append(s.astype(jnp.bfloat16))
-        for p in range(group // 2):
-            m = held[pl.ds(first + 2 * p, 2)].reshape(2 * samples, cells)
-            a = jnp.dot(sampled[p], m, preferred_element_type=jnp.float32)
+            s = jnp.dot(x, turned[p], preferred_element_type=jnp.float32)
+            to[p] = jnp.concatenate([jnp.where(low, s[:, :samples], 0.0), jnp.where(low, 0.0, s[:, samples:])], axis=1)
+
+    def spread(g, sampled):
+        for p in range(pairs):
+            a = jnp.dot(sampled[p].astype(jnp.bfloat16), weights(g, p), preferred_element_type=jnp.float32)
             left, right = a[:, :LANES], a[:, LANES:]
-            ret[pl.ds(line(first + 2 * p), SUB), :] = jnp.where(low, left, pltpu.roll(right, 4, 0))
-            ret[pl.ds(line(first + 2 * p + 1), SUB), :] = jnp.where(low, pltpu.roll(left, 4, 0), right)
+            ret[line(g * group + 2 * p), :] = jnp.where(low, left, pltpu.roll(right, 4, 0))
+            ret[line(g * group + 2 * p + 1), :] = jnp.where(low, pltpu.roll(left, 4, 0), right)
+
+    fetch(0).wait()
+    turn(0, turn_a)
+
+    def body(i, carry):
+        g = 2 * i
+        fetch(g + 1).wait()
+
+        @pl.when(g + 2 < groups)
+        def _():
+            fetch(g + 2).wait()
+
+        turn(g + 1, turn_b)
+        sample(g, turn_a, samp_a)
+        spread(jnp.maximum(g - 1, 0), samp_b)
+        turn(jnp.minimum(g + 2, groups - 1), turn_a)
+        sample(g + 1, turn_b, samp_b)
+        spread(g, samp_a)
         return carry
 
-    lax.fori_loop(0, count // group, body, 0)
+    lax.fori_loop(0, groups // 2, body, 0)
+    spread(groups - 1, samp_b)
     for d in range(devices):
         out_ref[d] = ret[pl.ds(d * lines, lines), :].astype(jnp.bfloat16)
 
 
-def bins(slot, fetched, blocks, cap):
+def bins(line, fetched, blocks):
     devices, lines, _ = fetched.shape
-    group = 32
-    return pl.pallas_call(
-        functools.partial(bins_kernel, group, cap),
-        in_specs=[whole(pltpu.SMEM), whole(), whole(pl.ANY)],
+    count, samples, cells = blocks.shape
+    group = 16
+    return pl.pallas_call(
+        functools.partial(bins_kernel, group),
+        in_specs=[whole(pltpu.SMEM), whole()] + [whole(pl.ANY)],
         out_specs=whole(),
         out_shape=jax.ShapeDtypeStruct((devices, lines, LANES), jnp.bfloat16),
-        scratch_shapes=[
-            pltpu.VMEM(blocks.shape, jnp.bfloat16),
-            pltpu.VMEM((devices * lines, LANES), jnp.float32),
-            pltpu.VMEM((devices * lines, LANES), jnp.float32),
-            pltpu.SemaphoreType.DMA((blocks.shape[0] // group,)),
-        ],
+        scratch_shapes=[pltpu.VMEM(blocks.shape, jnp.bfloat16)]
+        + [pltpu.VMEM((group // 2, cells, 2 * samples), jnp.bfloat16)] * 2
+        + [pltpu.VMEM((group // 2, SUB, 2 * samples), jnp.float32)] * 2
+        + [pltpu.VMEM((devices * lines, LANES), jnp.float32)] * 2
+        + [pltpu.SemaphoreType.DMA((count // group,))],
         compiler_params=params(50),
         name="bins",
-    )(slot, fetched, blocks)
+    )(line, fetched, blocks)
 
 
 def laplace_kernel(field_ref, above_ref, below_ref, left_ref, right_ref, out_ref):
@@ -239,7 +272,7 @@
         for r in range(0, cap, 2):
             pair = arrived_ref[d, r * SUB : (r + 2) * SUB, :].astype(jnp.float32)
             for q in range(min(2, cap - r)):
-                at = pl.ds(pl.multiple_of(jnp.maximum(wanted_ref[d, r + q], 0) * SUB, SUB), SUB)
+                at = pl.ds(pl.multiple_of(wanted_ref[d, r + q], SUB), SUB)
                 sums[(r + q) % len(sums)][at, :] += pair[q * SUB : (q + 1) * SUB]
         return carry
 
@@ -360,7 +393,7 @@
     cap = max(2, 3 * count // (2 * devices))
     lines = -(-cap // 2) * 2 * SUB
 
-    slot, request = prep(bin_owner.reshape(1, count), bin_tile.reshape(1, count), devices, cap)
+    line, request = prep(bin_owner.reshape(1, count), bin_tile.reshape(1, count), devices, cap, lines)
     wanted = exchange(request)
     own, top, bottom, sides = tiles(direction)
     above, below = shift(bottom, "tx", 1), shift(top, "tx", -1)
@@ -368,7 +401,7 @@
     left, right = shift(sides[:beacons], "ty", 1), shift(sides[beacons:], "ty", -1)
     smooth = laplace(direction, above, below, left, right)
     fetched = exchange(gather(wanted, own, lines))
-    arrived = exchange(bins(slot, fetched, blocks, cap))
+    arrived = exchange(bins(line, fetched, blocks))
     image, stats = image_of(wanted, arrived, smooth, direction, residual)
     return update(exchange(stats), solution, residual, direction, image)
 

time: 91.8 us -> 89.2 us (0.972)
  Pallas kernels: 20.1 us -> 16.9 us
    pallas_call x2, Pallas kernels: 12.3 us -> 10.8 us  [the longest x1 9.18 us: bins(): pl.pallas_call(functools.partial(bins_kernel, group), in_specs=[whole(plt...]
  transfers between devices with their start and end apart: 6 -> 6, of which waited for: 4 -> 4; matrix products, arithmetic and copies ran while one was open for 0% -> 0% of each run, Pallas kernels for 2% -> 1%
where the time goes in v3:
time: 89.2 us; the launch traced here: 88.8 us
  blocking collectives  32.8 us (37%)
  starting transfers between devices  19.1 us (21%)
  waiting for transfers between devices  17.5 us (20%)
  Pallas kernels  16.9 us (19%)
  local copies, waits for them, and re-layouts  1.73 us (2%)
    all_to_all x2, blocking collectives, exchange(): return lax.all_to_all(x, AXES, split_axis=0, concat_axis=0, tiled=True)  32.8 us
    all_to_all x2, waiting for transfers between devices, exchange(): return lax.all_to_all(x, AXES, split_axis=0, concat_axis=0, tiled=True)  16.2 us
    all_to_all x2, starting transfers between devices, exchange(): return lax.all_to_all(x, AXES, split_axis=0, concat_axis=0, tiled=True)  9.95 us
    pallas_call x1, Pallas kernels, bins(): pl.pallas_call(functools.partial(bins_kernel, group), in_specs=[whole(plt...  9.18 us
    ppermute x4, starting transfers between devices, shift(): lax.ppermute(x, axis, [(i, i + step) for i in range(size) if 0 <= i + ste...  9.15 us
    pallas_call x1, Pallas kernels, image_of(): pl.pallas_call(image_kernel, in_specs=[whole(pltpu.SMEM)] + [whole()] * 4...  2.33 us
  transfers between devices with their start and end apart: 6, of which 4 were waited for; matrix products, arithmetic and copies ran while one was open for 0% of the time, Pallas kernels for 1%

profile of v3, /device:TPU:0, one launch (start us, length us, event | category | flops | bytes accessed | tf_op | source)
XLA Modules:
  0.0 88.8 jit_solution(7822808087543631987)
XLA Ops:
  0.6 1.6 %prep.1 = (s32[1,256]{1,0:T(1,128)}, s32[32,12]{1,0:T(8,128)}) custom-call(s32[1,256]{1,0:T(1,128)} %bitcast.15, s32[1,256]{1,0:T(1,128)} %bitcast.16), custom_call_target="tpu_custom_call" | custom-call | tf_op jit(solution)/shard_map/prep/pallas_call | solution.py:66
  2.2 7.3 %all-to-all-start = ((s32[32,1,12]{2,1,0:T(1,128)}), s32[32,1,12]{2,1,0:T(1,128)S(1)}, u32[]{:S(2)}, u32[]{:S(2)}) async-start(s32[32,1,12]{2,1,0:T(1,128)} %bitcast.14), calls=%async_computation | async-start | bytes 32768 | tf_op jit(solution)/shard_map/all_to_all | solution.py:382
  9.5 0.0 copy-start
  9.6 1.0 %copy-done = f32[4,128,256]{2,1,0:T(8,128)S(1)} copy-done((f32[4,128,256]{2,1,0:T(8,128)S(1)}, f32[4,128,256]{2,1,0:T(8,128)}, u32[]{:S(2)}) %copy-start) | copy-done | bytes 524312
  10.6 0.7 tiles.1
  11.3 5.3 %all-to-all-done = s32[32,1,12]{2,1,0:T(1,128)S(1)} async-done(((s32[32,1,12]{2,1,0:T(1,128)}), s32[32,1,12]{2,1,0:T(1,128)S(1)}, u32[]{:S(2)}, u32[]{:S(2)}) %all-to-all-start) | async-done | bytes 1568 | tf_op jit(solution)/shard_map/all_to_all | solution.py:382
  16.6 1.1 %gather.1 = bf16[32,96,128]{2,1,0:T(8,128)(2,1)S(1)} custom-call(s32[32,12]{1,0:T(8,128)S(1)} %bitcast.10, f32[1024,128]{1,0:T(8,128)S(1)} %get-tuple-element.13.tiles_ref), custom_call_target="tpu_custom_call" | custom-call | tf_op jit(solution)/shard_map/gather/pallas_call | solution.py:138
  17.7 23.7 %all_to_all.32.fetched_ref = bf16[32,96,128]{2,1,0:T(8,128)(2,1)S(1)} all-to-all(bf16[32,96,128]{2,1,0:T(8,128)(2,1)S(1)} %gather.1), channel_id=1, replica_groups=mesh['tx'=4,'ty'=8] {'tx','ty'}, dimensions={0} | all-to-all | bytes 1572864 | tf_op jit(solution)/shard_map/all_to_all | solution.py:382
  41.4 0.7 copy-done.4
  42.1 9.2 %bins.1 = bf16[32,96,128]{2,1,0:T(8,128)(2,1)} custom-call(s32[1,256]{1,0:T(1,128)S(1)} %copy-done.4, bf16[32,96,128]{2,1,0:T(8,128)(2,1)S(1)} %all_to_all.32.fetched_ref, bf16[256,128,256]{2,1,0:T(8,128)(2,1)} %blocks_ref.1), custom_call_target="tpu_custom_call" | custom-call | tf_op jit(solution)/shard_map/bins/pallas_call | solution.py:223
  51.3 2.6 %all-to-all-start.2 = ((bf16[32,96,128]{2,1,0:T(8,128)(2,1)}), bf16[32,96,128]{2,1,0:T(8,128)(2,1)S(1)}, u32[]{:S(2)}, u32[]{:S(2)}) async-start(bf16[32,96,128]{2,1,0:T(8,128)(2,1)} %bins.1), calls=%async_computation.2 | async-start | bytes 1572864 | tf_op jit(solution)/shard_map/all_to_all | solution.py:382
  54.0 2.0 %collective-permute-start = (bf16[4,256]{1,0:T(4,128)(2,1)S(1)}, bf16[4,256]{1,0:T(4,128)(2,1)S(1)}, u32[]{:S(2)}, u32[]{:S(2)}) collective-permute-start(bf16[4,256]{1,0:T(4,128)(2,1)S(1)} %get-tuple-element.14), channel_id=1, source_target_pairs={{0,8},{8,16},{16,24},{1,9},{9,17},{17,25},{2,10},{10,18},{18,26},{... | collective-permute-start | bytes 6152 | tf_op jit(solution)/shard_map/ppermute | solution.py:387
  56.0 1.3 %collective-permute-start.1 = (bf16[4,256]{1,0:T(4,128)(2,1)S(1)}, bf16[4,256]{1,0:T(4,128)(2,1)S(1)}, u32[]{:S(2)}, u32[]{:S(2)}) collective-permute-start(bf16[4,256]{1,0:T(4,128)(2,1)S(1)} %get-tuple-element.15), channel_id=1, source_target_pairs={{8,0},{16,8},{24,16},{9,1},{17,9},{25,17},{10,2},{18,10},{26,18},{... | collective-permute-start | bytes 6152 | tf_op jit(solution)/shard_map/ppermute | solution.py:387
  57.3 1.3 %collective-permute-start.3 = (bf16[4,128]{1,0:T(4,128)(2,1)S(1)}, bf16[4,128]{1,0:T(4,128)(2,1)S(1)}, u32[]{:S(2)}, u32[]{:S(2)}) collective-permute-start(bf16[4,128]{1,0:T(4,128)(2,1)S(1)} %get-tuple-element.19), channel_id=1, source_target_pairs={{1,0},{2,1},{3,2},{4,3},{5,4},{6,5},{7,6},{9,8},{10,9},{11,10},{12... | collective-permute-start | bytes 3080 | tf_op jit(solution)/shard_map/ppermute | solution.py:387
  58.6 4.5 %collective-permute-start.2 = (bf16[4,128]{1,0:T(4,128)(2,1)S(1)}, bf16[4,128]{1,0:T(4,128)(2,1)S(1)}, u32[]{:S(2)}, u32[]{:S(2)}) collective-permute-start(bf16[4,128]{1,0:T(4,128)(2,1)S(1)} %get-tuple-element.20), channel_id=1, source_target_pairs={{0,1},{1,2},{2,3},{3,4},{4,5},{5,6},{6,7},{8,9},{9,10},{10,11},{11... | collective-permute-start | bytes 3080 | tf_op jit(solution)/shard_map/ppermute | solution.py:387
  63.1 0.5 collective-permute-done.3.right_ref
  63.7 0.8 collective-permute-done.2.left_ref
  64.4 0.0 collective-permute-done.above_ref
  64.4 0.0 collective-permute-done.1.below_ref
  64.4 0.6 laplace.1.smooth_ref
  65.0 10.9 %all-to-all-done.2.arrived_ref = bf16[32,96,128]{2,1,0:T(8,128)(2,1)S(1)} async-done(((bf16[32,96,128]{2,1,0:T(8,128)(2,1)}), bf16[32,96,128]{2,1,0:T(8,128)(2,1)S(1)}, u32[]{:S(2)}, u32[]{:S(2)}) %all-to-all-start.2) | async-done | bytes 786464 | tf_op jit(solution)/shard_map/all_to_all | solution.py:382
  75.9 2.3 %image.1 = (f32[4,128,256]{2,1,0:T(8,128)S(1)}, f32[32,128]{1,0:T(8,128)S(1)}) custom-call(s32[32,12]{1,0:T(8,128)S(1)} %bitcast.11, bf16[32,96,128]{2,1,0:T(8,128)(2,1)S(1)} %all-to-all-done.2.arrived_ref, f32[4,128,256]{2,1,0:T(8,128)S(1)} %laplace.1.smooth_ref, f32[4,128,256]{2,1,0:T(8,128)S(1)} %copy-done.1, f32[4,128,256]{2,1,0:T(8,128)S(1)} %copy-done.2), custom_call_target="tpu_custom_call" | custom-call | tf_op jit(solution)/shard_map/image/pallas_call | solution.py:324
  78.3 9.1 %all_to_all.33 = f32[32,1,128]{2,1,0:T(1,128)S(1)} all-to-all(f32[32,1,128]{2,1,0:T(1,128)S(1)} %bitcast.13), channel_id=1, replica_groups=mesh['tx'=4,'ty'=8] {'tx','ty'}, dimensions={0} | all-to-all | bytes 32768 | tf_op jit(solution)/shard_map/all_to_all | solution.py:382
  87.4 1.4 %update.1 = (f32[4,128,256]{2,1,0:T(8,128)}, f32[4,128,256]{2,1,0:T(8,128)}, f32[4,128,256]{2,1,0:T(8,128)}) custom-call(f32[32,128]{1,0:T(8,128)S(1)} %bitcast.12, f32[4,128,256]{2,1,0:T(8,128)S(1)} %copy-done.3, f32[4,128,256]{2,1,0:T(8,128)S(1)} %copy-done.2, f32[4,128,256]{2,1,0:T(8,128)S(1)} %copy-done.1, f32[4,128,256]{2,1,0:T(8,128)S(1)} %get-tuple-element.18.image_ref), custom_call_target="tpu_custom_call" | custom-call | tf_op jit(solution)/shard_map/update/pallas_call | solution.py:369
  (8 shorter events, 0.0 us)
Async XLA Ops:
  2.2 14.4 %all-to-all-start = ((s32[32,1,12]{2,1,0:T(1,128)}), s32[32,1,12]{2,1,0:T(1,128)S(1)}, u32[]{:S(2)}, u32[]{:S(2)}) async-start(s32[32,1,12]{2,1,0:T(1,128)} %bitcast.14), calls=%async_computation | async-start | bytes 32768 | tf_op jit(solution)/shard_map/all_to_all | solution.py:382
  9.5 1.0 %copy-start = (f32[4,128,256]{2,1,0:T(8,128)S(1)}, f32[4,128,256]{2,1,0:T(8,128)}, u32[]{:S(2)}) copy-start(f32[4,128,256]{2,1,0:T(8,128)} %direction_ref.3) | copy-start | bytes 1572868
  10.6 53.8 %copy-start.1 = (f32[4,128,256]{2,1,0:T(8,128)S(1)}, f32[4,128,256]{2,1,0:T(8,128)}, u32[]{:S(2)}) copy-start(f32[4,128,256]{2,1,0:T(8,128)} %direction_ref.3) | copy-start | bytes 1572868
  10.6 65.3 %copy-start.2 = (f32[4,128,256]{2,1,0:T(8,128)S(1)}, f32[4,128,256]{2,1,0:T(8,128)}, u32[]{:S(2)}) copy-start(f32[4,128,256]{2,1,0:T(8,128)} %residual_ref.3) | copy-start | bytes 1572868
  10.6 76.8 %copy-start.3 = (f32[4,128,256]{2,1,0:T(8,128)S(1)}, f32[4,128,256]{2,1,0:T(8,128)}, u32[]{:S(2)}) copy-start(f32[4,128,256]{2,1,0:T(8,128)} %solution_ref.1) | copy-start | bytes 1572868
  41.4 0.7 copy-start.4
  51.3 24.6 %all-to-all-start.2 = ((bf16[32,96,128]{2,1,0:T(8,128)(2,1)}), bf16[32,96,128]{2,1,0:T(8,128)(2,1)S(1)}, u32[]{:S(2)}, u32[]{:S(2)}) async-start(bf16[32,96,128]{2,1,0:T(8,128)(2,1)} %bins.1), calls=%async_computation.2 | async-start | bytes 1572864 | tf_op jit(solution)/shard_map/all_to_all | solution.py:382
  54.0 10.5 %collective-permute-start = (bf16[4,256]{1,0:T(4,128)(2,1)S(1)}, bf16[4,256]{1,0:T(4,128)(2,1)S(1)}, u32[]{:S(2)}, u32[]{:S(2)}) collective-permute-start(bf16[4,256]{1,0:T(4,128)(2,1)S(1)} %get-tuple-element.14), channel_id=1, source_target_pairs={{0,8},{8,16},{16,24},{1,9},{9,17},{17,25},{2,10},{10,18},{18,26},{... | collective-permute-start | bytes 6152 | tf_op jit(solution)/shard_map/ppermute | solution.py:387
  56.0 8.5 %collective-permute-start.1 = (bf16[4,256]{1,0:T(4,128)(2,1)S(1)}, bf16[4,256]{1,0:T(4,128)(2,1)S(1)}, u32[]{:S(2)}, u32[]{:S(2)}) collective-permute-start(bf16[4,256]{1,0:T(4,128)(2,1)S(1)} %get-tuple-element.15), channel_id=1, source_target_pairs={{8,0},{16,8},{24,16},{9,1},{17,9},{25,17},{10,2},{18,10},{26,18},{... | collective-permute-start | bytes 6152 | tf_op jit(solution)/shard_map/ppermute | solution.py:387
  57.3 6.4 %collective-permute-start.3 = (bf16[4,128]{1,0:T(4,128)(2,1)S(1)}, bf16[4,128]{1,0:T(4,128)(2,1)S(1)}, u32[]{:S(2)}, u32[]{:S(2)}) collective-permute-start(bf16[4,128]{1,0:T(4,128)(2,1)S(1)} %get-tuple-element.19), channel_id=1, source_target_pairs={{1,0},{2,1},{3,2},{4,3},{5,4},{6,5},{7,6},{9,8},{10,9},{11,10},{12... | collective-permute-start | bytes 3080 | tf_op jit(solution)/shard_map/ppermute | solution.py:387
  58.6 5.8 %collective-permute-start.2 = (bf16[4,128]{1,0:T(4,128)(2,1)S(1)}, bf16[4,128]{1,0:T(4,128)(2,1)S(1)}, u32[]{:S(2)}, u32[]{:S(2)}) collective-permute-start(bf16[4,128]{1,0:T(4,128)(2,1)S(1)} %get-tuple-element.20), channel_id=1, source_target_pairs={{0,1},{1,2},{2,3},{3,4},{4,5},{5,6},{6,7},{8,9},{9,10},{10,11},{11... | collective-permute-start | bytes 3080 | tf_op jit(solution)/shard_map/ppermute | solution.py:387

commit v4 on v3

--- a/solution.py
+++ b/solution.py
@@ -23,58 +23,52 @@
     return pltpu.CompilerParams(vmem_limit_bytes=mib << 20)
 
 
-def swap_chunks(x):
+def swap_chunks(blocks):
     row = lax.broadcasted_iota(jnp.int32, (SUB, LANES), 0)
-    chunk = SUB - 1 - lax.broadcasted_iota(jnp.int32, (SUB, LANES), 1) // TILE_SIDE
-    x = pltpu.roll(x, 0, 2, stride=TILE_SIDE, stride_axis=1)
-    for s in (1, 2, 4):
-        x = jnp.where(((chunk & s) != 0)[None], pltpu.roll(x, s, 1), x)
-    x = pltpu.roll(x, TILE_SIDE, 2, stride=TILE_SIDE, stride_axis=1)
-    x = pltpu.roll(x, 4, 1)
-    for s in (1, 2):
-        x = jnp.where(((row & s) != 0)[None], pltpu.roll(x, s, 1), pltpu.roll(x, SUB - s, 1))
-    return x
-
-
-def prep_kernel(step, owner_hbm, tile_hbm, line_ref, request_ref, owner_ref, tile_ref, sems):
-    devices, bins = request_ref.shape[0], owner_ref.shape[1]
-    copies = [
-        pltpu.make_async_copy(a, b, sems.at[i])
-        for i, (a, b) in enumerate(((owner_hbm, owner_ref), (tile_hbm, tile_ref)))
-    ]
-    for copy in copies:
-        copy.start()
+    lane = lax.broadcasted_iota(jnp.int32, (SUB, LANES), 1)
+    chunk, rest = lane // TILE_SIDE, lane % TILE_SIDE
+    first = (chunk + row) % SUB * TILE_SIDE + rest
+    second = (row - chunk + SUB) % SUB * TILE_SIDE + rest
+
+    def swap(x):
+        x = jnp.take_along_axis(x, first, axis=1)
+        for s in (1, 2, 4):
+            x = jnp.where((chunk & s) != 0, pltpu.roll(x, s, 0), x)
+        return jnp.take_along_axis(x, second, axis=1)
+
+    return [swap(x) for x in blocks]
+
+
+def prep_kernel(step, both_ref, line_ref, request_ref):
+    devices, bins = request_ref.shape[0], both_ref.shape[1]
+    owner, tile = both_ref[:1], both_ref[1:]
     earlier = (
         lax.broadcasted_iota(jnp.int32, (bins, bins), 0) < lax.broadcasted_iota(jnp.int32, (bins, bins), 1)
     ).astype(jnp.bfloat16)
-    copies[0].wait()
-    owner = owner_ref[...]
     member = (lax.broadcasted_iota(jnp.int32, (devices, bins), 0) == owner).astype(jnp.float32)
     member16 = member.astype(jnp.bfloat16)
     before = jnp.dot(member16, earlier, preferred_element_type=jnp.float32)
     rank = jnp.sum(before * member, axis=0, keepdims=True).astype(jnp.int32)
     line_ref[...] = owner * step + rank * SUB
     place = lax.broadcasted_iota(jnp.int32, (request_ref.shape[1], bins), 0) == rank
-    copies[1].wait()
-    named = jnp.where(place, tile_ref[...], 0).astype(jnp.float32).astype(jnp.bfloat16)
+    named = jnp.where(place, tile, 0).astype(jnp.float32).astype(jnp.bfloat16)
     request = lax.dot_general(member16, named, (((1,), (1,)), ((), ())), preferred_element_type=jnp.float32)
     request_ref[...] = request.astype(jnp.int32) * SUB
 
 
-def prep(owner, tile, devices, cap, lines):
-    bins = owner.shape[1]
+def prep(both, devices, cap, lines):
+    bins = both.shape[1]
     return pl.pallas_call(
         functools.partial(prep_kernel, lines),
-        in_specs=[whole(pl.ANY)] * 2,
+        in_specs=[whole()],
         out_specs=[whole()] * 2,
         out_shape=[
             jax.ShapeDtypeStruct((1, bins), jnp.int32),
             jax.ShapeDtypeStruct((devices, cap), jnp.int32),
         ],
-        scratch_shapes=[pltpu.VMEM((1, bins), jnp.int32)] * 2 + [pltpu.SemaphoreType.DMA((2,))],
-        compiler_params=params(60),
+        compiler_params=params(4),
         name="prep",
-    )(owner, tile)
+    )(both)
 
 
 def tiles_kernel(field_ref, out_ref, top_ref, bottom_ref, sides_ref):
@@ -82,8 +76,8 @@
     bands, groups = rows // TILE_SIDE, cols // LANES
     for k in range(beacons):
         for g in range(groups):
-            x = field_ref[k, :, g * LANES : (g + 1) * LANES].reshape(bands * 2, SUB, LANES)
-            x = swap_chunks(x.astype(jnp.bfloat16).astype(jnp.float32))
+            x = field_ref[k, :, g * LANES : (g + 1) * LANES].astype(jnp.bfloat16).astype(jnp.float32)
+            x = swap_chunks([x[i * SUB : (i + 1) * SUB] for i in range(bands * 2)])
             for band in range(bands):
                 for h in range(2):
                     at = (band * groups + g) * SUB * SUB + h * beacons + k
@@ -287,7 +281,7 @@
                 for h in range(2):
                     at = pl.ds((band * groups + g) * SUB * SUB + h * beacons + k, SUB, stride=SUB)
                     x.append(sum(total[at, :] for total in sums))
-            x = swap_chunks(jnp.stack(x)).reshape(rows, LANES)
+            x = jnp.concatenate(swap_chunks(x), axis=0)
             x = x + smooth_ref[k, :, g * LANES : (g + 1) * LANES]
             image_ref[k, :, g * LANES : (g + 1) * LANES] = x
             unit = jnp.maximum(unit, jnp.max(jnp.abs(x).reshape(bands * 2, SUB, LANES), axis=0))
@@ -393,7 +387,8 @@
     cap = max(2, 3 * count // (2 * devices))
     lines = -(-cap // 2) * 2 * SUB
 
-    line, request = prep(bin_owner.reshape(1, count), bin_tile.reshape(1, count), devices, cap, lines)
+    both = jnp.concatenate([bin_owner.reshape(1, count), bin_tile.reshape(1, count)], axis=0)
+    line, request = prep(both, devices, cap, lines)
     wanted = exchange(request)
     own, top, bottom, sides = tiles(direction)
     above, below = shift(bottom, "tx", 1), shift(top, "tx", -1)

time: 89.2 us -> 88.3 us (0.990)
  Pallas kernels: 16.9 us -> 15.7 us
where the time goes in v4:
time: 88.3 us; the launch traced here: 87.9 us
  blocking collectives  32.8 us (37%)
  starting transfers between devices  19.1 us (22%)
  waiting for transfers between devices  17.8 us (20%)
  Pallas kernels  15.7 us (18%)
  local copies, waits for them, and re-layouts  1.05 us (1%)
    all_to_all x2, blocking collectives, exchange(): return lax.all_to_all(x, AXES, split_axis=0, concat_axis=0, tiled=True)  32.8 us
    all_to_all x2, waiting for transfers between devices, exchange(): return lax.all_to_all(x, AXES, split_axis=0, concat_axis=0, tiled=True)  16.5 us
    all_to_all x2, starting transfers between devices, exchange(): return lax.all_to_all(x, AXES, split_axis=0, concat_axis=0, tiled=True)  9.94 us
    ppermute x4, starting transfers between devices, shift(): lax.ppermute(x, axis, [(i, i + step) for i in range(size) if 0 <= i + ste...  9.15 us
    pallas_call x1, Pallas kernels, bins(): pl.pallas_call(functools.partial(bins_kernel, group), in_specs=[whole(plt...  9.08 us
    pallas_call x1, Pallas kernels, image_of(): pl.pallas_call(image_kernel, in_specs=[whole(pltpu.SMEM)] + [whole()] * 4...  2.22 us
  transfers between devices with their start and end apart: 6, of which 4 were waited for; matrix products, arithmetic and copies ran while one was open for 0% of the time, Pallas kernels for 1%

profile of v4, /device:TPU:0, one launch (start us, length us, event | category | flops | bytes accessed | tf_op | source)
XLA Modules:
  0.0 87.9 jit_solution(4466263793530131601)
XLA Ops:
  0.6 0.7 pad_add_fusion.both_ref
  1.3 0.9 %prep.1 = (s32[1,256]{1,0:T(1,128)S(1)}, s32[32,12]{1,0:T(8,128)}) custom-call(s32[2,256]{1,0:T(2,128)S(1)} %pad_add_fusion.both_ref), custom_call_target="tpu_custom_call" | custom-call | tf_op jit(solution)/shard_map/prep/pallas_call | solution.py:61
  2.2 7.3 %all-to-all-start = ((s32[32,1,12]{2,1,0:T(1,128)}), s32[32,1,12]{2,1,0:T(1,128)S(1)}, u32[]{:S(2)}, u32[]{:S(2)}) async-start(s32[32,1,12]{2,1,0:T(1,128)} %bitcast.3), calls=%async_computation | async-start | bytes 32768 | tf_op jit(solution)/shard_map/all_to_all | solution.py:376
  9.5 0.0 copy-start
  9.6 1.0 %copy-done = f32[4,128,256]{2,1,0:T(8,128)S(1)} copy-done((f32[4,128,256]{2,1,0:T(8,128)S(1)}, f32[4,128,256]{2,1,0:T(8,128)}, u32[]{:S(2)}) %copy-start) | copy-done | bytes 524312
  10.6 0.4 tiles.1
  11.0 5.6 %all-to-all-done = s32[32,1,12]{2,1,0:T(1,128)S(1)} async-done(((s32[32,1,12]{2,1,0:T(1,128)}), s32[32,1,12]{2,1,0:T(1,128)S(1)}, u32[]{:S(2)}, u32[]{:S(2)}) %all-to-all-start) | async-done | bytes 1568 | tf_op jit(solution)/shard_map/all_to_all | solution.py:376
  16.6 1.1 %gather.1 = bf16[32,96,128]{2,1,0:T(8,128)(2,1)S(1)} custom-call(s32[32,12]{1,0:T(8,128)S(1)} %bitcast.10, f32[1024,128]{1,0:T(8,128)S(1)} %get-tuple-element.13.tiles_ref), custom_call_target="tpu_custom_call" | custom-call | tf_op jit(solution)/shard_map/gather/pallas_call | solution.py:132
  17.7 23.7 %all_to_all.32.fetched_ref = bf16[32,96,128]{2,1,0:T(8,128)(2,1)S(1)} all-to-all(bf16[32,96,128]{2,1,0:T(8,128)(2,1)S(1)} %gather.1), channel_id=1, replica_groups=mesh['tx'=4,'ty'=8] {'tx','ty'}, dimensions={0} | all-to-all | bytes 1572864 | tf_op jit(solution)/shard_map/all_to_all | solution.py:376
  41.4 9.1 %bins.1 = bf16[32,96,128]{2,1,0:T(8,128)(2,1)} custom-call(s32[1,256]{1,0:T(1,128)S(1)} %get-tuple-element.12.line_ref, bf16[32,96,128]{2,1,0:T(8,128)(2,1)S(1)} %all_to_all.32.fetched_ref, bf16[256,128,256]{2,1,0:T(8,128)(2,1)} %blocks_ref.1), custom_call_target="tpu_custom_call" | custom-call | tf_op jit(solution)/shard_map/bins/pallas_call | solution.py:217
  50.5 2.6 %all-to-all-start.2 = ((bf16[32,96,128]{2,1,0:T(8,128)(2,1)}), bf16[32,96,128]{2,1,0:T(8,128)(2,1)S(1)}, u32[]{:S(2)}, u32[]{:S(2)}) async-start(bf16[32,96,128]{2,1,0:T(8,128)(2,1)} %bins.1), calls=%async_computation.2 | async-start | bytes 1572864 | tf_op jit(solution)/shard_map/all_to_all | solution.py:376
  53.2 2.0 %collective-permute-start = (bf16[4,256]{1,0:T(4,128)(2,1)S(1)}, bf16[4,256]{1,0:T(4,128)(2,1)S(1)}, u32[]{:S(2)}, u32[]{:S(2)}) collective-permute-start(bf16[4,256]{1,0:T(4,128)(2,1)S(1)} %get-tuple-element.14), channel_id=1, source_target_pairs={{0,8},{8,16},{16,24},{1,9},{9,17},{17,25},{2,10},{10,18},{18,26},{... | collective-permute-start | bytes 6152 | tf_op jit(solution)/shard_map/ppermute | solution.py:381
  55.2 1.3 %collective-permute-start.1 = (bf16[4,256]{1,0:T(4,128)(2,1)S(1)}, bf16[4,256]{1,0:T(4,128)(2,1)S(1)}, u32[]{:S(2)}, u32[]{:S(2)}) collective-permute-start(bf16[4,256]{1,0:T(4,128)(2,1)S(1)} %get-tuple-element.15), channel_id=1, source_target_pairs={{8,0},{16,8},{24,16},{9,1},{17,9},{25,17},{10,2},{18,10},{26,18},{... | collective-permute-start | bytes 6152 | tf_op jit(solution)/shard_map/ppermute | solution.py:381
  56.5 1.3 %collective-permute-start.3 = (bf16[4,128]{1,0:T(4,128)(2,1)S(1)}, bf16[4,128]{1,0:T(4,128)(2,1)S(1)}, u32[]{:S(2)}, u32[]{:S(2)}) collective-permute-start(bf16[4,128]{1,0:T(4,128)(2,1)S(1)} %get-tuple-element.19), channel_id=1, source_target_pairs={{1,0},{2,1},{3,2},{4,3},{5,4},{6,5},{7,6},{9,8},{10,9},{11,10},{12... | collective-permute-start | bytes 3080 | tf_op jit(solution)/shard_map/ppermute | solution.py:381
  57.8 4.5 %collective-permute-start.2 = (bf16[4,128]{1,0:T(4,128)(2,1)S(1)}, bf16[4,128]{1,0:T(4,128)(2,1)S(1)}, u32[]{:S(2)}, u32[]{:S(2)}) collective-permute-start(bf16[4,128]{1,0:T(4,128)(2,1)S(1)} %get-tuple-element.20), channel_id=1, source_target_pairs={{0,1},{1,2},{2,3},{3,4},{4,5},{5,6},{6,7},{8,9},{9,10},{10,11},{11... | collective-permute-start | bytes 3080 | tf_op jit(solution)/shard_map/ppermute | solution.py:381
  62.4 0.5 collective-permute-done.3.right_ref
  62.9 0.8 collective-permute-done.2.left_ref
  63.6 0.0 collective-permute-done.above_ref
  63.7 0.0 collective-permute-done.1.below_ref
  63.7 0.6 laplace.1.smooth_ref
  64.2 10.9 %all-to-all-done.2.arrived_ref = bf16[32,96,128]{2,1,0:T(8,128)(2,1)S(1)} async-done(((bf16[32,96,128]{2,1,0:T(8,128)(2,1)}), bf16[32,96,128]{2,1,0:T(8,128)(2,1)S(1)}, u32[]{:S(2)}, u32[]{:S(2)}) %all-to-all-start.2) | async-done | bytes 786464 | tf_op jit(solution)/shard_map/all_to_all | solution.py:376
  75.1 2.2 %image.1 = (f32[4,128,256]{2,1,0:T(8,128)S(1)}, f32[32,128]{1,0:T(8,128)S(1)}) custom-call(s32[32,12]{1,0:T(8,128)S(1)} %bitcast.11, bf16[32,96,128]{2,1,0:T(8,128)(2,1)S(1)} %all-to-all-done.2.arrived_ref, f32[4,128,256]{2,1,0:T(8,128)S(1)} %laplace.1.smooth_ref, f32[4,128,256]{2,1,0:T(8,128)S(1)} %copy-done.1, f32[4,128,256]{2,1,0:T(8,128)S(1)} %copy-done.2), custom_call_target="tpu_custom_call" | custom-call | tf_op jit(solution)/shard_map/image/pallas_call | solution.py:318
  77.4 9.1 %all_to_all.33 = f32[32,1,128]{2,1,0:T(1,128)S(1)} all-to-all(f32[32,1,128]{2,1,0:T(1,128)S(1)} %bitcast.13), channel_id=1, replica_groups=mesh['tx'=4,'ty'=8] {'tx','ty'}, dimensions={0} | all-to-all | bytes 32768 | tf_op jit(solution)/shard_map/all_to_all | solution.py:376
  86.5 1.4 %update.1 = (f32[4,128,256]{2,1,0:T(8,128)}, f32[4,128,256]{2,1,0:T(8,128)}, f32[4,128,256]{2,1,0:T(8,128)}) custom-call(f32[32,128]{1,0:T(8,128)S(1)} %bitcast.12, f32[4,128,256]{2,1,0:T(8,128)S(1)} %copy-done.3, f32[4,128,256]{2,1,0:T(8,128)S(1)} %copy-done.2, f32[4,128,256]{2,1,0:T(8,128)S(1)} %copy-done.1, f32[4,128,256]{2,1,0:T(8,128)S(1)} %get-tuple-element.18.image_ref), custom_call_target="tpu_custom_call" | custom-call | tf_op jit(solution)/shard_map/update/pallas_call | solution.py:363
  (7 shorter events, 0.0 us)
Async XLA Ops:
  2.2 14.3 %all-to-all-start = ((s32[32,1,12]{2,1,0:T(1,128)}), s32[32,1,12]{2,1,0:T(1,128)S(1)}, u32[]{:S(2)}, u32[]{:S(2)}) async-start(s32[32,1,12]{2,1,0:T(1,128)} %bitcast.3), calls=%async_computation | async-start | bytes 32768 | tf_op jit(solution)/shard_map/all_to_all | solution.py:376
  9.5 1.0 %copy-start = (f32[4,128,256]{2,1,0:T(8,128)S(1)}, f32[4,128,256]{2,1,0:T(8,128)}, u32[]{:S(2)}) copy-start(f32[4,128,256]{2,1,0:T(8,128)} %direction_ref.3) | copy-start | bytes 1572868
  10.6 53.1 %copy-start.1 = (f32[4,128,256]{2,1,0:T(8,128)S(1)}, f32[4,128,256]{2,1,0:T(8,128)}, u32[]{:S(2)}) copy-start(f32[4,128,256]{2,1,0:T(8,128)} %direction_ref.3) | copy-start | bytes 1572868
  10.6 64.6 %copy-start.2 = (f32[4,128,256]{2,1,0:T(8,128)S(1)}, f32[4,128,256]{2,1,0:T(8,128)}, u32[]{:S(2)}) copy-start(f32[4,128,256]{2,1,0:T(8,128)} %residual_ref.3) | copy-start | bytes 1572868
  10.6 75.9 %copy-start.3 = (f32[4,128,256]{2,1,0:T(8,128)S(1)}, f32[4,128,256]{2,1,0:T(8,128)}, u32[]{:S(2)}) copy-start(f32[4,128,256]{2,1,0:T(8,128)} %solution_ref.1) | copy-start | bytes 1572868
  50.5 24.6 %all-to-all-start.2 = ((bf16[32,96,128]{2,1,0:T(8,128)(2,1)}), bf16[32,96,128]{2,1,0:T(8,128)(2,1)S(1)}, u32[]{:S(2)}, u32[]{:S(2)}) async-start(bf16[32,96,128]{2,1,0:T(8,128)(2,1)} %bins.1), calls=%async_computation.2 | async-start | bytes 1572864 | tf_op jit(solution)/shard_map/all_to_all | solution.py:376
  53.2 10.5 %collective-permute-start = (bf16[4,256]{1,0:T(4,128)(2,1)S(1)}, bf16[4,256]{1,0:T(4,128)(2,1)S(1)}, u32[]{:S(2)}, u32[]{:S(2)}) collective-permute-start(bf16[4,256]{1,0:T(4,128)(2,1)S(1)} %get-tuple-element.14), channel_id=1, source_target_pairs={{0,8},{8,16},{16,24},{1,9},{9,17},{17,25},{2,10},{10,18},{18,26},{... | collective-permute-start | bytes 6152 | tf_op jit(solution)/shard_map/ppermute | solution.py:381
  55.2 8.5 %collective-permute-start.1 = (bf16[4,256]{1,0:T(4,128)(2,1)S(1)}, bf16[4,256]{1,0:T(4,128)(2,1)S(1)}, u32[]{:S(2)}, u32[]{:S(2)}) collective-permute-start(bf16[4,256]{1,0:T(4,128)(2,1)S(1)} %get-tuple-element.15), channel_id=1, source_target_pairs={{8,0},{16,8},{24,16},{9,1},{17,9},{25,17},{10,2},{18,10},{26,18},{... | collective-permute-start | bytes 6152 | tf_op jit(solution)/shard_map/ppermute | solution.py:381
  56.5 6.4 %collective-permute-start.3 = (bf16[4,128]{1,0:T(4,128)(2,1)S(1)}, bf16[4,128]{1,0:T(4,128)(2,1)S(1)}, u32[]{:S(2)}, u32[]{:S(2)}) collective-permute-start(bf16[4,128]{1,0:T(4,128)(2,1)S(1)} %get-tuple-element.19), channel_id=1, source_target_pairs={{1,0},{2,1},{3,2},{4,3},{5,4},{6,5},{7,6},{9,8},{10,9},{11,10},{12... | collective-permute-start | bytes 3080 | tf_op jit(solution)/shard_map/ppermute | solution.py:381
  57.8 5.8 %collective-permute-start.2 = (bf16[4,128]{1,0:T(4,128)(2,1)S(1)}, bf16[4,128]{1,0:T(4,128)(2,1)S(1)}, u32[]{:S(2)}, u32[]{:S(2)}) collective-permute-start(bf16[4,128]{1,0:T(4,128)(2,1)S(1)} %get-tuple-element.20), channel_id=1, source_target_pairs={{0,1},{1,2},{2,3},{3,4},{4,5},{5,6},{6,7},{8,9},{9,10},{10,11},{11... | collective-permute-start | bytes 3080 | tf_op jit(solution)/shard_map/ppermute | solution.py:381

commit v5 on v4

--- a/solution.py
+++ b/solution.py
@@ -12,7 +12,9 @@
 SUB = 8
 smooth_weight = 0.25
 
-AXES = ("tx", "ty")
+TY = ("th", "tl")
+AXES = ("tx", "th", "tl")
+HALF = ("tx", "tl")
 
 
 def whole(memory=pltpu.VMEM):
@@ -39,31 +41,35 @@
     return [swap(x) for x in blocks]
 
 
-def prep_kernel(step, both_ref, line_ref, request_ref):
+def prep_kernel(step, span, tiles, both_ref, line_ref, request_ref):
     devices, bins = request_ref.shape[0], both_ref.shape[1]
     owner, tile = both_ref[:1], both_ref[1:]
+    column = lax.rem(owner, 2 * span)
+    far = (lax.div(column, span) != lax.axis_index("th")).astype(jnp.int32)
+    place = (lax.div(owner, 2 * span) * span + lax.rem(column, span)) * 2 + far
     earlier = (
         lax.broadcasted_iota(jnp.int32, (bins, bins), 0) < lax.broadcasted_iota(jnp.int32, (bins, bins), 1)
     ).astype(jnp.bfloat16)
-    member = (lax.broadcasted_iota(jnp.int32, (devices, bins), 0) == owner).astype(jnp.float32)
+    member = (lax.broadcasted_iota(jnp.int32, (devices, bins), 0) == place).astype(jnp.float32)
     member16 = member.astype(jnp.bfloat16)
     before = jnp.dot(member16, earlier, preferred_element_type=jnp.float32)
     rank = jnp.sum(before * member, axis=0, keepdims=True).astype(jnp.int32)
-    line_ref[...] = owner * step + rank * SUB
-    place = lax.broadcasted_iota(jnp.int32, (request_ref.shape[1], bins), 0) == rank
-    named = jnp.where(place, tile, 0).astype(jnp.float32).astype(jnp.bfloat16)
+    line_ref[:1] = place * step + rank * SUB
+    line_ref[1:] = owner * step + rank * SUB
+    at = lax.broadcasted_iota(jnp.int32, (request_ref.shape[1], bins), 0) == rank
+    named = jnp.where(at, tile + far * tiles, 0).astype(jnp.float32).astype(jnp.bfloat16)
     request = lax.dot_general(member16, named, (((1,), (1,)), ((), ())), preferred_element_type=jnp.float32)
     request_ref[...] = request.astype(jnp.int32) * SUB
 
 
-def prep(both, devices, cap, lines):
+def prep(both, devices, cap, lines, span, tiles):
     bins = both.shape[1]
     return pl.pallas_call(
-        functools.partial(prep_kernel, lines),
+        functools.partial(prep_kernel, lines, span, tiles),
         in_specs=[whole()],
         out_specs=[whole()] * 2,
         out_shape=[
-            jax.ShapeDtypeStruct((1, bins), jnp.int32),
+            jax.ShapeDtypeStruct((2, bins), jnp.int32),
             jax.ShapeDtypeStruct((devices, cap), jnp.int32),
         ],
         compiler_params=params(4),
@@ -71,17 +77,18 @@
     )(both)
 
 
-def tiles_kernel(field_ref, out_ref, top_ref, bottom_ref, sides_ref):
+def tiles_kernel(field_ref, out_ref, top_ref, bottom_ref, sides_ref, held):
     beacons, rows, cols = field_ref.shape
     bands, groups = rows // TILE_SIDE, cols // LANES
     for k in range(beacons):
         for g in range(groups):
-            x = field_ref[k, :, g * LANES : (g + 1) * LANES].astype(jnp.bfloat16).astype(jnp.float32)
+            x = field_ref[k, :, g * LANES : (g + 1) * LANES]
             x = swap_chunks([x[i * SUB : (i + 1) * SUB] for i in range(bands * 2)])
             for band in range(bands):
                 for h in range(2):
                     at = (band * groups + g) * SUB * SUB + h * beacons + k
-                    out_ref[pl.ds(at, SUB, stride=SUB), :] = x[band * 2 + h]
+                    held[pl.ds(at, SUB, stride=SUB), :] = x[band * 2 + h]
+    out_ref[...] = held[...].astype(jnp.bfloat16)
     top_ref[...] = field_ref[:, 0, :].astype(jnp.bfloat16)
     bottom_ref[...] = field_ref[:, rows - 1, :].astype(jnp.bfloat16)
     lane = lax.broadcasted_iota(jnp.int32, (rows, LANES), 1)
@@ -99,44 +106,50 @@
         in_specs=[whole()],
         out_specs=[whole()] * 4,
         out_shape=[
-            jax.ShapeDtypeStruct((beacons * rows * cols // LANES, LANES), jnp.float32),
+            jax.ShapeDtypeStruct((beacons * rows * cols // LANES, LANES), jnp.bfloat16),
             jax.ShapeDtypeStruct((beacons, cols), jnp.bfloat16),
             jax.ShapeDtypeStruct((beacons, cols), jnp.bfloat16),
             jax.ShapeDtypeStruct((2 * beacons, rows), jnp.bfloat16),
         ],
+        scratch_shapes=[pltpu.VMEM((beacons * rows * cols // LANES, LANES), jnp.float32)],
         compiler_params=params(8),
         name="tiles",
     )(field)
 
 
-def gather_kernel(wanted_ref, tiles_ref, out_ref):
-    devices, cap = wanted_ref.shape
+def gather_kernel(cap, wanted_ref, own_ref, other_ref, *rest):
+    *after, out_ref, held = rest
+    peers, lines = wanted_ref.shape[0], out_ref.shape[1] // 2
+    rows = own_ref.shape[0]
+    held[:rows] = own_ref[...].astype(jnp.float32)
+    held[rows:] = other_ref[...].astype(jnp.float32)
 
     def at(d, r):
-        return tiles_ref[pl.ds(pl.multiple_of(wanted_ref[d, r], SUB), SUB), :]
+        return held[pl.ds(pl.multiple_of(wanted_ref[d, r], SUB), SUB), :]
 
     def body(d, carry):
-        for r in range(0, cap - 1, 2):
-            pair = jnp.concatenate([at(d, r), at(d, r + 1)], axis=0)
-            out_ref[d, r * SUB : (r + 2) * SUB, :] = pair.astype(jnp.bfloat16)
-        if cap % 2:
-            pair = jnp.concatenate([at(d, cap - 1), jnp.zeros((SUB, LANES), jnp.float32)], axis=0)
-            out_ref[d, (cap - 1) * SUB : (cap + 1) * SUB, :] = pair.astype(jnp.bfloat16)
+        for block in range(2):
+            for r in range(0, cap, 2):
+                to = block * lines + r * SUB
+                one = at(d, block * cap + r)
+                two = at(d, block * cap + r + 1) if r + 1 < cap else jnp.zeros_like(one)
+                out_ref[d, to : to + 2 * SUB, :] = jnp.concatenate([one, two], axis=0).astype(jnp.bfloat16)
         return carry
 
-    lax.fori_loop(0, devices, body, 0, unroll=4)
-
-
-def gather(wanted, own, lines):
-    devices = wanted.shape[0]
-    return pl.pallas_call(
-        gather_kernel,
-        in_specs=[whole(pltpu.SMEM), whole()],
+    lax.fori_loop(0, peers, body, 0, unroll=2)
+
+
+def gather(wanted, own, other, lines, *after):
+    peers = wanted.shape[0]
+    return pl.pallas_call(
+        functools.partial(gather_kernel, wanted.shape[1] // 2),
+        in_specs=[whole(pltpu.SMEM), whole(), whole()] + [whole(pl.ANY)] * len(after),
         out_specs=whole(),
-        out_shape=jax.ShapeDtypeStruct((devices, lines, LANES), jnp.bfloat16),
+        out_shape=jax.ShapeDtypeStruct((peers, 2 * lines, LANES), jnp.bfloat16),
+        scratch_shapes=[pltpu.VMEM((2 * own.shape[0], LANES), jnp.float32)],
         compiler_params=params(8),
         name="gather",
-    )(wanted, own)
+    )(wanted, own, other, *after)
 
 
 def bins_kernel(
@@ -165,13 +178,13 @@
         for p in range(pairs):
             to[p] = weights(g, p).T
 
-    def line(b):
-        return pl.ds(pl.multiple_of(line_ref[0, b], SUB), SUB)
+    def line(b, back):
+        return pl.ds(pl.multiple_of(line_ref[back, b], SUB), SUB)
 
     def sample(g, turned, to):
         for p in range(pairs):
-            f0 = pick[line(g * group + 2 * p), :]
-            f1 = pick[line(g * group + 2 * p + 1), :]
+            f0 = pick[line(g * group + 2 * p, 0), :]
+            f1 = pick[line(g * group + 2 * p + 1, 0), :]
             left = jnp.where(low, f0, pltpu.roll(f1, 4, 0))
             right = jnp.where(low, pltpu.roll(f0, 4, 0), f1)
             x = jnp.concatenate([left, right], axis=1).astype(jnp.bfloat16)
@@ -182,8 +195,8 @@
         for p in range(pairs):
             a = jnp.dot(sampled[p].astype(jnp.bfloat16), weights(g, p), preferred_element_type=jnp.float32)
             left, right = a[:, :LANES], a[:, LANES:]
-            ret[line(g * group + 2 * p), :] = jnp.where(low, left, pltpu.roll(right, 4, 0))
-            ret[line(g * group + 2 * p + 1), :] = jnp.where(low, pltpu.roll(left, 4, 0), right)
+            ret[line(g * group + 2 * p, 1), :] = jnp.where(low, left, pltpu.roll(right, 4, 0))
+            ret[line(g * group + 2 * p + 1, 1), :] = jnp.where(low, pltpu.roll(left, 4, 0), right)
 
     fetch(0).wait()
     turn(0, turn_a)
@@ -255,22 +268,30 @@
     )(field, above, below, left, right)
 
 
-def image_kernel(wanted_ref, arrived_ref, smooth_ref, direction_ref, residual_ref, image_ref, stats_ref, *sums):
-    devices, cap = wanted_ref.shape
+def image_kernel(near_ref, far_ref, arrived_ref, smooth_ref, direction_ref, residual_ref, image_ref, stats_ref, *sums):
+    peers, cap = near_ref.shape[0], near_ref.shape[1] // 2
     beacons, rows, cols = direction_ref.shape
     bands, groups = rows // TILE_SIDE, cols // LANES
+    span = lax.axis_size("tl")
+    half = lax.axis_index("th")
     for total in sums:
         total[...] = jnp.zeros_like(total)
 
-    def body(d, carry):
-        for r in range(0, cap, 2):
-            pair = arrived_ref[d, r * SUB : (r + 2) * SUB, :].astype(jnp.float32)
-            for q in range(min(2, cap - r)):
-                at = pl.ds(pl.multiple_of(wanted_ref[d, r + q], SUB), SUB)
-                sums[(r + q) % len(sums)][at, :] += pair[q * SUB : (q + 1) * SUB]
+    def body(q, carry):
+        row, place = lax.div(q, span) * (2 * span), lax.rem(q, span)
+        for away in range(2):
+            d = row + (1 - half if away else half) * span + place
+            for r in range(0, cap, 2):
+                pair = arrived_ref[d, r * SUB : (r + 2) * SUB, :].astype(jnp.float32)
+                for e in range(min(2, cap - r)):
+                    first = far_ref[q, cap + r + e] - sums[0].shape[0] if away else near_ref[q, r + e]
+                    if away:
+                        first = jnp.maximum(first, 0)
+                    at = pl.ds(pl.multiple_of(first, SUB), SUB)
+                    sums[(r + e) % len(sums)][at, :] += pair[e * SUB : (e + 1) * SUB]
         return carry
 
-    lax.fori_loop(0, devices, body, 0, unroll=2)
+    lax.fori_loop(0, peers, body, 0)
     lines = []
     units = []
     for k in range(beacons):
@@ -313,20 +334,20 @@
     stats_ref[...] = jnp.broadcast_to(stats, stats_ref.shape)
 
 
-def image_of(wanted, arrived, smooth, direction, residual):
+def image_of(near, far, arrived, smooth, direction, residual):
     beacons, rows, cols = direction.shape
     return pl.pallas_call(
         image_kernel,
-        in_specs=[whole(pltpu.SMEM)] + [whole()] * 4,
+        in_specs=[whole(pltpu.SMEM)] * 2 + [whole()] * 4,
         out_specs=[whole(), whole()],
         out_shape=[
             jax.ShapeDtypeStruct(direction.shape, jnp.float32),
-            jax.ShapeDtypeStruct((wanted.shape[0], LANES), jnp.float32),
+            jax.ShapeDtypeStruct((arrived.shape[0], LANES), jnp.float32),
         ],
         scratch_shapes=[pltpu.VMEM((beacons * rows * cols // LANES, LANES), jnp.float32)] * 4,
         compiler_params=params(16),
         name="image",
-    )(wanted, arrived, smooth, direction, residual)
+    )(near, far, arrived, smooth, direction, residual)
 
 
 def update_kernel(
@@ -372,8 +393,8 @@
     )(stats, solution, residual, direction, image)
 
 
-def exchange(x):
-    return lax.all_to_all(x, AXES, split_axis=0, concat_axis=0, tiled=True)
+def exchange(x, axes):
+    return lax.all_to_all(x, axes, split_axis=0, concat_axis=0, tiled=True)
 
 
 def shift(x, axis, step):
@@ -381,39 +402,40 @@
     return lax.ppermute(x, axis, [(i, i + step) for i in range(size) if 0 <= i + step < size])
 
 
+def trade(x):
+    return lax.ppermute(x, "th", [(0, 1), (1, 0)])
+
+
 def per_device(solution, residual, direction, blocks, bin_owner, bin_tile):
-    devices = lax.axis_size("tx") * lax.axis_size("ty")
+    devices, span = lax.axis_size(AXES), lax.axis_size("tl")
     count = blocks.shape[0]
     cap = max(2, 3 * count // (2 * devices))
     lines = -(-cap // 2) * 2 * SUB
-
+    beacons, rows, cols = direction.shape
+
+    own, top, bottom, sides = tiles(direction)
+    other = trade(own)
     both = jnp.concatenate([bin_owner.reshape(1, count), bin_tile.reshape(1, count)], axis=0)
-    line, request = prep(both, devices, cap, lines)
-    wanted = exchange(request)
-    own, top, bottom, sides = tiles(direction)
+    line, request = prep(both, devices, cap, lines, span, rows * cols // TILE_SIDE**2)
+    near = exchange(request.reshape(devices // 2, 2 * cap), HALF)
+    far = trade(near)
     above, below = shift(bottom, "tx", 1), shift(top, "tx", -1)
-    beacons = direction.shape[0]
-    left, right = shift(sides[:beacons], "ty", 1), shift(sides[beacons:], "ty", -1)
+    left, right = shift(sides[:beacons], TY, 1), shift(sides[beacons:], TY, -1)
     smooth = laplace(direction, above, below, left, right)
-    fetched = exchange(gather(wanted, own, lines))
-    arrived = exchange(bins(line, fetched, blocks))
-    image, stats = image_of(wanted, arrived, smooth, direction, residual)
-    return update(exchange(stats), solution, residual, direction, image)
+    fetched = exchange(gather(near, own, other, lines, far), HALF).reshape(devices, lines, LANES)
+    arrived = exchange(bins(line, fetched, blocks), AXES)
+    image, stats = image_of(near, far, arrived, smooth, direction, residual)
+    return update(exchange(stats, AXES), solution, residual, direction, image)
 
 
 def solution(mesh):
-    placed = (
-        P(None, "tx", "ty"),
-        P(None, "tx", "ty"),
-        P(None, "tx", "ty"),
-        P(AXES, None, None),
-        P(AXES, None),
-        P(AXES),
-    )
+    rows, cols = mesh.devices.shape
+    halves = jax.sharding.Mesh(mesh.devices.reshape(rows, 2, cols // 2), AXES)
+    field = P(None, "tx", TY)
     return jax.shard_map(
         per_device,
-        mesh=mesh,
-        in_specs=placed,
-        out_specs=(P(None, "tx", "ty"),) * 3,
+        mesh=halves,
+        in_specs=(field, field, field, P(AXES, None, None), P(AXES, None), P(AXES)),
+        out_specs=(field,) * 3,
         check_vma=False,
     )

time: 88.3 us -> 85.6 us (0.969)
  starting transfers between devices: 19.1 us -> 16 us
  blocking collectives: 32.8 us -> 34.8 us
  waiting for transfers between devices: 17.8 us -> 16.6 us
    all_to_all x2 -> x1, starting transfers between devices: 9.94 us -> 2.64 us  [exchange(): return lax.all_to_all(x, axes, split_axis=0, concat_axis=0, tiled=True)]
    all_to_all x2 -> x1, waiting for transfers between devices: 16.5 us -> 10.9 us  [exchange(): return lax.all_to_all(x, axes, split_axis=0, concat_axis=0, tiled=True)]
    ppermute x0 -> x2, waiting for transfers between devices: none -> 4.41 us  [trade(): return lax.ppermute(x, 'th', [(0, 1), (1, 0)])]
    ppermute x0 -> x2, starting transfers between devices: none -> 4.21 us  [trade(): return lax.ppermute(x, 'th', [(0, 1), (1, 0)])]
    all_to_all x2 -> x3, blocking collectives: 32.8 us -> 34.8 us  [exchange(): return lax.all_to_all(x, axes, split_axis=0, concat_axis=0, tiled=True)]
  transfers between devices with their start and end apart: 6 -> 7, of which waited for: 4 -> 4; matrix products, arithmetic and copies ran while one was open for 0% -> 1% of each run, Pallas kernels for 1% -> 1%
where the time goes in v5:
time: 85.6 us; the launch traced here: 85.2 us
  blocking collectives  34.8 us (41%)
  waiting for transfers between devices  16.6 us (19%)
  starting transfers between devices  16 us (19%)
  Pallas kernels  15.3 us (18%)
  local copies, waits for them, and re-layouts  1.13 us (1%)
    all_to_all x3, blocking collectives, exchange(): return lax.all_to_all(x, axes, split_axis=0, concat_axis=0, tiled=True)  34.8 us
    all_to_all x1, waiting for transfers between devices, exchange(): return lax.all_to_all(x, axes, split_axis=0, concat_axis=0, tiled=True)  10.9 us
    ppermute x4, starting transfers between devices, shift(): lax.ppermute(x, axis, [(i, i + step) for i in range(size) if 0 <= i + ste...  9.15 us
    pallas_call x1, Pallas kernels, bins(): pl.pallas_call(functools.partial(bins_kernel, group), in_specs=[whole(plt...  9.1 us
    ppermute x2, waiting for transfers between devices, trade(): return lax.ppermute(x, 'th', [(0, 1), (1, 0)])  4.41 us
    ppermute x2, starting transfers between devices, trade(): return lax.ppermute(x, 'th', [(0, 1), (1, 0)])  4.21 us
    all_to_all x1, starting transfers between devices, exchange(): return lax.all_to_all(x, axes, split_axis=0, concat_axis=0, tiled=True)  2.64 us
    pallas_call x1, Pallas kernels, image_of(): pl.pallas_call(image_kernel, in_specs=[whole(pltpu.SMEM)] * 2 + [whole()]...  2.29 us
  transfers between devices with their start and end apart: 7, of which 4 were waited for; matrix products, arithmetic and copies ran while one was open for 1% of the time, Pallas kernels for 1%

profile of v5, /device:TPU:0, one launch (start us, length us, event | category | flops | bytes accessed | tf_op | source)
XLA Modules:
  0.0 85.2 jit_solution(8837485671232956169)
XLA Ops:
  0.6 1.0 %copy-done = f32[4,128,256]{2,1,0:T(8,128)S(1)} copy-done((f32[4,128,256]{2,1,0:T(8,128)S(1)}, f32[4,128,256]{2,1,0:T(8,128)}, u32[]{:S(2)}) %copy-start) | copy-done | bytes 524312
  1.7 0.6 tiles.1
  2.2 4.1 %collective-permute-start.1 = (bf16[1024,128]{1,0:T(8,128)(2,1)S(1)}, bf16[1024,128]{1,0:T(8,128)(2,1)S(1)}, u32[]{:S(2)}, u32[]{:S(2)}) collective-permute-start(bf16[1024,128]{1,0:T(8,128)(2,1)S(1)} %get-tuple-element.13.own_ref), channel_id=1, source_target_pairs={{0,4},{4,0},{1,5},{5,1},{2,6},{6,2},{3,7},{7,3},{8,12},{12,8},{9,1... | collective-permute-start | bytes 786440 | tf_op jit(solution)/shard_map/ppermute | solution.py:406
  6.3 0.7 pad_add_fusion.both_ref
  7.0 0.3 prep.1
  7.3 0.1 all_to_all.20
  7.4 10.3 %all_to_all.32 = s32[16,1,24]{2,1,0:T(1,128)S(1)} all-to-all(s32[16,1,24]{2,1,0:T(1,128)S(1)} %bitcast.15), channel_id=1, replica_groups=mesh['tx'=4,'th'=2,'tl'=4] {'tx','tl'}, dimensions={0} | all-to-all | bytes 3072 | tf_op jit(solution)/shard_map/all_to_all | solution.py:397
  17.7 0.1 collective-permute-start
  17.8 4.4 %collective-permute-done.rest_0_.far_ref = s32[16,24]{1,0:T(8,128)S(1)} collective-permute-done((s32[16,24]{1,0:T(8,128)S(1)}, s32[16,24]{1,0:T(8,128)S(1)}, u32[]{:S(2)}, u32[]{:S(2)}) %collective-permute-start) | collective-permute-done | bytes 1568 | tf_op jit(solution)/shard_map/ppermute | solution.py:406
  22.2 1.1 %gather.1 = bf16[16,192,128]{2,1,0:T(8,128)(2,1)S(1)} custom-call(s32[16,24]{1,0:T(8,128)S(1)} %bitcast.11, bf16[1024,128]{1,0:T(8,128)(2,1)S(1)} %get-tuple-element.13.own_ref, bf16[1024,128]{1,0:T(8,128)(2,1)S(1)} %collective-permute-done.1.other_ref, s32[16,24]{1,0:T(8,128)S(1)} %collective-permute-done.rest_0_.far_ref), custom_call_target="tpu_custom_call" | custom-call | tf_op jit(solution)/shard_map/gather/pallas_call | solution.py:144
  23.3 15.4 %all_to_all.33 = bf16[16,192,128]{2,1,0:T(8,128)(2,1)S(1)} all-to-all(bf16[16,192,128]{2,1,0:T(8,128)(2,1)S(1)} %gather.1), channel_id=1, replica_groups=mesh['tx'=4,'th'=2,'tl'=4] {'tx','tl'}, dimensions={0} | all-to-all | bytes 1572864 | tf_op jit(solution)/shard_map/all_to_all | solution.py:397
  38.7 9.1 %bins.1 = bf16[32,96,128]{2,1,0:T(8,128)(2,1)} custom-call(s32[2,256]{1,0:T(2,128)S(1)} %get-tuple-element.12.line_ref, bf16[32,96,128]{2,1,0:T(8,128)(2,1)S(1)} %bitcast.9, bf16[256,128,256]{2,1,0:T(8,128)(2,1)} %blocks_ref.1), custom_call_target="tpu_custom_call" | custom-call | tf_op jit(solution)/shard_map/bins/pallas_call | solution.py:230
  47.8 2.6 %all-to-all-start.2 = ((bf16[32,96,128]{2,1,0:T(8,128)(2,1)}), bf16[32,96,128]{2,1,0:T(8,128)(2,1)S(1)}, u32[]{:S(2)}, u32[]{:S(2)}) async-start(bf16[32,96,128]{2,1,0:T(8,128)(2,1)} %bins.1), calls=%async_computation.2 | async-start | bytes 1572864 | tf_op jit(solution)/shard_map/all_to_all | solution.py:397
  50.4 2.0 %collective-permute-start.2 = (bf16[4,256]{1,0:T(4,128)(2,1)S(1)}, bf16[4,256]{1,0:T(4,128)(2,1)S(1)}, u32[]{:S(2)}, u32[]{:S(2)}) collective-permute-start(bf16[4,256]{1,0:T(4,128)(2,1)S(1)} %get-tuple-element.14), channel_id=1, source_target_pairs={{0,8},{8,16},{16,24},{1,9},{9,17},{17,25},{2,10},{10,18},{18,26},{... | collective-permute-start | bytes 6152 | tf_op jit(solution)/shard_map/ppermute | solution.py:402
  52.5 1.3 %collective-permute-start.3 = (bf16[4,256]{1,0:T(4,128)(2,1)S(1)}, bf16[4,256]{1,0:T(4,128)(2,1)S(1)}, u32[]{:S(2)}, u32[]{:S(2)}) collective-permute-start(bf16[4,256]{1,0:T(4,128)(2,1)S(1)} %get-tuple-element.15), channel_id=1, source_target_pairs={{8,0},{16,8},{24,16},{9,1},{17,9},{25,17},{10,2},{18,10},{26,18},{... | collective-permute-start | bytes 6152 | tf_op jit(solution)/shard_map/ppermute | solution.py:402
  53.8 1.3 %collective-permute-start.5 = (bf16[4,128]{1,0:T(4,128)(2,1)S(1)}, bf16[4,128]{1,0:T(4,128)(2,1)S(1)}, u32[]{:S(2)}, u32[]{:S(2)}) collective-permute-start(bf16[4,128]{1,0:T(4,128)(2,1)S(1)} %get-tuple-element.19), channel_id=1, source_target_pairs={{1,0},{2,1},{3,2},{4,3},{5,4},{6,5},{7,6},{9,8},{10,9},{11,10},{12... | collective-permute-start | bytes 3080 | tf_op jit(solution)/shard_map/ppermute | solution.py:402
  55.1 4.5 %collective-permute-start.4 = (bf16[4,128]{1,0:T(4,128)(2,1)S(1)}, bf16[4,128]{1,0:T(4,128)(2,1)S(1)}, u32[]{:S(2)}, u32[]{:S(2)}) collective-permute-start(bf16[4,128]{1,0:T(4,128)(2,1)S(1)} %get-tuple-element.20), channel_id=1, source_target_pairs={{0,1},{1,2},{2,3},{3,4},{4,5},{5,6},{6,7},{8,9},{9,10},{10,11},{11... | collective-permute-start | bytes 3080 | tf_op jit(solution)/shard_map/ppermute | solution.py:402
  59.6 0.5 collective-permute-done.5.right_ref
  60.2 0.8 collective-permute-done.4.left_ref
  60.9 0.6 laplace.1.smooth_ref
  61.5 10.9 %all-to-all-done.2.arrived_ref = bf16[32,96,128]{2,1,0:T(8,128)(2,1)S(1)} async-done(((bf16[32,96,128]{2,1,0:T(8,128)(2,1)}), bf16[32,96,128]{2,1,0:T(8,128)(2,1)S(1)}, u32[]{:S(2)}, u32[]{:S(2)}) %all-to-all-start.2) | async-done | bytes 786464 | tf_op jit(solution)/shard_map/all_to_all | solution.py:397
  72.4 2.3 %image.1 = (f32[4,128,256]{2,1,0:T(8,128)S(1)}, f32[32,128]{1,0:T(8,128)S(1)}) custom-call(s32[16,24]{1,0:T(8,128)S(1)} %bitcast.12, s32[16,24]{1,0:T(8,128)S(1)} %collective-permute-done.rest_0_.far_ref, bf16[32,96,128]{2,1,0:T(8,128)(2,1)S(1)} %all-to-all-done.2.arrived_ref, f32[4,128,256]{2,1,0:T(8,128)S(1)} %laplace.1.smooth_ref, ...), custom_call_target="tpu_custom_call" | custom-call | tf_op jit(solution)/shard_map/image/pallas_call | solution.py:339
  74.7 9.1 %all_to_all.34 = f32[32,1,128]{2,1,0:T(1,128)S(1)} all-to-all(f32[32,1,128]{2,1,0:T(1,128)S(1)} %bitcast.14), channel_id=1, replica_groups=mesh['tx'=4,'th'=2,'tl'=4] {'tx','th','tl'}, dimensions={0} | all-to-all | bytes 32768 | tf_op jit(solution)/shard_map/all_to_all | solution.py:397
  83.8 1.4 %update.1 = (f32[4,128,256]{2,1,0:T(8,128)}, f32[4,128,256]{2,1,0:T(8,128)}, f32[4,128,256]{2,1,0:T(8,128)}) custom-call(f32[32,128]{1,0:T(8,128)S(1)} %bitcast.13, f32[4,128,256]{2,1,0:T(8,128)S(1)} %copy-done.3, f32[4,128,256]{2,1,0:T(8,128)S(1)} %copy-done.2, f32[4,128,256]{2,1,0:T(8,128)S(1)} %copy-done.1, f32[4,128,256]{2,1,0:T(8,128)S(1)} %get-tuple-element.18.image_ref), custom_call_target="tpu_custom_call" | custom-call | tf_op jit(solution)/shard_map/update/pallas_call | solution.py:384
  (11 shorter events, 0.0 us)
Async XLA Ops:
  0.6 1.0 %copy-start = (f32[4,128,256]{2,1,0:T(8,128)S(1)}, f32[4,128,256]{2,1,0:T(8,128)}, u32[]{:S(2)}) copy-start(f32[4,128,256]{2,1,0:T(8,128)} %direction_ref.3) | copy-start | bytes 1572868
  1.7 59.2 %copy-start.1 = (f32[4,128,256]{2,1,0:T(8,128)S(1)}, f32[4,128,256]{2,1,0:T(8,128)}, u32[]{:S(2)}) copy-start(f32[4,128,256]{2,1,0:T(8,128)} %direction_ref.3) | copy-start | bytes 1572868
  1.7 70.7 %copy-start.2 = (f32[4,128,256]{2,1,0:T(8,128)S(1)}, f32[4,128,256]{2,1,0:T(8,128)}, u32[]{:S(2)}) copy-start(f32[4,128,256]{2,1,0:T(8,128)} %residual_ref.3) | copy-start | bytes 1572868
  1.7 82.1 %copy-start.3 = (f32[4,128,256]{2,1,0:T(8,128)S(1)}, f32[4,128,256]{2,1,0:T(8,128)}, u32[]{:S(2)}) copy-start(f32[4,128,256]{2,1,0:T(8,128)} %solution_ref.1) | copy-start | bytes 1572868
  2.2 20.0 %collective-permute-start.1 = (bf16[1024,128]{1,0:T(8,128)(2,1)S(1)}, bf16[1024,128]{1,0:T(8,128)(2,1)S(1)}, u32[]{:S(2)}, u32[]{:S(2)}) collective-permute-start(bf16[1024,128]{1,0:T(8,128)(2,1)S(1)} %get-tuple-element.13.own_ref), channel_id=1, source_target_pairs={{0,4},{4,0},{1,5},{5,1},{2,6},{6,2},{3,7},{7,3},{8,12},{12,8},{9,1... | collective-permute-start | bytes 786440 | tf_op jit(solution)/shard_map/ppermute | solution.py:406
  17.7 4.5 %collective-permute-start = (s32[16,24]{1,0:T(8,128)S(1)}, s32[16,24]{1,0:T(8,128)S(1)}, u32[]{:S(2)}, u32[]{:S(2)}) collective-permute-start(s32[16,24]{1,0:T(8,128)S(1)} %bitcast.10), channel_id=1, source_target_pairs={{0,4},{4,0},{1,5},{5,1},{2,6},{6,2},{3,7},{7,3},{8,12},{12,8},{9,1... | collective-permute-start | bytes 4616 | tf_op jit(solution)/shard_map/ppermute | solution.py:406
  47.8 24.6 %all-to-all-start.2 = ((bf16[32,96,128]{2,1,0:T(8,128)(2,1)}), bf16[32,96,128]{2,1,0:T(8,128)(2,1)S(1)}, u32[]{:S(2)}, u32[]{:S(2)}) async-start(bf16[32,96,128]{2,1,0:T(8,128)(2,1)} %bins.1), calls=%async_computation.2 | async-start | bytes 1572864 | tf_op jit(solution)/shard_map/all_to_all | solution.py:397
  50.4 10.5 %collective-permute-start.2 = (bf16[4,256]{1,0:T(4,128)(2,1)S(1)}, bf16[4,256]{1,0:T(4,128)(2,1)S(1)}, u32[]{:S(2)}, u32[]{:S(2)}) collective-permute-start(bf16[4,256]{1,0:T(4,128)(2,1)S(1)} %get-tuple-element.14), channel_id=1, source_target_pairs={{0,8},{8,16},{16,24},{1,9},{9,17},{17,25},{2,10},{10,18},{18,26},{... | collective-permute-start | bytes 6152 | tf_op jit(solution)/shard_map/ppermute | solution.py:402
  52.5 8.5 %collective-permute-start.3 = (bf16[4,256]{1,0:T(4,128)(2,1)S(1)}, bf16[4,256]{1,0:T(4,128)(2,1)S(1)}, u32[]{:S(2)}, u32[]{:S(2)}) collective-permute-start(bf16[4,256]{1,0:T(4,128)(2,1)S(1)} %get-tuple-element.15), channel_id=1, source_target_pairs={{8,0},{16,8},{24,16},{9,1},{17,9},{25,17},{10,2},{18,10},{26,18},{... | collective-permute-start | bytes 6152 | tf_op jit(solution)/shard_map/ppermute | solution.py:402
  53.8 6.4 %collective-permute-start.5 = (bf16[4,128]{1,0:T(4,128)(2,1)S(1)}, bf16[4,128]{1,0:T(4,128)(2,1)S(1)}, u32[]{:S(2)}, u32[]{:S(2)}) collective-permute-start(bf16[4,128]{1,0:T(4,128)(2,1)S(1)} %get-tuple-element.19), channel_id=1, source_target_pairs={{1,0},{2,1},{3,2},{4,3},{5,4},{6,5},{7,6},{9,8},{10,9},{11,10},{12... | collective-permute-start | bytes 3080 | tf_op jit(solution)/shard_map/ppermute | solution.py:402
  55.1 5.8 %collective-permute-start.4 = (bf16[4,128]{1,0:T(4,128)(2,1)S(1)}, bf16[4,128]{1,0:T(4,128)(2,1)S(1)}, u32[]{:S(2)}, u32[]{:S(2)}) collective-permute-start(bf16[4,128]{1,0:T(4,128)(2,1)S(1)} %get-tuple-element.20), channel_id=1, source_target_pairs={{0,1},{1,2},{2,3},{3,4},{4,5},{5,6},{6,7},{8,9},{9,10},{10,11},{11... | collective-permute-start | bytes 3080 | tf_op jit(solution)/shard_map/ppermute | solution.py:402

commit v6 on v5

--- a/solution.py
+++ b/solution.py
@@ -77,7 +77,7 @@
     )(both)
 
 
-def tiles_kernel(field_ref, out_ref, top_ref, bottom_ref, sides_ref, held):
+def tiles_kernel(field_ref, out_ref, edges_ref, copy_ref, held):
     beacons, rows, cols = field_ref.shape
     bands, groups = rows // TILE_SIDE, cols // LANES
     for k in range(beacons):
@@ -88,15 +88,17 @@
                 for h in range(2):
                     at = (band * groups + g) * SUB * SUB + h * beacons + k
                     held[pl.ds(at, SUB, stride=SUB), :] = x[band * 2 + h]
-    out_ref[...] = held[...].astype(jnp.bfloat16)
-    top_ref[...] = field_ref[:, 0, :].astype(jnp.bfloat16)
-    bottom_ref[...] = field_ref[:, rows - 1, :].astype(jnp.bfloat16)
+    copy_ref[...] = field_ref[...]
+    count = held.shape[0]
+    out_ref[:count] = held[...].astype(jnp.bfloat16)
+    ends = [field_ref[k, r : r + 1, g * LANES : (g + 1) * LANES] for r in (0, rows - 1) for k in range(beacons) for g in range(groups)]
+    edges_ref[...] = jnp.concatenate(ends, axis=0).astype(jnp.bfloat16)
     lane = lax.broadcasted_iota(jnp.int32, (rows, LANES), 1)
-    ends = jnp.zeros((rows, LANES), jnp.float32)
-    for k in range(beacons):
-        ends = jnp.where(lane == k, field_ref[k, :, cols - 1 :], ends)
-        ends = jnp.where(lane == beacons + k, field_ref[k, :, :1], ends)
-    sides_ref[...] = ends.T[: 2 * beacons].astype(jnp.bfloat16)
+    sides = jnp.zeros((rows, LANES), jnp.float32)
+    for k in range(beacons):
+        sides = jnp.where(lane == k, field_ref[k, :, cols - 1 :], sides)
+        sides = jnp.where(lane == beacons + k, field_ref[k, :, :1], sides)
+    out_ref[count:] = sides.T[: 2 * SUB].astype(jnp.bfloat16)
 
 
 def tiles(field):
@@ -104,12 +106,11 @@
     return pl.pallas_call(
         tiles_kernel,
         in_specs=[whole()],
-        out_specs=[whole()] * 4,
+        out_specs=[whole()] * 3,
         out_shape=[
-            jax.ShapeDtypeStruct((beacons * rows * cols // LANES, LANES), jnp.bfloat16),
-            jax.ShapeDtypeStruct((beacons, cols), jnp.bfloat16),
-            jax.ShapeDtypeStruct((beacons, cols), jnp.bfloat16),
-            jax.ShapeDtypeStruct((2 * beacons, rows), jnp.bfloat16),
+            jax.ShapeDtypeStruct((beacons * rows * cols // LANES + 2 * SUB, LANES), jnp.bfloat16),
+            jax.ShapeDtypeStruct((2 * SUB, LANES), jnp.bfloat16),
+            jax.ShapeDtypeStruct(field.shape, field.dtype),
         ],
         scratch_shapes=[pltpu.VMEM((beacons * rows * cols // LANES, LANES), jnp.float32)],
         compiler_params=params(8),
@@ -117,12 +118,11 @@
     )(field)
 
 
-def gather_kernel(cap, wanted_ref, own_ref, other_ref, *rest):
-    *after, out_ref, held = rest
-    peers, lines = wanted_ref.shape[0], out_ref.shape[1] // 2
-    rows = own_ref.shape[0]
-    held[:rows] = own_ref[...].astype(jnp.float32)
-    held[rows:] = other_ref[...].astype(jnp.float32)
+def gather_kernel(cap, wanted_ref, own_ref, other_ref, edges_ref, after_ref, out_ref, held):
+    peers, lines = wanted_ref.shape[0], out_ref.shape[1] // 2 - SUB
+    rows = held.shape[0] // 2
+    held[:rows] = own_ref[:rows].astype(jnp.float32)
+    held[rows:] = other_ref[:rows].astype(jnp.float32)
 
     def at(d, r):
         return held[pl.ds(pl.multiple_of(wanted_ref[d, r], SUB), SUB), :]
@@ -138,24 +138,73 @@
 
     lax.fori_loop(0, peers, body, 0, unroll=2)
 
-
-def gather(wanted, own, other, lines, *after):
+    tx, th, tl = (lax.axis_index(axis) for axis in AXES)
+    deep, span = lax.axis_size("tx"), lax.axis_size("tl")
+    edges = edges_ref[...].astype(jnp.float32)
+    none = jnp.zeros((SUB, LANES), jnp.float32)
+    own = jnp.concatenate([none, own_ref[rows:].astype(jnp.float32)[:SUB]], axis=0).astype(jnp.bfloat16)
+    other = jnp.concatenate([none, other_ref[rows:].astype(jnp.float32)[:SUB]], axis=0).astype(jnp.bfloat16)
+    top = jnp.concatenate([edges[:SUB], none], axis=0).astype(jnp.bfloat16)
+    bottom = jnp.concatenate([edges[SUB:], none], axis=0).astype(jnp.bfloat16)
+    for there, x, y, block in (
+        (tx > 0, tx - 1, tl, top),
+        (tx < deep - 1, tx + 1, tl, bottom),
+        (tl > 0, tx, tl - 1, own),
+        (tl < span - 1, tx, tl + 1, own),
+        ((th == 0) & (tl == 0), tx, span - 1, other),
+        ((th == 1) & (tl == span - 1), tx, 0, other),
+    ):
+
+        @pl.when(there)
+        def _(x=x, y=y, block=block):
+            out_ref[jnp.clip(x * span + y, 0, peers - 1), 2 * lines :, :] = block
+
+
+def gather(wanted, own, other, edges, after, lines):
     peers = wanted.shape[0]
     return pl.pallas_call(
         functools.partial(gather_kernel, wanted.shape[1] // 2),
-        in_specs=[whole(pltpu.SMEM), whole(), whole()] + [whole(pl.ANY)] * len(after),
+        in_specs=[whole(pltpu.SMEM), whole(), whole(), whole(), whole(pl.ANY)],
         out_specs=whole(),
-        out_shape=jax.ShapeDtypeStruct((peers, 2 * lines, LANES), jnp.bfloat16),
-        scratch_shapes=[pltpu.VMEM((2 * own.shape[0], LANES), jnp.float32)],
+        out_shape=jax.ShapeDtypeStruct((peers, 2 * lines + 2 * SUB, LANES), jnp.bfloat16),
+        scratch_shapes=[pltpu.VMEM((2 * own.shape[0] - 4 * SUB, LANES), jnp.float32)],
         compiler_params=params(8),
         name="gather",
-    )(wanted, own, other, *after)
+    )(wanted, own, other, edges, after)
+
+
+def smooth(field_ref, fetched_ref, at, out_ref):
+    beacons, rows, cols = field_ref.shape
+    tx, th, tl = (lax.axis_index(axis) for axis in AXES)
+    deep, span = lax.axis_size("tx"), lax.axis_size("tl")
+    peers = fetched_ref.shape[0]
+
+    def edge(there, x, y):
+        peer = jnp.clip(x * span + y, 0, peers - 1)
+        return jnp.where(there, fetched_ref[peer, at : at + 2 * SUB, :].astype(jnp.float32), 0.0)
+
+    def line_of(block, k):
+        return jnp.concatenate([block[2 * k : 2 * k + 1], block[2 * k + 1 : 2 * k + 2]], axis=1)
+
+    above, below = edge(tx > 0, tx - 1, tl), edge(tx < deep - 1, tx + 1, tl)
+    left = edge((tl > 0) | (th == 1), tx, jnp.where(tl > 0, tl - 1, span - 1))
+    right = edge((tl < span - 1) | (th == 0), tx, jnp.where(tl < span - 1, tl + 1, 0))
+    sides = jnp.concatenate([left[SUB : SUB + beacons], right[SUB + beacons : SUB + 2 * beacons]], axis=0).T
+    row = lax.broadcasted_iota(jnp.int32, (rows, cols), 0)
+    col = lax.broadcasted_iota(jnp.int32, (rows, cols), 1)
+    for k in range(beacons):
+        x = field_ref[k]
+        near = jnp.where(row == 0, line_of(above, k), pltpu.roll(x, 1, 0))
+        near += jnp.where(row == rows - 1, line_of(below, k), pltpu.roll(x, rows - 1, 0))
+        near += jnp.where(col == 0, sides[:, k : k + 1], pltpu.roll(x, 1, 1))
+        near += jnp.where(col == cols - 1, sides[:, beacons + k : beacons + k + 1], pltpu.roll(x, cols - 1, 1))
+        out_ref[k] = smooth_weight * (4.0 * x - near)
 
 
 def bins_kernel(
-    group, line_ref, fetched_ref, blocks_ref, out_ref, held_ref, turn_a, turn_b, samp_a, samp_b, pick, ret, sems
+    group, line_ref, fetched_ref, blocks_ref, field_ref, out_ref, smooth_ref, held_ref, turn_a, turn_b, samp_a, samp_b, pick, ret, sems
 ):
-    devices, lines, _ = fetched_ref.shape
+    devices, lines, _ = out_ref.shape
     count, samples, cells = blocks_ref.shape
     groups, pairs = count // group, group // 2
 
@@ -166,9 +215,10 @@
     for i in range(groups):
         fetch(i).start()
     for d in range(devices):
-        pick[pl.ds(d * lines, lines), :] = fetched_ref[d].astype(jnp.float32)
+        pick[pl.ds(d * lines, lines), :] = fetched_ref[d // 2, d % 2 * lines : (d % 2 + 1) * lines, :].astype(jnp.float32)
         ret[pl.ds(d * lines, lines), :] = jnp.zeros((lines, LANES), jnp.float32)
     samp_b[...] = jnp.zeros_like(samp_b)
+    smooth(field_ref, fetched_ref, 2 * lines, smooth_ref)
     low = lax.broadcasted_iota(jnp.int32, (SUB, LANES), 0) < 4
 
     def weights(g, p):
@@ -223,15 +273,18 @@
         out_ref[d] = ret[pl.ds(d * lines, lines), :].astype(jnp.bfloat16)
 
 
-def bins(line, fetched, blocks):
-    devices, lines, _ = fetched.shape
+def bins(line, fetched, blocks, field, lines):
     count, samples, cells = blocks.shape
+    devices = 2 * fetched.shape[0]
     group = 16
     return pl.pallas_call(
         functools.partial(bins_kernel, group),
-        in_specs=[whole(pltpu.SMEM), whole()] + [whole(pl.ANY)],
-        out_specs=whole(),
-        out_shape=jax.ShapeDtypeStruct((devices, lines, LANES), jnp.bfloat16),
+        in_specs=[whole(pltpu.SMEM), whole(), whole(pl.ANY), whole()],
+        out_specs=[whole()] * 2,
+        out_shape=[
+            jax.ShapeDtypeStruct((devices, lines, LANES), jnp.bfloat16),
+            jax.ShapeDtypeStruct(field.shape, jnp.float32),
+        ],
         scratch_shapes=[pltpu.VMEM(blocks.shape, jnp.bfloat16)]
         + [pltpu.VMEM((group // 2, cells, 2 * samples), jnp.bfloat16)] * 2
         + [pltpu.VMEM((group // 2, SUB, 2 * samples), jnp.float32)] * 2
@@ -239,33 +292,7 @@
         + [pltpu.SemaphoreType.DMA((count // group,))],
         compiler_params=params(50),
         name="bins",
-    )(line, fetched, blocks)
-
-
-def laplace_kernel(field_ref, above_ref, below_ref, left_ref, right_ref, out_ref):
-    beacons, rows, cols = field_ref.shape
-    row = lax.broadcasted_iota(jnp.int32, (rows, cols), 0)
-    col = lax.broadcasted_iota(jnp.int32, (rows, cols), 1)
-    above, below = above_ref[...].astype(jnp.float32), below_ref[...].astype(jnp.float32)
-    sides = jnp.concatenate([left_ref[...].astype(jnp.float32), right_ref[...].astype(jnp.float32)], axis=0).T
-    for k in range(beacons):
-        x = field_ref[k]
-        up = jnp.where(row == 0, above[k : k + 1, :], pltpu.roll(x, 1, 0))
-        down = jnp.where(row == rows - 1, below[k : k + 1, :], pltpu.roll(x, rows - 1, 0))
-        left = jnp.where(col == 0, sides[:, k : k + 1], pltpu.roll(x, 1, 1))
-        right = jnp.where(col == cols - 1, sides[:, beacons + k : beacons + k + 1], pltpu.roll(x, cols - 1, 1))
-        out_ref[k] = smooth_weight * (4.0 * x - (down + up + right + left))
-
-
-def laplace(field, above, below, left, right):
-    return pl.pallas_call(
-        laplace_kernel,
-        in_specs=[whole()] * 5,
-        out_specs=whole(),
-        out_shape=jax.ShapeDtypeStruct(field.shape, jnp.float32),
-        compiler_params=params(8),
-        name="laplace",
-    )(field, above, below, left, right)
+    )(line, fetched, blocks, field)
 
 
 def image_kernel(near_ref, far_ref, arrived_ref, smooth_ref, direction_ref, residual_ref, image_ref, stats_ref, *sums):
@@ -397,11 +424,6 @@
     return lax.all_to_all(x, axes, split_axis=0, concat_axis=0, tiled=True)
 
 
-def shift(x, axis, step):
-    size = lax.axis_size(axis)
-    return lax.ppermute(x, axis, [(i, i + step) for i in range(size) if 0 <= i + step < size])
-
-
 def trade(x):
     return lax.ppermute(x, "th", [(0, 1), (1, 0)])
 
@@ -413,18 +435,16 @@
     lines = -(-cap // 2) * 2 * SUB
     beacons, rows, cols = direction.shape
 
-    own, top, bottom, sides = tiles(direction)
+    own, edges, direction = tiles(direction)
     other = trade(own)
     both = jnp.concatenate([bin_owner.reshape(1, count), bin_tile.reshape(1, count)], axis=0)
     line, request = prep(both, devices, cap, lines, span, rows * cols // TILE_SIDE**2)
     near = exchange(request.reshape(devices // 2, 2 * cap), HALF)
     far = trade(near)
-    above, below = shift(bottom, "tx", 1), shift(top, "tx", -1)
-    left, right = shift(sides[:beacons], TY, 1), shift(sides[beacons:], TY, -1)
-    smooth = laplace(direction, above, below, left, right)
-    fetched = exchange(gather(near, own, other, lines, far), HALF).reshape(devices, lines, LANES)
-    arrived = exchange(bins(line, fetched, blocks), AXES)
-    image, stats = image_of(near, far, arrived, smooth, direction, residual)
+    fetched = exchange(gather(near, own, other, edges, far, lines), HALF)
+    returned, smoothed = bins(line, fetched, blocks, direction, lines)
+    arrived = exchange(returned, AXES)
+    image, stats = image_of(near, far, arrived, smoothed, direction, residual)
     return update(exchange(stats, AXES), solution, residual, direction, image)
 
 

time: 85.6 us -> 85 us (level)
  blocking collectives: 34.8 us -> 59.7 us
  waiting for transfers between devices: 16.6 us -> 4.41 us
  starting transfers between devices: 16 us -> 4.21 us
  Pallas kernels: 15.3 us -> 13.9 us
    all_to_all x3 -> x4, blocking collectives: 34.8 us -> 59.7 us  [exchange(): return lax.all_to_all(x, axes, split_axis=0, concat_axis=0, tiled=True)]
    all_to_all x1 -> x0, waiting for transfers between devices: 10.9 us -> none  [exchange(): return lax.all_to_all(x, axes, split_axis=0, concat_axis=0, tiled=True)]
    ppermute x4 -> x0, starting transfers between devices: 9.15 us -> none  [shift(): lax.ppermute(x, axis, [(i, i + step) for i in range(size) if 0 <= i + ste...]
    all_to_all x1 -> x0, starting transfers between devices: 2.64 us -> none  [exchange(): return lax.all_to_all(x, axes, split_axis=0, concat_axis=0, tiled=True)]
    ppermute x4 -> x0, waiting for transfers between devices: 1.29 us -> none  [shift(): lax.ppermute(x, axis, [(i, i + step) for i in range(size) if 0 <= i + ste...]
  transfers between devices with their start and end apart: 7 -> 2, of which waited for: 4 -> 1; matrix products, arithmetic and copies ran while one was open for 1% -> 1% of each run, Pallas kernels for 1% -> 0%
where the time goes in v6:
time: 85 us; the launch traced here: 84.8 us
  blocking collectives  59.7 us (70%)
  Pallas kernels  13.9 us (16%)
  waiting for transfers between devices  4.41 us (5%)
  starting transfers between devices  4.21 us (5%)
  local copies, waits for them, and re-layouts  1.17 us (1%)
    all_to_all x4, blocking collectives, exchange(): return lax.all_to_all(x, axes, split_axis=0, concat_axis=0, tiled=True)  59.7 us
    pallas_call x1, Pallas kernels, bins(): pl.pallas_call(functools.partial(bins_kernel, group), in_specs=[whole(plt...  8.28 us
    ppermute x2, waiting for transfers between devices, trade(): return lax.ppermute(x, 'th', [(0, 1), (1, 0)])  4.41 us
    ppermute x2, starting transfers between devices, trade(): return lax.ppermute(x, 'th', [(0, 1), (1, 0)])  4.21 us
    pallas_call x1, Pallas kernels, image_of(): pl.pallas_call(image_kernel, in_specs=[whole(pltpu.SMEM)] * 2 + [whole()]...  2.3 us
  transfers between devices with their start and end apart: 2, of which 1 were waited for; matrix products, arithmetic and copies ran while one was open for 1% of the time, Pallas kernels for 0%

profile of v6, /device:TPU:0, one launch (start us, length us, event | category | flops | bytes accessed | tf_op | source)
XLA Modules:
  0.0 84.8 jit_solution(6187590923319999439)
XLA Ops:
  0.6 0.0 copy-start
  0.6 0.0 copy-start.1
  0.7 1.1 %copy-done.1 = f32[4,128,256]{2,1,0:T(8,128)S(1)} copy-done((f32[4,128,256]{2,1,0:T(8,128)S(1)}, f32[4,128,256]{2,1,0:T(8,128)}, u32[]{:S(2)}) %copy-start.1) | copy-done | bytes 524312
  1.7 0.0 copy-start.2
  1.7 0.6 tiles.1
  2.3 4.1 %collective-permute-start.1 = (bf16[1040,128]{1,0:T(8,128)(2,1)S(1)}, bf16[1040,128]{1,0:T(8,128)(2,1)S(1)}, u32[]{:S(2)}, u32[]{:S(2)}) collective-permute-start(bf16[1040,128]{1,0:T(8,128)(2,1)S(1)} %get-tuple-element.14.own_ref), channel_id=1, source_target_pairs={{0,4},{4,0},{1,5},{5,1},{2,6},{6,2},{3,7},{7,3},{8,12},{12,8},{9,1... | collective-permute-start | bytes 798728 | tf_op jit(solution)/shard_map/ppermute | solution.py:428
  6.4 0.7 pad_add_fusion.both_ref
  7.1 0.3 prep.1
  7.4 0.1 all_to_all.20
  7.4 10.3 %all_to_all.32 = s32[16,1,24]{2,1,0:T(1,128)S(1)} all-to-all(s32[16,1,24]{2,1,0:T(1,128)S(1)} %bitcast.13), channel_id=1, replica_groups=mesh['tx'=4,'th'=2,'tl'=4] {'tx','tl'}, dimensions={0} | all-to-all | bytes 3072 | tf_op jit(solution)/shard_map/all_to_all | solution.py:424
  17.7 0.1 collective-permute-start
  17.9 4.4 %collective-permute-done.after_ref.far_ref = s32[16,24]{1,0:T(8,128)S(1)} collective-permute-done((s32[16,24]{1,0:T(8,128)S(1)}, s32[16,24]{1,0:T(8,128)S(1)}, u32[]{:S(2)}, u32[]{:S(2)}) %collective-permute-start) | collective-permute-done | bytes 1568 | tf_op jit(solution)/shard_map/ppermute | solution.py:428
  22.3 0.0 collective-permute-done.1.other_ref
  22.3 1.1 %gather.1 = bf16[16,208,128]{2,1,0:T(8,128)(2,1)S(1)} custom-call(s32[16,24]{1,0:T(8,128)S(1)} %bitcast.9, bf16[1040,128]{1,0:T(8,128)(2,1)S(1)} %get-tuple-element.14.own_ref, bf16[1040,128]{1,0:T(8,128)(2,1)S(1)} %collective-permute-done.1.other_ref, bf16[16,128]{1,0:T(8,128)(2,1)S(1)} %get-tuple-element.15.edges_ref, ...), custom_call_target="tpu_custom_call" | custom-call | tf_op jit(solution)/shard_map/gather/pallas_call | solution.py:165
  23.4 16.0 %all_to_all.33.fetched_ref = bf16[16,208,128]{2,1,0:T(8,128)(2,1)S(1)} all-to-all(bf16[16,208,128]{2,1,0:T(8,128)(2,1)S(1)} %gather.1), channel_id=1, replica_groups=mesh['tx'=4,'th'=2,'tl'=4] {'tx','tl'}, dimensions={0} | all-to-all | bytes 1703936 | tf_op jit(solution)/shard_map/all_to_all | solution.py:424
  39.5 8.3 %bins.1 = (bf16[32,96,128]{2,1,0:T(8,128)(2,1)S(1)}, f32[4,128,256]{2,1,0:T(8,128)S(1)}) custom-call(s32[2,256]{1,0:T(2,128)S(1)} %get-tuple-element.13.line_ref, bf16[16,208,128]{2,1,0:T(8,128)(2,1)S(1)} %all_to_all.33.fetched_ref, bf16[256,128,256]{2,1,0:T(8,128)(2,1)} %blocks_ref.1, f32[4,128,256]{2,1,0:T(8,128)S(1)} %get-tuple-element.16.field_ref.direction_ref), custom_call_target="tpu_custom_call" | custom-call | tf_op jit(solution)/shard_map/bins/pallas_call | solution.py:280
  47.8 24.1 %all_to_all.34.arrived_ref = bf16[32,96,128]{2,1,0:T(8,128)(2,1)S(1)} all-to-all(bf16[32,96,128]{2,1,0:T(8,128)(2,1)S(1)} %get-tuple-element.17), channel_id=1, replica_groups=mesh['tx'=4,'th'=2,'tl'=4] {'tx','th','tl'}, dimensions={0} | all-to-all | bytes 1572864 | tf_op jit(solution)/shard_map/all_to_all | solution.py:424
  71.9 0.0 copy-done
  71.9 2.3 %image.1 = (f32[4,128,256]{2,1,0:T(8,128)S(1)}, f32[32,128]{1,0:T(8,128)S(1)}) custom-call(s32[16,24]{1,0:T(8,128)S(1)} %bitcast.10, s32[16,24]{1,0:T(8,128)S(1)} %collective-permute-done.after_ref.far_ref, bf16[32,96,128]{2,1,0:T(8,128)(2,1)S(1)} %all_to_all.34.arrived_ref, f32[4,128,256]{2,1,0:T(8,128)S(1)} %get-tuple-element.18.smooth_ref, ...), custom_call_target="tpu_custom_call" | custom-call | tf_op jit(solution)/shard_map/image/pallas_call | solution.py:366
  74.2 9.2 %all_to_all.35 = f32[32,1,128]{2,1,0:T(1,128)S(1)} all-to-all(f32[32,1,128]{2,1,0:T(1,128)S(1)} %bitcast.12), channel_id=1, replica_groups=mesh['tx'=4,'th'=2,'tl'=4] {'tx','th','tl'}, dimensions={0} | all-to-all | bytes 32768 | tf_op jit(solution)/shard_map/all_to_all | solution.py:424
  83.4 0.0 copy-done.2
  83.4 1.4 %update.1 = (f32[4,128,256]{2,1,0:T(8,128)}, f32[4,128,256]{2,1,0:T(8,128)}, f32[4,128,256]{2,1,0:T(8,128)}) custom-call(f32[32,128]{1,0:T(8,128)S(1)} %bitcast.11, f32[4,128,256]{2,1,0:T(8,128)S(1)} %copy-done.2, f32[4,128,256]{2,1,0:T(8,128)S(1)} %copy-done, f32[4,128,256]{2,1,0:T(8,128)S(1)} %get-tuple-element.16.field_ref.direction_ref, ...), custom_call_target="tpu_custom_call" | custom-call | tf_op jit(solution)/shard_map/update/pallas_call | solution.py:411
Async XLA Ops:
  0.6 71.2 %copy-start = (f32[4,128,256]{2,1,0:T(8,128)S(1)}, f32[4,128,256]{2,1,0:T(8,128)}, u32[]{:S(2)}) copy-start(f32[4,128,256]{2,1,0:T(8,128)} %residual_ref.3) | copy-start | bytes 1572868
  0.6 1.1 %copy-start.1 = (f32[4,128,256]{2,1,0:T(8,128)S(1)}, f32[4,128,256]{2,1,0:T(8,128)}, u32[]{:S(2)}) copy-start(f32[4,128,256]{2,1,0:T(8,128)} %field_ref.1) | copy-start | bytes 1572868
  1.7 81.6 %copy-start.2 = (f32[4,128,256]{2,1,0:T(8,128)S(1)}, f32[4,128,256]{2,1,0:T(8,128)}, u32[]{:S(2)}) copy-start(f32[4,128,256]{2,1,0:T(8,128)} %solution_ref.1) | copy-start | bytes 1572868
  2.3 20.0 %collective-permute-start.1 = (bf16[1040,128]{1,0:T(8,128)(2,1)S(1)}, bf16[1040,128]{1,0:T(8,128)(2,1)S(1)}, u32[]{:S(2)}, u32[]{:S(2)}) collective-permute-start(bf16[1040,128]{1,0:T(8,128)(2,1)S(1)} %get-tuple-element.14.own_ref), channel_id=1, source_target_pairs={{0,4},{4,0},{1,5},{5,1},{2,6},{6,2},{3,7},{7,3},{8,12},{12,8},{9,1... | collective-permute-start | bytes 798728 | tf_op jit(solution)/shard_map/ppermute | solution.py:428
  17.7 4.5 %collective-permute-start = (s32[16,24]{1,0:T(8,128)S(1)}, s32[16,24]{1,0:T(8,128)S(1)}, u32[]{:S(2)}, u32[]{:S(2)}) collective-permute-start(s32[16,24]{1,0:T(8,128)S(1)} %bitcast.8), channel_id=1, source_target_pairs={{0,4},{4,0},{1,5},{5,1},{2,6},{6,2},{3,7},{7,3},{8,12},{12,8},{9,1... | collective-permute-start | bytes 4616 | tf_op jit(solution)/shard_map/ppermute | solution.py:428

commit v7 on v6

--- a/solution.py
+++ b/solution.py
@@ -118,11 +118,14 @@
     )(field)
 
 
-def gather_kernel(cap, wanted_ref, own_ref, other_ref, edges_ref, after_ref, out_ref, held):
+def gather_kernel(cap, wanted_vmem, own_ref, other_ref, edges_ref, after_ref, out_ref, held, wanted_ref, sem):
+    copy = pltpu.make_async_copy(wanted_vmem, wanted_ref, sem)
+    copy.start()
     peers, lines = wanted_ref.shape[0], out_ref.shape[1] // 2 - SUB
     rows = held.shape[0] // 2
     held[:rows] = own_ref[:rows].astype(jnp.float32)
     held[rows:] = other_ref[:rows].astype(jnp.float32)
+    copy.wait()
 
     def at(d, r):
         return held[pl.ds(pl.multiple_of(wanted_ref[d, r], SUB), SUB), :]
@@ -164,10 +167,14 @@
     peers = wanted.shape[0]
     return pl.pallas_call(
         functools.partial(gather_kernel, wanted.shape[1] // 2),
-        in_specs=[whole(pltpu.SMEM), whole(), whole(), whole(), whole(pl.ANY)],
+        in_specs=[whole()] * 4 + [whole(pl.ANY)],
         out_specs=whole(),
         out_shape=jax.ShapeDtypeStruct((peers, 2 * lines + 2 * SUB, LANES), jnp.bfloat16),
-        scratch_shapes=[pltpu.VMEM((2 * own.shape[0] - 4 * SUB, LANES), jnp.float32)],
+        scratch_shapes=[
+            pltpu.VMEM((2 * own.shape[0] - 4 * SUB, LANES), jnp.float32),
+            pltpu.SMEM(wanted.shape, jnp.int32),
+            pltpu.SemaphoreType.DMA,
+        ],
         compiler_params=params(8),
         name="gather",
     )(wanted, own, other, edges, after)
@@ -202,8 +209,9 @@
 
 
 def bins_kernel(
-    group, line_ref, fetched_ref, blocks_ref, field_ref, out_ref, smooth_ref, held_ref, turn_a, turn_b, samp_a, samp_b, pick, ret, sems
+    group, line_vmem, fetched_ref, blocks_ref, field_ref, out_ref, smooth_ref, *scratch
 ):
+    held_ref, turn_a, turn_b, samp_a, samp_b, pick, ret, line_ref, sems, sem = scratch
     devices, lines, _ = out_ref.shape
     count, samples, cells = blocks_ref.shape
     groups, pairs = count // group, group // 2
@@ -214,6 +222,8 @@
 
     for i in range(groups):
         fetch(i).start()
+    copy = pltpu.make_async_copy(line_vmem, line_ref, sem)
+    copy.start()
     for d in range(devices):
         pick[pl.ds(d * lines, lines), :] = fetched_ref[d // 2, d % 2 * lines : (d % 2 + 1) * lines, :].astype(jnp.float32)
         ret[pl.ds(d * lines, lines), :] = jnp.zeros((lines, LANES), jnp.float32)
@@ -248,6 +258,7 @@
             ret[line(g * group + 2 * p, 1), :] = jnp.where(low, left, pltpu.roll(right, 4, 0))
             ret[line(g * group + 2 * p + 1, 1), :] = jnp.where(low, pltpu.roll(left, 4, 0), right)
 
+    copy.wait()
     fetch(0).wait()
     turn(0, turn_a)
 
@@ -279,7 +290,7 @@
     group = 16
     return pl.pallas_call(
         functools.partial(bins_kernel, group),
-        in_specs=[whole(pltpu.SMEM), whole(), whole(pl.ANY), whole()],
+        in_specs=[whole(), whole(), whole(pl.ANY), whole()],
         out_specs=[whole()] * 2,
         out_shape=[
             jax.ShapeDtypeStruct((devices, lines, LANES), jnp.bfloat16),
@@ -289,13 +300,19 @@
         + [pltpu.VMEM((group // 2, cells, 2 * samples), jnp.bfloat16)] * 2
         + [pltpu.VMEM((group // 2, SUB, 2 * samples), jnp.float32)] * 2
         + [pltpu.VMEM((devices * lines, LANES), jnp.float32)] * 2
-        + [pltpu.SemaphoreType.DMA((count // group,))],
+        + [pltpu.SMEM(line.shape, jnp.int32), pltpu.SemaphoreType.DMA((count // group,)), pltpu.SemaphoreType.DMA],
         compiler_params=params(50),
         name="bins",
     )(line, fetched, blocks, field)
 
 
-def image_kernel(near_ref, far_ref, arrived_ref, smooth_ref, direction_ref, residual_ref, image_ref, stats_ref, *sums):
+def image_kernel(near_vmem, far_vmem, arrived_ref, smooth_ref, direction_ref, residual_ref, image_ref, stats_ref, *scratch):
+    *sums, near_ref, far_ref, sems = scratch
+    copies = [
+        pltpu.make_async_copy(a, b, sems.at[i]) for i, (a, b) in enumerate(((near_vmem, near_ref), (far_vmem, far_ref)))
+    ]
+    for copy in copies:
+        copy.start()
     peers, cap = near_ref.shape[0], near_ref.shape[1] // 2
     beacons, rows, cols = direction_ref.shape
     bands, groups = rows // TILE_SIDE, cols // LANES
@@ -303,6 +320,8 @@
     half = lax.axis_index("th")
     for total in sums:
         total[...] = jnp.zeros_like(total)
+    for copy in copies:
+        copy.wait()
 
     def body(q, carry):
         row, place = lax.div(q, span) * (2 * span), lax.rem(q, span)
@@ -365,13 +384,15 @@
     beacons, rows, cols = direction.shape
     return pl.pallas_call(
         image_kernel,
-        in_specs=[whole(pltpu.SMEM)] * 2 + [whole()] * 4,
+        in_specs=[whole()] * 6,
         out_specs=[whole(), whole()],
         out_shape=[
             jax.ShapeDtypeStruct(direction.shape, jnp.float32),
             jax.ShapeDtypeStruct((arrived.shape[0], LANES), jnp.float32),
         ],
-        scratch_shapes=[pltpu.VMEM((beacons * rows * cols // LANES, LANES), jnp.float32)] * 4,
+        scratch_shapes=[pltpu.VMEM((beacons * rows * cols // LANES, LANES), jnp.float32)] * 4
+        + [pltpu.SMEM(near.shape, jnp.int32)] * 2
+        + [pltpu.SemaphoreType.DMA((2,))],
         compiler_params=params(16),
         name="image",
     )(near, far, arrived, smooth, direction, residual)

time: 85 us -> 84.7 us (level)
  no operation moved by 1% of the time
where the time goes in v7:
time: 84.7 us; the launch traced here: 84.4 us
  blocking collectives  59.6 us (70%)
  Pallas kernels  13.6 us (16%)
  waiting for transfers between devices  4.41 us (5%)
  starting transfers between devices  4.21 us (5%)
  local copies, waits for them, and re-layouts  1.17 us (1%)
    all_to_all x4, blocking collectives, exchange(): return lax.all_to_all(x, axes, split_axis=0, concat_axis=0, tiled=True)  59.6 us
    pallas_call x1, Pallas kernels, bins(): pl.pallas_call(functools.partial(bins_kernel, group), in_specs=[whole(),...  8.11 us
    ppermute x2, waiting for transfers between devices, trade(): return lax.ppermute(x, 'th', [(0, 1), (1, 0)])  4.41 us
    ppermute x2, starting transfers between devices, trade(): return lax.ppermute(x, 'th', [(0, 1), (1, 0)])  4.21 us
    pallas_call x1, Pallas kernels, image_of(): pl.pallas_call(image_kernel, in_specs=[whole()] * 6, out_specs=[whole(),...  2.19 us
  transfers between devices with their start and end apart: 2, of which 1 were waited for; matrix products, arithmetic and copies ran while one was open for 1% of the time, Pallas kernels for 0%

profile of v7, /device:TPU:0, one launch (start us, length us, event | category | flops | bytes accessed | tf_op | source)
XLA Modules:
  0.0 84.4 jit_solution(13631010495204482054)
XLA Ops:
  0.6 0.0 copy-start
  0.6 0.0 copy-start.1
  0.7 1.1 %copy-done.1 = f32[4,128,256]{2,1,0:T(8,128)S(1)} copy-done((f32[4,128,256]{2,1,0:T(8,128)S(1)}, f32[4,128,256]{2,1,0:T(8,128)}, u32[]{:S(2)}) %copy-start.1) | copy-done | bytes 524312
  1.7 0.0 copy-start.2
  1.7 0.6 tiles.1
  2.3 4.1 %collective-permute-start.1 = (bf16[1040,128]{1,0:T(8,128)(2,1)S(1)}, bf16[1040,128]{1,0:T(8,128)(2,1)S(1)}, u32[]{:S(2)}, u32[]{:S(2)}) collective-permute-start(bf16[1040,128]{1,0:T(8,128)(2,1)S(1)} %get-tuple-element.14.own_ref), channel_id=1, source_target_pairs={{0,4},{4,0},{1,5},{5,1},{2,6},{6,2},{3,7},{7,3},{8,12},{12,8},{9,1... | collective-permute-start | bytes 798728 | tf_op jit(solution)/shard_map/ppermute | solution.py:449
  6.4 0.7 pad_add_fusion.both_ref
  7.1 0.3 prep.1
  7.4 0.1 all_to_all.20
  7.4 10.3 %all_to_all.32 = s32[16,1,24]{2,1,0:T(1,128)S(1)} all-to-all(s32[16,1,24]{2,1,0:T(1,128)S(1)} %bitcast.13), channel_id=1, replica_groups=mesh['tx'=4,'th'=2,'tl'=4] {'tx','tl'}, dimensions={0} | all-to-all | bytes 3072 | tf_op jit(solution)/shard_map/all_to_all | solution.py:445
  17.7 0.1 collective-permute-start
  17.9 4.4 %collective-permute-done.after_ref.far_vmem = s32[16,24]{1,0:T(8,128)S(1)} collective-permute-done((s32[16,24]{1,0:T(8,128)S(1)}, s32[16,24]{1,0:T(8,128)S(1)}, u32[]{:S(2)}, u32[]{:S(2)}) %collective-permute-start) | collective-permute-done | bytes 1568 | tf_op jit(solution)/shard_map/ppermute | solution.py:449
  22.3 0.0 collective-permute-done.1.other_ref
  22.3 1.1 %gather.1 = bf16[16,208,128]{2,1,0:T(8,128)(2,1)S(1)} custom-call(s32[16,24]{1,0:T(8,128)S(1)} %bitcast.9, bf16[1040,128]{1,0:T(8,128)(2,1)S(1)} %get-tuple-element.14.own_ref, bf16[1040,128]{1,0:T(8,128)(2,1)S(1)} %collective-permute-done.1.other_ref, bf16[16,128]{1,0:T(8,128)(2,1)S(1)} %get-tuple-element.15.edges_ref, ...), custom_call_target="tpu_custom_call" | custom-call | tf_op jit(solution)/shard_map/gather/pallas_call | solution.py:168
  23.4 16.0 %all_to_all.33.fetched_ref = bf16[16,208,128]{2,1,0:T(8,128)(2,1)S(1)} all-to-all(bf16[16,208,128]{2,1,0:T(8,128)(2,1)S(1)} %gather.1), channel_id=1, replica_groups=mesh['tx'=4,'th'=2,'tl'=4] {'tx','tl'}, dimensions={0} | all-to-all | bytes 1703936 | tf_op jit(solution)/shard_map/all_to_all | solution.py:445
  39.4 8.1 %bins.1 = (bf16[32,96,128]{2,1,0:T(8,128)(2,1)S(1)}, f32[4,128,256]{2,1,0:T(8,128)S(1)}) custom-call(s32[2,256]{1,0:T(2,128)S(1)} %get-tuple-element.13.line_vmem, bf16[16,208,128]{2,1,0:T(8,128)(2,1)S(1)} %all_to_all.33.fetched_ref, bf16[256,128,256]{2,1,0:T(8,128)(2,1)} %blocks_ref.1, f32[4,128,256]{2,1,0:T(8,128)S(1)} %get-tuple-element.16.field_ref.direction_ref), custom_call_target="tpu_custom_call" | custom-call | tf_op jit(solution)/shard_map/bins/pallas_call | solution.py:291
  47.5 24.1 %all_to_all.34.arrived_ref = bf16[32,96,128]{2,1,0:T(8,128)(2,1)S(1)} all-to-all(bf16[32,96,128]{2,1,0:T(8,128)(2,1)S(1)} %get-tuple-element.17), channel_id=1, replica_groups=mesh['tx'=4,'th'=2,'tl'=4] {'tx','th','tl'}, dimensions={0} | all-to-all | bytes 1572864 | tf_op jit(solution)/shard_map/all_to_all | solution.py:445
  71.6 0.0 copy-done
  71.6 2.2 %image.1 = (f32[4,128,256]{2,1,0:T(8,128)S(1)}, f32[32,128]{1,0:T(8,128)S(1)}) custom-call(s32[16,24]{1,0:T(8,128)S(1)} %bitcast.10, s32[16,24]{1,0:T(8,128)S(1)} %collective-permute-done.after_ref.far_vmem, bf16[32,96,128]{2,1,0:T(8,128)(2,1)S(1)} %all_to_all.34.arrived_ref, f32[4,128,256]{2,1,0:T(8,128)S(1)} %get-tuple-element.18.smooth_ref, ...), custom_call_target="tpu_custom_call" | custom-call | tf_op jit(solution)/shard_map/image/pallas_call | solution.py:385
  73.8 9.2 %all_to_all.35 = f32[32,1,128]{2,1,0:T(1,128)S(1)} all-to-all(f32[32,1,128]{2,1,0:T(1,128)S(1)} %bitcast.12), channel_id=1, replica_groups=mesh['tx'=4,'th'=2,'tl'=4] {'tx','th','tl'}, dimensions={0} | all-to-all | bytes 32768 | tf_op jit(solution)/shard_map/all_to_all | solution.py:445
  83.0 0.0 copy-done.2
  83.0 1.4 %update.1 = (f32[4,128,256]{2,1,0:T(8,128)}, f32[4,128,256]{2,1,0:T(8,128)}, f32[4,128,256]{2,1,0:T(8,128)}) custom-call(f32[32,128]{1,0:T(8,128)S(1)} %bitcast.11, f32[4,128,256]{2,1,0:T(8,128)S(1)} %copy-done.2, f32[4,128,256]{2,1,0:T(8,128)S(1)} %copy-done, f32[4,128,256]{2,1,0:T(8,128)S(1)} %get-tuple-element.16.field_ref.direction_ref, ...), custom_call_target="tpu_custom_call" | custom-call | tf_op jit(solution)/shard_map/update/pallas_call | solution.py:432
Async XLA Ops:
  0.6 71.0 %copy-start = (f32[4,128,256]{2,1,0:T(8,128)S(1)}, f32[4,128,256]{2,1,0:T(8,128)}, u32[]{:S(2)}) copy-start(f32[4,128,256]{2,1,0:T(8,128)} %residual_ref.3) | copy-start | bytes 1572868
  0.6 1.1 %copy-start.1 = (f32[4,128,256]{2,1,0:T(8,128)S(1)}, f32[4,128,256]{2,1,0:T(8,128)}, u32[]{:S(2)}) copy-start(f32[4,128,256]{2,1,0:T(8,128)} %field_ref.1) | copy-start | bytes 1572868
  1.7 81.3 %copy-start.2 = (f32[4,128,256]{2,1,0:T(8,128)S(1)}, f32[4,128,256]{2,1,0:T(8,128)}, u32[]{:S(2)}) copy-start(f32[4,128,256]{2,1,0:T(8,128)} %solution_ref.1) | copy-start | bytes 1572868
  2.3 20.0 %collective-permute-start.1 = (bf16[1040,128]{1,0:T(8,128)(2,1)S(1)}, bf16[1040,128]{1,0:T(8,128)(2,1)S(1)}, u32[]{:S(2)}, u32[]{:S(2)}) collective-permute-start(bf16[1040,128]{1,0:T(8,128)(2,1)S(1)} %get-tuple-element.14.own_ref), channel_id=1, source_target_pairs={{0,4},{4,0},{1,5},{5,1},{2,6},{6,2},{3,7},{7,3},{8,12},{12,8},{9,1... | collective-permute-start | bytes 798728 | tf_op jit(solution)/shard_map/ppermute | solution.py:449
  17.7 4.5 %collective-permute-start = (s32[16,24]{1,0:T(8,128)S(1)}, s32[16,24]{1,0:T(8,128)S(1)}, u32[]{:S(2)}, u32[]{:S(2)}) collective-permute-start(s32[16,24]{1,0:T(8,128)S(1)} %bitcast.8), channel_id=1, source_target_pairs={{0,4},{4,0},{1,5},{5,1},{2,6},{6,2},{3,7},{7,3},{8,12},{12,8},{9,1... | collective-permute-start | bytes 4616 | tf_op jit(solution)/shard_map/ppermute | solution.py:449

commit v8 on v7

--- a/solution.py
+++ b/solution.py
@@ -227,7 +227,6 @@
     for d in range(devices):
         pick[pl.ds(d * lines, lines), :] = fetched_ref[d // 2, d % 2 * lines : (d % 2 + 1) * lines, :].astype(jnp.float32)
         ret[pl.ds(d * lines, lines), :] = jnp.zeros((lines, LANES), jnp.float32)
-    samp_b[...] = jnp.zeros_like(samp_b)
     smooth(field_ref, fetched_ref, 2 * lines, smooth_ref)
     low = lax.broadcasted_iota(jnp.int32, (SUB, LANES), 0) < 4
 
@@ -261,6 +260,13 @@
     copy.wait()
     fetch(0).wait()
     turn(0, turn_a)
+    fetch(1).wait()
+    turn(1, turn_b)
+    sample(0, turn_a, samp_a)
+    fetch(2).wait()
+    turn(2, turn_a)
+    sample(1, turn_b, samp_b)
+    spread(0, samp_a)
 
     def body(i, carry):
         g = 2 * i
@@ -272,13 +278,13 @@
 
         turn(g + 1, turn_b)
         sample(g, turn_a, samp_a)
-        spread(jnp.maximum(g - 1, 0), samp_b)
+        spread(g - 1, samp_b)
         turn(jnp.minimum(g + 2, groups - 1), turn_a)
         sample(g + 1, turn_b, samp_b)
         spread(g, samp_a)
         return carry
 
-    lax.fori_loop(0, groups // 2, body, 0)
+    lax.fori_loop(1, groups // 2, body, 0)
     spread(groups - 1, samp_b)
     for d in range(devices):
         out_ref[d] = ret[pl.ds(d * lines, lines), :].astype(jnp.bfloat16)

time: 84.7 us -> 84.7 us (level)
  no operation moved by 1% of the time
where the time goes in v8:
time: 84.7 us; the launch traced here: 84.4 us
  blocking collectives  59.6 us (70%)
  Pallas kernels  13.6 us (16%)
  waiting for transfers between devices  4.41 us (5%)
  starting transfers between devices  4.21 us (5%)
  local copies, waits for them, and re-layouts  1.17 us (1%)
    all_to_all x4, blocking collectives, exchange(): return lax.all_to_all(x, axes, split_axis=0, concat_axis=0, tiled=True)  59.6 us
    pallas_call x1, Pallas kernels, bins(): pl.pallas_call(functools.partial(bins_kernel, group), in_specs=[whole(),...  8.08 us
    ppermute x2, waiting for transfers between devices, trade(): return lax.ppermute(x, 'th', [(0, 1), (1, 0)])  4.41 us
    ppermute x2, starting transfers between devices, trade(): return lax.ppermute(x, 'th', [(0, 1), (1, 0)])  4.21 us
    pallas_call x1, Pallas kernels, image_of(): pl.pallas_call(image_kernel, in_specs=[whole()] * 6, out_specs=[whole(),...  2.2 us
  transfers between devices with their start and end apart: 2, of which 1 were waited for; matrix products, arithmetic and copies ran while one was open for 1% of the time, Pallas kernels for 0%

profile of v8, /device:TPU:0, one launch (start us, length us, event | category | flops | bytes accessed | tf_op | source)
XLA Modules:
  0.0 84.4 jit_solution(16384611830473833927)
XLA Ops:
  0.6 0.0 copy-start
  0.6 0.0 copy-start.1
  0.7 1.1 %copy-done.1 = f32[4,128,256]{2,1,0:T(8,128)S(1)} copy-done((f32[4,128,256]{2,1,0:T(8,128)S(1)}, f32[4,128,256]{2,1,0:T(8,128)}, u32[]{:S(2)}) %copy-start.1) | copy-done | bytes 524312
  1.7 0.0 copy-start.2
  1.7 0.6 tiles.1
  2.3 4.1 %collective-permute-start.1 = (bf16[1040,128]{1,0:T(8,128)(2,1)S(1)}, bf16[1040,128]{1,0:T(8,128)(2,1)S(1)}, u32[]{:S(2)}, u32[]{:S(2)}) collective-permute-start(bf16[1040,128]{1,0:T(8,128)(2,1)S(1)} %get-tuple-element.14.own_ref), channel_id=1, source_target_pairs={{0,4},{4,0},{1,5},{5,1},{2,6},{6,2},{3,7},{7,3},{8,12},{12,8},{9,1... | collective-permute-start | bytes 798728 | tf_op jit(solution)/shard_map/ppermute | solution.py:455
  6.4 0.7 pad_add_fusion.both_ref
  7.1 0.3 prep.1
  7.4 0.1 all_to_all.20
  7.4 10.3 %all_to_all.32 = s32[16,1,24]{2,1,0:T(1,128)S(1)} all-to-all(s32[16,1,24]{2,1,0:T(1,128)S(1)} %bitcast.13), channel_id=1, replica_groups=mesh['tx'=4,'th'=2,'tl'=4] {'tx','tl'}, dimensions={0} | all-to-all | bytes 3072 | tf_op jit(solution)/shard_map/all_to_all | solution.py:451
  17.7 0.1 collective-permute-start
  17.9 4.4 %collective-permute-done.after_ref.far_vmem = s32[16,24]{1,0:T(8,128)S(1)} collective-permute-done((s32[16,24]{1,0:T(8,128)S(1)}, s32[16,24]{1,0:T(8,128)S(1)}, u32[]{:S(2)}, u32[]{:S(2)}) %collective-permute-start) | collective-permute-done | bytes 1568 | tf_op jit(solution)/shard_map/ppermute | solution.py:455
  22.3 0.0 collective-permute-done.1.other_ref
  22.3 1.1 %gather.1 = bf16[16,208,128]{2,1,0:T(8,128)(2,1)S(1)} custom-call(s32[16,24]{1,0:T(8,128)S(1)} %bitcast.9, bf16[1040,128]{1,0:T(8,128)(2,1)S(1)} %get-tuple-element.14.own_ref, bf16[1040,128]{1,0:T(8,128)(2,1)S(1)} %collective-permute-done.1.other_ref, bf16[16,128]{1,0:T(8,128)(2,1)S(1)} %get-tuple-element.15.edges_ref, ...), custom_call_target="tpu_custom_call" | custom-call | tf_op jit(solution)/shard_map/gather/pallas_call | solution.py:168
  23.4 16.0 %all_to_all.33.fetched_ref = bf16[16,208,128]{2,1,0:T(8,128)(2,1)S(1)} all-to-all(bf16[16,208,128]{2,1,0:T(8,128)(2,1)S(1)} %gather.1), channel_id=1, replica_groups=mesh['tx'=4,'th'=2,'tl'=4] {'tx','tl'}, dimensions={0} | all-to-all | bytes 1703936 | tf_op jit(solution)/shard_map/all_to_all | solution.py:451
  39.4 8.1 %bins.1 = (bf16[32,96,128]{2,1,0:T(8,128)(2,1)S(1)}, f32[4,128,256]{2,1,0:T(8,128)S(1)}) custom-call(s32[2,256]{1,0:T(2,128)S(1)} %get-tuple-element.13.line_vmem, bf16[16,208,128]{2,1,0:T(8,128)(2,1)S(1)} %all_to_all.33.fetched_ref, bf16[256,128,256]{2,1,0:T(8,128)(2,1)} %blocks_ref.1, f32[4,128,256]{2,1,0:T(8,128)S(1)} %get-tuple-element.16.field_ref.direction_ref), custom_call_target="tpu_custom_call" | custom-call | tf_op jit(solution)/shard_map/bins/pallas_call | solution.py:297
  47.5 24.1 %all_to_all.34.arrived_ref = bf16[32,96,128]{2,1,0:T(8,128)(2,1)S(1)} all-to-all(bf16[32,96,128]{2,1,0:T(8,128)(2,1)S(1)} %get-tuple-element.17), channel_id=1, replica_groups=mesh['tx'=4,'th'=2,'tl'=4] {'tx','th','tl'}, dimensions={0} | all-to-all | bytes 1572864 | tf_op jit(solution)/shard_map/all_to_all | solution.py:451
  71.6 0.0 copy-done
  71.6 2.2 %image.1 = (f32[4,128,256]{2,1,0:T(8,128)S(1)}, f32[32,128]{1,0:T(8,128)S(1)}) custom-call(s32[16,24]{1,0:T(8,128)S(1)} %bitcast.10, s32[16,24]{1,0:T(8,128)S(1)} %collective-permute-done.after_ref.far_vmem, bf16[32,96,128]{2,1,0:T(8,128)(2,1)S(1)} %all_to_all.34.arrived_ref, f32[4,128,256]{2,1,0:T(8,128)S(1)} %get-tuple-element.18.smooth_ref, ...), custom_call_target="tpu_custom_call" | custom-call | tf_op jit(solution)/shard_map/image/pallas_call | solution.py:391
  73.8 9.2 %all_to_all.35 = f32[32,1,128]{2,1,0:T(1,128)S(1)} all-to-all(f32[32,1,128]{2,1,0:T(1,128)S(1)} %bitcast.12), channel_id=1, replica_groups=mesh['tx'=4,'th'=2,'tl'=4] {'tx','th','tl'}, dimensions={0} | all-to-all | bytes 32768 | tf_op jit(solution)/shard_map/all_to_all | solution.py:451
  83.0 0.0 copy-done.2
  83.0 1.4 %update.1 = (f32[4,128,256]{2,1,0:T(8,128)}, f32[4,128,256]{2,1,0:T(8,128)}, f32[4,128,256]{2,1,0:T(8,128)}) custom-call(f32[32,128]{1,0:T(8,128)S(1)} %bitcast.11, f32[4,128,256]{2,1,0:T(8,128)S(1)} %copy-done.2, f32[4,128,256]{2,1,0:T(8,128)S(1)} %copy-done, f32[4,128,256]{2,1,0:T(8,128)S(1)} %get-tuple-element.16.field_ref.direction_ref, ...), custom_call_target="tpu_custom_call" | custom-call | tf_op jit(solution)/shard_map/update/pallas_call | solution.py:438
Async XLA Ops:
  0.6 71.0 %copy-start = (f32[4,128,256]{2,1,0:T(8,128)S(1)}, f32[4,128,256]{2,1,0:T(8,128)}, u32[]{:S(2)}) copy-start(f32[4,128,256]{2,1,0:T(8,128)} %residual_ref.3) | copy-start | bytes 1572868
  0.6 1.1 %copy-start.1 = (f32[4,128,256]{2,1,0:T(8,128)S(1)}, f32[4,128,256]{2,1,0:T(8,128)}, u32[]{:S(2)}) copy-start(f32[4,128,256]{2,1,0:T(8,128)} %field_ref.1) | copy-start | bytes 1572868
  1.7 81.3 %copy-start.2 = (f32[4,128,256]{2,1,0:T(8,128)S(1)}, f32[4,128,256]{2,1,0:T(8,128)}, u32[]{:S(2)}) copy-start(f32[4,128,256]{2,1,0:T(8,128)} %solution_ref.1) | copy-start | bytes 1572868
  2.3 20.0 %collective-permute-start.1 = (bf16[1040,128]{1,0:T(8,128)(2,1)S(1)}, bf16[1040,128]{1,0:T(8,128)(2,1)S(1)}, u32[]{:S(2)}, u32[]{:S(2)}) collective-permute-start(bf16[1040,128]{1,0:T(8,128)(2,1)S(1)} %get-tuple-element.14.own_ref), channel_id=1, source_target_pairs={{0,4},{4,0},{1,5},{5,1},{2,6},{6,2},{3,7},{7,3},{8,12},{12,8},{9,1... | collective-permute-start | bytes 798728 | tf_op jit(solution)/shard_map/ppermute | solution.py:455
  17.7 4.5 %collective-permute-start = (s32[16,24]{1,0:T(8,128)S(1)}, s32[16,24]{1,0:T(8,128)S(1)}, u32[]{:S(2)}, u32[]{:S(2)}) collective-permute-start(s32[16,24]{1,0:T(8,128)S(1)} %bitcast.8), channel_id=1, source_target_pairs={{0,4},{4,0},{1,5},{5,1},{2,6},{6,2},{3,7},{7,3},{8,12},{12,8},{9,1... | collective-permute-start | bytes 4616 | tf_op jit(solution)/shard_map/ppermute | solution.py:455

commit v9 on v8

--- a/solution.py
+++ b/solution.py
@@ -420,16 +420,20 @@
     moved = jnp.sum(size * (size * column(stats, 3) - 2.0 * column(stats, 2)), axis=0, keepdims=True)
     beta = (total + moved) / total
     copies = []
-    for k in range(beacons):
-        a, b = alpha[:1, k : k + 1], beta[:1, k : k + 1]
-        d = direction_ref[k]
-        r = residual_ref[k] - a * image_ref[k]
-        sol[k] = solution_ref[k] + a * d
-        res[k] = r
-        dire[k] = r + b * d
-        for q, (held, out) in enumerate(((sol, sol_ref), (res, res_ref), (dire, dir_ref))):
-            copies.append(pltpu.make_async_copy(held.at[k], out.at[k], sems.at[q, k]))
-            copies[-1].start()
+
+    def send(q, k, held, out):
+        copies.append(pltpu.make_async_copy(held.at[k], out.at[k], sems.at[q, k]))
+        copies[-1].start()
+
+    for k in range(beacons):
+        sol[k] = solution_ref[k] + alpha[:1, k : k + 1] * direction_ref[k]
+        send(0, k, sol, sol_ref)
+    for k in range(beacons):
+        res[k] = residual_ref[k] - alpha[:1, k : k + 1] * image_ref[k]
+        send(1, k, res, res_ref)
+    for k in range(beacons):
+        dire[k] = res[k] + beta[:1, k : k + 1] * direction_ref[k]
+        send(2, k, dire, dir_ref)
     for copy in copies:
         copy.wait()
 

time: 84.7 us -> 84.7 us (level)
  no operation moved by 1% of the time
where the time goes in v9:
time: 84.7 us; the launch traced here: 84.4 us
  blocking collectives  59.7 us (70%)
  Pallas kernels  13.6 us (16%)
  waiting for transfers between devices  4.41 us (5%)
  starting transfers between devices  4.21 us (5%)
  local copies, waits for them, and re-layouts  1.17 us (1%)
    all_to_all x4, blocking collectives, exchange(): return lax.all_to_all(x, axes, split_axis=0, concat_axis=0, tiled=True)  59.7 us
    pallas_call x1, Pallas kernels, bins(): pl.pallas_call(functools.partial(bins_kernel, group), in_specs=[whole(),...  8.09 us
    ppermute x2, waiting for transfers between devices, trade(): return lax.ppermute(x, 'th', [(0, 1), (1, 0)])  4.41 us
    ppermute x2, starting transfers between devices, trade(): return lax.ppermute(x, 'th', [(0, 1), (1, 0)])  4.21 us
    pallas_call x1, Pallas kernels, image_of(): pl.pallas_call(image_kernel, in_specs=[whole()] * 6, out_specs=[whole(),...  2.19 us
  transfers between devices with their start and end apart: 2, of which 1 were waited for; matrix products, arithmetic and copies ran while one was open for 1% of the time, Pallas kernels for 0%

profile of v9, /device:TPU:0, one launch (start us, length us, event | category | flops | bytes accessed | tf_op | source)
XLA Modules:
  0.0 84.4 jit_solution(10045016530060619815)
XLA Ops:
  0.6 0.0 copy-start
  0.6 0.0 copy-start.1
  0.7 1.1 %copy-done.1 = f32[4,128,256]{2,1,0:T(8,128)S(1)} copy-done((f32[4,128,256]{2,1,0:T(8,128)S(1)}, f32[4,128,256]{2,1,0:T(8,128)}, u32[]{:S(2)}) %copy-start.1) | copy-done | bytes 524312
  1.7 0.0 copy-start.2
  1.7 0.6 tiles.1
  2.3 4.1 %collective-permute-start.1 = (bf16[1040,128]{1,0:T(8,128)(2,1)S(1)}, bf16[1040,128]{1,0:T(8,128)(2,1)S(1)}, u32[]{:S(2)}, u32[]{:S(2)}) collective-permute-start(bf16[1040,128]{1,0:T(8,128)(2,1)S(1)} %get-tuple-element.14.own_ref), channel_id=1, source_target_pairs={{0,4},{4,0},{1,5},{5,1},{2,6},{6,2},{3,7},{7,3},{8,12},{12,8},{9,1... | collective-permute-start | bytes 798728 | tf_op jit(solution)/shard_map/ppermute | solution.py:459
  6.4 0.7 pad_add_fusion.both_ref
  7.1 0.3 prep.1
  7.4 0.1 all_to_all.20
  7.4 10.3 %all_to_all.32 = s32[16,1,24]{2,1,0:T(1,128)S(1)} all-to-all(s32[16,1,24]{2,1,0:T(1,128)S(1)} %bitcast.13), channel_id=1, replica_groups=mesh['tx'=4,'th'=2,'tl'=4] {'tx','tl'}, dimensions={0} | all-to-all | bytes 3072 | tf_op jit(solution)/shard_map/all_to_all | solution.py:455
  17.7 0.1 collective-permute-start
  17.9 4.4 %collective-permute-done.after_ref.far_vmem = s32[16,24]{1,0:T(8,128)S(1)} collective-permute-done((s32[16,24]{1,0:T(8,128)S(1)}, s32[16,24]{1,0:T(8,128)S(1)}, u32[]{:S(2)}, u32[]{:S(2)}) %collective-permute-start) | collective-permute-done | bytes 1568 | tf_op jit(solution)/shard_map/ppermute | solution.py:459
  22.3 0.0 collective-permute-done.1.other_ref
  22.3 1.1 %gather.1 = bf16[16,208,128]{2,1,0:T(8,128)(2,1)S(1)} custom-call(s32[16,24]{1,0:T(8,128)S(1)} %bitcast.9, bf16[1040,128]{1,0:T(8,128)(2,1)S(1)} %get-tuple-element.14.own_ref, bf16[1040,128]{1,0:T(8,128)(2,1)S(1)} %collective-permute-done.1.other_ref, bf16[16,128]{1,0:T(8,128)(2,1)S(1)} %get-tuple-element.15.edges_ref, ...), custom_call_target="tpu_custom_call" | custom-call | tf_op jit(solution)/shard_map/gather/pallas_call | solution.py:168
  23.4 16.0 %all_to_all.33.fetched_ref = bf16[16,208,128]{2,1,0:T(8,128)(2,1)S(1)} all-to-all(bf16[16,208,128]{2,1,0:T(8,128)(2,1)S(1)} %gather.1), channel_id=1, replica_groups=mesh['tx'=4,'th'=2,'tl'=4] {'tx','tl'}, dimensions={0} | all-to-all | bytes 1703936 | tf_op jit(solution)/shard_map/all_to_all | solution.py:455
  39.4 8.1 %bins.1 = (bf16[32,96,128]{2,1,0:T(8,128)(2,1)S(1)}, f32[4,128,256]{2,1,0:T(8,128)S(1)}) custom-call(s32[2,256]{1,0:T(2,128)S(1)} %get-tuple-element.13.line_vmem, bf16[16,208,128]{2,1,0:T(8,128)(2,1)S(1)} %all_to_all.33.fetched_ref, bf16[256,128,256]{2,1,0:T(8,128)(2,1)} %blocks_ref.1, f32[4,128,256]{2,1,0:T(8,128)S(1)} %get-tuple-element.16.field_ref.direction_ref), custom_call_target="tpu_custom_call" | custom-call | tf_op jit(solution)/shard_map/bins/pallas_call | solution.py:297
  47.5 24.1 %all_to_all.34.arrived_ref = bf16[32,96,128]{2,1,0:T(8,128)(2,1)S(1)} all-to-all(bf16[32,96,128]{2,1,0:T(8,128)(2,1)S(1)} %get-tuple-element.17), channel_id=1, replica_groups=mesh['tx'=4,'th'=2,'tl'=4] {'tx','th','tl'}, dimensions={0} | all-to-all | bytes 1572864 | tf_op jit(solution)/shard_map/all_to_all | solution.py:455
  71.6 0.0 copy-done
  71.6 2.2 %image.1 = (f32[4,128,256]{2,1,0:T(8,128)S(1)}, f32[32,128]{1,0:T(8,128)S(1)}) custom-call(s32[16,24]{1,0:T(8,128)S(1)} %bitcast.10, s32[16,24]{1,0:T(8,128)S(1)} %collective-permute-done.after_ref.far_vmem, bf16[32,96,128]{2,1,0:T(8,128)(2,1)S(1)} %all_to_all.34.arrived_ref, f32[4,128,256]{2,1,0:T(8,128)S(1)} %get-tuple-element.18.smooth_ref, ...), custom_call_target="tpu_custom_call" | custom-call | tf_op jit(solution)/shard_map/image/pallas_call | solution.py:391
  73.8 9.2 %all_to_all.35 = f32[32,1,128]{2,1,0:T(1,128)S(1)} all-to-all(f32[32,1,128]{2,1,0:T(1,128)S(1)} %bitcast.12), channel_id=1, replica_groups=mesh['tx'=4,'th'=2,'tl'=4] {'tx','th','tl'}, dimensions={0} | all-to-all | bytes 32768 | tf_op jit(solution)/shard_map/all_to_all | solution.py:455
  83.0 0.0 copy-done.2
  83.0 1.4 %update.1 = (f32[4,128,256]{2,1,0:T(8,128)}, f32[4,128,256]{2,1,0:T(8,128)}, f32[4,128,256]{2,1,0:T(8,128)}) custom-call(f32[32,128]{1,0:T(8,128)S(1)} %bitcast.11, f32[4,128,256]{2,1,0:T(8,128)S(1)} %copy-done.2, f32[4,128,256]{2,1,0:T(8,128)S(1)} %copy-done, f32[4,128,256]{2,1,0:T(8,128)S(1)} %get-tuple-element.16.field_ref.direction_ref, ...), custom_call_target="tpu_custom_call" | custom-call | tf_op jit(solution)/shard_map/update/pallas_call | solution.py:442
Async XLA Ops:
  0.6 71.0 %copy-start = (f32[4,128,256]{2,1,0:T(8,128)S(1)}, f32[4,128,256]{2,1,0:T(8,128)}, u32[]{:S(2)}) copy-start(f32[4,128,256]{2,1,0:T(8,128)} %residual_ref.3) | copy-start | bytes 1572868
  0.6 1.1 %copy-start.1 = (f32[4,128,256]{2,1,0:T(8,128)S(1)}, f32[4,128,256]{2,1,0:T(8,128)}, u32[]{:S(2)}) copy-start(f32[4,128,256]{2,1,0:T(8,128)} %field_ref.1) | copy-start | bytes 1572868
  1.7 81.3 %copy-start.2 = (f32[4,128,256]{2,1,0:T(8,128)S(1)}, f32[4,128,256]{2,1,0:T(8,128)}, u32[]{:S(2)}) copy-start(f32[4,128,256]{2,1,0:T(8,128)} %solution_ref.1) | copy-start | bytes 1572868
  2.3 20.0 %collective-permute-start.1 = (bf16[1040,128]{1,0:T(8,128)(2,1)S(1)}, bf16[1040,128]{1,0:T(8,128)(2,1)S(1)}, u32[]{:S(2)}, u32[]{:S(2)}) collective-permute-start(bf16[1040,128]{1,0:T(8,128)(2,1)S(1)} %get-tuple-element.14.own_ref), channel_id=1, source_target_pairs={{0,4},{4,0},{1,5},{5,1},{2,6},{6,2},{3,7},{7,3},{8,12},{12,8},{9,1... | collective-permute-start | bytes 798728 | tf_op jit(solution)/shard_map/ppermute | solution.py:459
  17.7 4.5 %collective-permute-start = (s32[16,24]{1,0:T(8,128)S(1)}, s32[16,24]{1,0:T(8,128)S(1)}, u32[]{:S(2)}, u32[]{:S(2)}) collective-permute-start(s32[16,24]{1,0:T(8,128)S(1)} %bitcast.8), channel_id=1, source_target_pairs={{0,4},{4,0},{1,5},{5,1},{2,6},{6,2},{3,7},{7,3},{8,12},{12,8},{9,1... | collective-permute-start | bytes 4616 | tf_op jit(solution)/shard_map/ppermute | solution.py:459
